TPU v7x, 256 devices: a whole 4x4x8 slice. The times are simulated.
256 devices in a mesh: row: 2 (over core), col: 4 (over x), depth: 32 (over z, y).
Axes of the slice: x: 4, y: 4, z: 8, core: 2. Of those that a mesh axis runs over, the one named last changes fastest.
Arguments:
- act_forward: bfloat16 [8192, 4096], P(('depth', 'col'), 'row'), may hold values from -6 to 6
- weight: bfloat16 [4096, 14336], P('row', 'col'), may hold values from -0.09375 to 0.09375
- act_backward: bfloat16 [8192, 4096], P(('depth', 'col'), 'row'), may hold values from -6 to 6
- pre_backward: bfloat16 [8192, 14336], P(('depth', 'row'), 'col'), may hold values from -8 to 8
- grad_backward: bfloat16 [8192, 14336], P(('depth', 'row'), 'col'), may hold values from -6 to 6
Outputs:
- hidden_forward: bfloat16 [8192, 14336], P(('depth', 'row'), 'col')
- grad_inputs: bfloat16 [8192, 4096], P(('depth', 'col'), 'row')
- grad_weight: float32 [4096, 14336], P('row', ('col', 'depth'))
All inputs are finite; a program needn't handle non-finite values.
Results may differ from a plain program's by a relative error of at most 0.02.
Values may be sent and summed in bfloat16 or wider, within the bound.
No kernel may reach another device: no remote copies, remote signals or barrier semaphores. Data moves between devices by JAX's collectives and lax.ppermute only.
A program may use at most 128 MiB of HBM per device.

v0:
```python
import math

import jax
import jax.numpy as jnp
from jax import lax
from jax.sharding import PartitionSpec as P

coeff = math.sqrt(2.0 / math.pi)


def gelu_value(v):
    inner = coeff * (v + 0.044715 * v * v * v)
    return 0.5 * v * (1.0 + jnp.tanh(inner))


def gelu_slope(v):
    tanh_part = jnp.tanh(coeff * (v + 0.044715 * v * v * v))
    return 0.5 * (1.0 + tanh_part) + 0.5 * v * (1.0 - tanh_part * tanh_part) * coeff * (
        1.0 + 3.0 * 0.044715 * v * v
    )


def on_device(act_forward, weight, act_backward, pre_backward, grad_backward):
    gathered_fwd, gathered_back = (
        lax.all_gather(act_forward, "col", axis=0, tiled=True),
        lax.all_gather(act_backward, "col", axis=0, tiled=True),
    )
    grad_pre = (
        grad_backward.astype(jnp.float32) * gelu_slope(pre_backward.astype(jnp.float32))
    ).astype(jnp.bfloat16)
    grad_full = lax.all_gather(grad_pre, "row", axis=0, tiled=True)
    rows = gathered_fwd
    pre_forward = lax.psum_scatter(
        jnp.dot(rows, weight, preferred_element_type=jnp.float32).astype(jnp.bfloat16),
        "row",
        scatter_dimension=0,
        tiled=True,
    ).astype(jnp.float32)
    hidden_forward = gelu_value(pre_forward).astype(jnp.bfloat16)
    rows = grad_full
    grad_inputs = lax.psum_scatter(
        lax.dot_general(
            rows, weight, (((1,), (1,)), ((), ())), preferred_element_type=jnp.float32
        ).astype(jnp.bfloat16),
        "col",
        scatter_dimension=0,
        tiled=True,
    )
    summed = lax.psum_scatter(
        lax.dot_general(
            grad_full, gathered_back, (((0,), (0,)), ((), ())), preferred_element_type=jnp.float32
        ).astype(jnp.bfloat16),
        "depth",
        scatter_dimension=0,
        tiled=True,
    ).astype(jnp.float32)
    grad_weight = summed.T
    return (hidden_forward, grad_inputs, grad_weight)


def solution(mesh):
    in_specs = (
        P(("depth", "col"), "row"),
        P("row", "col"),
        P(("depth", "col"), "row"),
        P(("depth", "row"), "col"),
        P(("depth", "row"), "col"),
    )
    out_specs = (P(("depth", "row"), "col"), P(("depth", "col"), "row"), P("row", ("col", "depth")))
    return jax.shard_map(
        on_device, mesh=mesh, in_specs=in_specs, out_specs=out_specs, check_vma=False
    )
```

profile of v0, /device:TPU:2, one launch (start us, length us, event | category | flops | bytes accessed | tf_op | source)
XLA Modules:
  0.0 384.3 jit_solution(11100307281941533631)
XLA Ops:
  7.2 0.0 all-gather.4.cloned.1.call-start
  7.2 0.7 all-gather.4.cloned.1.call-update
  7.9 0.0 all-gather.8.cloned.1.call-start
  7.9 0.7 all-gather.8.cloned.1.call-update
  8.6 0.0 all-gather.6.cloned.1.call-start
  8.7 3.7 fusion.12
  12.3 0.0 all-gather.6.cloned.1.call-update
  12.4 0.0 reduce-scatter.4.cloned.1.call-start
  12.4 26.0 %all-gather.4.cloned.1.call-done = bf16[256,2048]{1,0:T(8,128)(2,1)} async-done(((bf16[64,2048]{1,0:T(8,128)(2,1)}), bf16[256,2048]{1,0:T(8,128)(2,1)}) %all-gather.4.cloned.1.call-update) | async-done | bytes 1048592 | tf_op jit(solution)/shard_map/all_gather | solution.py:25
  38.4 10.7 %convolution_convert_fusion.1 = bf16[256,3584]{1,0:T(8,128)(2,1)} fusion(bf16[256,2048]{1,0:T(8,128)(2,1)} %all-gather.4.cloned.1.call-done, bf16[2048,3584]{1,0:T(8,128)(2,1)} %param.6), kind=kOutput, calls=%fused_computation.1 | convolution fusion | flops 3759013888 | bytes 17563648 | tf_op jit(solution)/shard_map/dot_general | solution.py:34
  49.1 0.0 reduce-scatter.8.cloned.1.call-start
  49.2 17.9 %all-gather.8.cloned.1.call-done = bf16[256,2048]{1,0:T(8,128)(2,1)} async-done(((bf16[64,2048]{1,0:T(8,128)(2,1)}), bf16[256,2048]{1,0:T(8,128)(2,1)}) %all-gather.8.cloned.1.call-update) | async-done | bytes 1048592 | tf_op jit(solution)/shard_map/all_gather | solution.py:26
  67.1 19.2 %all-gather.6.cloned.1.call-done = bf16[256,3584]{1,0:T(8,128)(2,1)} async-done(((bf16[128,3584]{1,0:T(8,128)(2,1)}), bf16[256,3584]{1,0:T(8,128)(2,1)}) %all-gather.6.cloned.1.call-update) | async-done | bytes 1835024 | tf_op jit(solution)/shard_map/all_gather | solution.py:31
  86.3 11.0 %convolution_convert_fusion = bf16[3584,2048]{1,0:T(8,128)(2,1)} fusion(bf16[256,3584]{1,0:T(8,128)(2,1)} %all-gather.6.cloned.1.call-done, bf16[256,2048]{1,0:T(8,128)(2,1)} %all-gather.8.cloned.1.call-done), kind=kOutput, calls=%fused_computation | convolution fusion | flops 3765436416 | bytes 17563648 | tf_op jit(solution)/shard_map/dot_general | solution.py:50
  97.3 0.0 reduce-scatter.8.cloned.1.call-update
  97.3 0.0 reduce-scatter.6.cloned.1.call-start
  97.4 1.4 copy-done
  98.8 9.2 %convolution_convert_fusion.2 = bf16[256,2048]{1,0:T(8,128)(2,1)} fusion(bf16[256,3584]{1,0:T(8,128)(2,1)S(1)} %copy-done, bf16[2048,3584]{1,0:T(8,128)(2,1)} %param.6), kind=kOutput, calls=%fused_computation.14 | convolution fusion | flops 3758620672 | bytes 17563648 | tf_op jit(solution)/shard_map/dot_general | solution.py:42
  108.0 0.0 reduce-scatter.6.cloned.1.call-update
  108.0 0.0 reduce-scatter.4.cloned.1.call-done
  108.0 2.7 fusion.1
  110.8 240.9 %reduce-scatter.8.cloned.1.call-done = bf16[112,2048]{1,0:T(8,128)(2,1)} async-done(((bf16[3584,2048]{1,0:T(8,128)(2,1)}), bf16[112,2048]{1,0:T(8,128)(2,1)}) %reduce-scatter.8.cloned.1.call-update) | async-done | bytes 458768 | tf_op jit(solution)/shard_map/reduce_scatter | solution.py:49
  351.7 2.0 convert_bitcast_fusion
  353.7 23.7 %reduce-scatter.6.cloned.1.call-done = bf16[64,2048]{1,0:T(8,128)(2,1)} async-done(((bf16[256,2048]{1,0:T(8,128)(2,1)}), bf16[64,2048]{1,0:T(8,128)(2,1)}) %reduce-scatter.6.cloned.1.call-update) | async-done | bytes 262160 | tf_op jit(solution)/shard_map/reduce_scatter | solution.py:41
  (2 shorter events, 0.0 us)
Async XLA Ops:
  7.2 31.2 %all-gather.4.cloned.1.call-start = ((), (), s32[]{:S(2)}) async-start(), calls=%async_computation.3 | async-start | bytes 1310720 | tf_op jit(solution)/shard_map/all_gather | solution.py:25
  7.9 59.2 %all-gather.8.cloned.1.call-start = ((), (), s32[]{:S(2)}) async-start(), calls=%async_computation.7 | async-start | bytes 1310720 | tf_op jit(solution)/shard_map/all_gather | solution.py:26
  8.6 77.6 %all-gather.6.cloned.1.call-start = ((), (), s32[]{:S(2)}) async-start(), calls=%async_computation.5 | async-start | bytes 2752512 | tf_op jit(solution)/shard_map/all_gather | solution.py:31
  12.4 95.7 %reduce-scatter.4.cloned.1.call-start = ((), (), s32[]{:S(2)}) async-start(), calls=%async_computation.4 | async-start | bytes 2752512 | tf_op jit(solution)/shard_map/reduce_scatter | solution.py:33
  49.1 302.5 %reduce-scatter.8.cloned.1.call-start = ((), (), s32[]{:S(2)}) async-start(), calls=%async_computation.8 | async-start | bytes 15138816 | tf_op jit(solution)/shard_map/reduce_scatter | solution.py:49
  97.3 1.5 copy-start
  97.3 280.1 %reduce-scatter.6.cloned.1.call-start = ((), (), s32[]{:S(2)}) async-start(), calls=%async_computation.6 | async-start | bytes 1310720 | tf_op jit(solution)/shard_map/reduce_scatter | solution.py:41
Sparse Core Ops, SparseCore 0:
  9.8 28.5 all-gather.3
  40.2 26.8 all-gather.7
  69.5 16.7 all-gather.5
  88.6 15.9 reduce-scatter.3
  109.3 242.3 reduce-scatter.7
  354.8 22.5 reduce-scatter.5
where the time goes:
time: 386 us; the launch traced here: 384 us
  waiting for transfers between devices  329 us (85%)
  matrix products  30.9 us (8%)
  between operations  14.1 us (4%)
  other arithmetic  8.41 us (2%)
    reduce_scatter x1, waiting for transfers between devices, on_device(): lax.psum_scatter(lax.dot_general(grad_full, gathered_back, (((0,), (0,)),...  241 us
    all_gather x1, waiting for transfers between devices, on_device(): lax.all_gather(act_forward, 'col', axis=0, tiled=True)  26 us
    reduce_scatter x1, waiting for transfers between devices, on_device(): lax.psum_scatter(lax.dot_general(rows, weight, (((1,), (1,)), ((), ())),...  23.7 us
    all_gather x1, waiting for transfers between devices, on_device(): grad_full = lax.all_gather(grad_pre, 'row', axis=0, tiled=True)  19.2 us
    all_gather x1, waiting for transfers between devices, on_device(): lax.all_gather(act_backward, 'col', axis=0, tiled=True)  17.9 us
    dot_general x1, matrix products, on_device(): lax.dot_general(grad_full, gathered_back, (((0,), (0,)), ((), ())), prefe...  11 us
    dot_general x1, matrix products, on_device(): jnp.dot(rows, weight, preferred_element_type=jnp.float32)  10.7 us
    dot_general x1, matrix products, on_device(): lax.dot_general(rows, weight, (((1,), (1,)), ((), ())), preferred_element...  9.2 us
  transfers between devices with their start and end apart: 6, of which 5 were waited for; matrix products, arithmetic and copies ran while one was open for 10% of the time, Pallas kernels for 0%

commit v1 on v0

v1 whole, which is shorter than its diff:
```python
import math

import jax
import jax.numpy as jnp
from jax import lax
from jax.experimental import pallas as pl
from jax.experimental.pallas import tpu as pltpu
from jax.sharding import Mesh, PartitionSpec as P

coeff = math.sqrt(2.0 / math.pi)
BF = jnp.bfloat16
F32 = jnp.float32
SIZES = {"row": 2, "col": 4, "z": 8, "y": 4}


def gelu_value(v):
    inner = coeff * (v + 0.044715 * v * v * v)
    return 0.5 * v * (1.0 + jnp.tanh(inner))


def gelu_slope(v):
    tanh_part = jnp.tanh(coeff * (v + 0.044715 * v * v * v))
    return 0.5 * (1.0 + tanh_part) + 0.5 * v * (1.0 - tanh_part * tanh_part) * coeff * (
        1.0 + 3.0 * 0.044715 * v * v
    )


def send(value, axis, step):
    n = SIZES[axis]
    return lax.ppermute(value, axis, [(i, (i + step) % n) for i in range(n)])


def grad_kernel(pre_ref, grad_ref, out_ref, flip_ref):
    g = grad_ref[...].astype(F32) * gelu_slope(pre_ref[...].astype(F32))
    out_ref[...] = g.astype(BF)
    flip_ref[...] = g.T.astype(BF)


def grad_pre_both(pre, grad):
    rows, cols = pre.shape
    tile = 512
    return pl.pallas_call(
        grad_kernel,
        grid=(cols // tile,),
        in_specs=[pl.BlockSpec((rows, tile), lambda i: (0, i))] * 2,
        out_specs=[
            pl.BlockSpec((rows, tile), lambda i: (0, i)),
            pl.BlockSpec((tile, rows), lambda i: (i, 0)),
        ],
        out_shape=[
            jax.ShapeDtypeStruct((rows, cols), BF),
            jax.ShapeDtypeStruct((cols, rows), BF),
        ],
        compiler_params=pltpu.CompilerParams(vmem_limit_bytes=16 * 2**20),
        cost_estimate=pl.CostEstimate(
            flops=30 * rows * cols, bytes_accessed=8 * rows * cols, transcendentals=rows * cols
        ),
    )(pre, grad)


def part_kernel(place_ref, own_ref, oth_ref, b0, b1, b2, b3, out_ref, acts):
    @pl.when(pl.program_id(0) == 0)
    def _():
        x, r = place_ref[0], place_ref[1]
        for d, block in enumerate((b0, b1, b2, b3)):
            at = lax.rem(x + d, 4)
            start = ((at // 2) ^ r) * 512 + lax.rem(at, 2) * 64
            for j in range(4):
                rows = pl.ds(pl.multiple_of(start + j * 128, 64), 64)
                acts[rows, :] = block[j * 64 : (j + 1) * 64, :]

    total = jnp.dot(own_ref[...], acts[0:512, :], preferred_element_type=F32)
    total += jnp.dot(oth_ref[...], acts[512:1024, :], preferred_element_type=F32)
    out_ref[...] = total.astype(BF)


def weight_part(place, own, oth, blocks):
    rows, wide = own.shape[0], blocks[0].shape[1]
    tile = 256
    whole = pl.BlockSpec((256, wide), lambda i, s: (0, 0))
    return pl.pallas_call(
        part_kernel,
        grid_spec=pltpu.PrefetchScalarGridSpec(
            num_scalar_prefetch=1,
            grid=(rows // tile,),
            in_specs=[pl.BlockSpec((tile, 512), lambda i, s: (i, 0))] * 2 + [whole] * 4,
            out_specs=pl.BlockSpec((tile, wide), lambda i, s: (i, 0)),
            scratch_shapes=[pltpu.VMEM((1024, wide), BF)],
        ),
        out_shape=jax.ShapeDtypeStruct((rows, wide), BF),
        compiler_params=pltpu.CompilerParams(vmem_limit_bytes=24 * 2**20),
        cost_estimate=pl.CostEstimate(
            flops=2 * rows * 1024 * wide, bytes_accessed=2 * rows * (1024 + wide), transcendentals=0
        ),
    )(place, own, oth, *blocks)


def reduce_z(part, z, step):
    def piece(offset):
        return lax.dynamic_index_in_dim(part, (z + offset) % 8, 0, keepdims=False)

    far, near = piece(4), piece(-3 * step)
    for hop in (3, 2, 1, 0):
        far = send(far, "z", step)
        if hop >= 1:
            near = send(near, "z", -step)
            far = far + piece(hop * step)
            if hop > 1:
                near = near + piece(-(hop - 1) * step)
    return piece(0).astype(F32) + far.astype(F32) + near.astype(F32)


def on_device(act_forward, weight, act_backward, pre_backward, grad_backward):
    r, x, z, y = (lax.axis_index(name) for name in ("row", "col", "z", "y"))
    ym, yn = y % 2, y // 2
    place = jnp.stack([x, r]).astype(jnp.int32)

    same = lax.dynamic_slice(act_backward, (0, ym * 1024), (64, 1024))
    other = lax.dynamic_slice(act_backward, (0, (1 - ym) * 1024), (64, 1024))
    acts = [same, send(other, "y", 1), send(other, "y", -1), send(same, "y", 2)]

    fwd = [
        act_forward,
        send(act_forward, "col", -1),
        send(act_forward, "col", 2),
        send(act_forward, "col", 1),
    ]

    grad_pre, flipped = grad_pre_both(pre_backward, grad_backward)
    flipped = flipped.reshape(8, 2, 224, 128)

    def hidden_half(which):
        return lax.dynamic_index_in_dim(flipped, which, 1, keepdims=False).reshape(1792, 128)

    grads = [
        hidden_half(yn),
        send(hidden_half(((y + 1) % 4) // 2), "y", 1),
        send(hidden_half(((y + 3) % 4) // 2), "y", -1),
        send(hidden_half(1 - yn), "y", 2),
    ]
    grads_own = jnp.concatenate(grads, axis=1)
    grads_other = send(grads_own, "row", 1)

    acts = jnp.concatenate(acts, axis=0)
    sums = []
    for c in range(2):
        mine = acts[:, c * 512 : (c + 1) * 512]
        blocks = (mine, send(mine, "col", -1), send(mine, "col", 2), send(mine, "col", 1))
        part = weight_part(place, grads_own, grads_other, blocks).reshape(8, 224, 512)
        sums.append(reduce_z(part, z, 1 - 2 * c))
    total = jnp.concatenate(sums, axis=1).reshape(2, 112, 1024)
    kept = lax.dynamic_index_in_dim(total, ym, 0, keepdims=False)
    given = lax.dynamic_index_in_dim(total, 1 - ym, 0, keepdims=False).astype(BF)
    got = lax.ppermute(given, "y", [(0, 1), (1, 0), (2, 3), (3, 2)]).astype(F32)
    grad_weight = jnp.where(
        ym == 0, jnp.concatenate([kept, got], axis=1), jnp.concatenate([got, kept], axis=1)
    ).T

    rows_fwd = jnp.zeros((256, 2048), BF)
    for d, block in enumerate(fwd):
        at = (x + d) % 4
        rows_fwd = lax.dynamic_update_slice(
            rows_fwd, block, (((at // 2) ^ r) * 128 + (at % 2) * 64, 0)
        )
    part_fwd = jnp.dot(rows_fwd, weight, preferred_element_type=F32).astype(BF)
    pre_forward = part_fwd[:128].astype(F32) + send(part_fwd[128:], "row", 1).astype(F32)
    hidden_forward = gelu_value(pre_forward).astype(BF)

    grad_full = jnp.concatenate([grad_pre, send(grad_pre, "row", 1)], axis=0)
    part_in = lax.dot_general(
        grad_full, weight, (((1,), (1,)), ((), ())), preferred_element_type=F32
    ).astype(BF)

    def tokens_of(offset):
        at = (x + offset) % 4
        return lax.dynamic_slice(part_in, (((at // 2) ^ r) * 128 + (at % 2) * 64, 0), (64, 2048))

    grad_inputs = (
        tokens_of(0).astype(F32)
        + send(tokens_of(1), "col", 1).astype(F32)
        + send(tokens_of(3), "col", -1).astype(F32)
        + send(tokens_of(2), "col", 2).astype(F32)
    ).astype(BF)
    return hidden_forward, grad_inputs, grad_weight


def solution(mesh):
    fine = Mesh(mesh.devices.reshape(2, 4, 8, 4), ("row", "col", "z", "y"))
    in_specs = (
        P(("z", "y", "col"), "row"),
        P("row", "col"),
        P(("z", "y", "col"), "row"),
        P(("z", "y", "row"), "col"),
        P(("z", "y", "row"), "col"),
    )
    out_specs = (
        P(("z", "y", "row"), "col"),
        P(("z", "y", "col"), "row"),
        P("row", ("col", "z", "y")),
    )
    return jax.shard_map(
        on_device, mesh=fine, in_specs=in_specs, out_specs=out_specs, check_vma=False
    )
```

time: 386 us -> 146 us (0.38)
  waiting for transfers between devices: 329 us -> 43.2 us
  starting transfers between devices: 0.24 us -> 48.6 us
  between operations: 14.1 us -> 0.96 us
  local copies, waits for them, and re-layouts: 1.42 us -> 13.7 us
  matrix products: 30.9 us -> 19.9 us
  Pallas kernels: 0 us -> 10.7 us
    reduce_scatter x3 -> x0, waiting for transfers between devices: 265 us -> none  [the longest x1 241 us: on_device(): lax.psum_scatter(lax.dot_general(grad_full, gathered_back, (((0,), (0,)),...]
    all_gather x3 -> x0, waiting for transfers between devices: 63.1 us -> none  [the longest x1 26 us: on_device(): lax.all_gather(act_forward, 'col', axis=0, tiled=True)]
    ppermute x0 -> x36, starting transfers between devices: none -> 48.6 us  [the longest x35 48.5 us: send(): return lax.ppermute(value, axis, [(i, (i + step) % n) for i in range(n)])]
    ppermute x0 -> x36, waiting for transfers between devices: none -> 43.2 us  [the longest x35 39.1 us: send(): return lax.ppermute(value, axis, [(i, (i + step) % n) for i in range(n)])]
    dot_general x3 -> x2, matrix products: 30.9 us -> 19.9 us  [the longest x1 10.5 us: on_device(): lax.dot_general(grad_full, weight, (((1,), (1,)), ((), ())), preferred_el...]
    pallas_call x0 -> x3, Pallas kernels: none -> 10.7 us  [the longest x2 8.65 us: weight_part(): pl.pallas_call(part_kernel, grid_spec=pltpu.PrefetchScalarGridSpec(num_sc...]
    dynamic_update_slice x0 -> x4, local copies, waits for them, and re-layouts: none -> 4.79 us  [on_device(): lax.dynamic_update_slice(rows_fwd, block, ((at // 2 ^ r) * 128 + at % 2 *...]
  transfers between devices with their start and end apart: 6 -> 36, of which waited for: 5 -> 11; matrix products, arithmetic and copies ran while one was open for 10% -> 25% of each run, Pallas kernels for 0% -> 7%
where the time goes in v1:
time: 146 us; the launch traced here: 145 us
  starting transfers between devices  48.6 us (33%)
  waiting for transfers between devices  43.2 us (30%)
  matrix products  19.9 us (14%)
  local copies, waits for them, and re-layouts  13.7 us (9%)
  Pallas kernels  10.7 us (7%)
  other arithmetic  7.84 us (5%)
    ppermute x35, starting transfers between devices, send(): return lax.ppermute(value, axis, [(i, (i + step) % n) for i in range(n)])  48.5 us
    ppermute x35, waiting for transfers between devices, send(): return lax.ppermute(value, axis, [(i, (i + step) % n) for i in range(n)])  39.1 us
    dot_general x1, matrix products, on_device(): lax.dot_general(grad_full, weight, (((1,), (1,)), ((), ())), preferred_el...  10.5 us
    dot_general x1, matrix products, on_device(): part_fwd = jnp.dot(rows_fwd, weight, preferred_element_type=F32).astype(BF)  9.45 us
    pallas_call x2, Pallas kernels, weight_part(): pl.pallas_call(part_kernel, grid_spec=pltpu.PrefetchScalarGridSpec(num_sc...  8.65 us
    dynamic_update_slice x4, local copies, waits for them, and re-layouts, on_device(): lax.dynamic_update_slice(rows_fwd, block, ((at // 2 ^ r) * 128 + at % 2 *...  4.79 us
    ppermute x1, waiting for transfers between devices, on_device(): got = lax.ppermute(given, 'y', [(0, 1), (1, 0), (2, 3), (3, 2)]).astype(F32)  4.14 us
    unnamed x12, local copies, waits for them, and re-layouts  3.29 us
  transfers between devices with their start and end apart: 36, of which 11 were waited for; matrix products, arithmetic and copies ran while one was open for 25% of the time, Pallas kernels for 7%

profile of v1, /device:TPU:2, one launch (start us, length us, event | category | flops | bytes accessed | tf_op | source)
XLA Modules:
  0.0 144.9 jit_solution(2590875348773209923)
XLA Ops:
  5.0 2.3 %collective-permute-start = (bf16[64,2048]{1,0:T(8,128)(2,1)}, bf16[64,2048]{1,0:T(8,128)(2,1)}, u32[]{:S(2)}, u32[]{:S(2)}) collective-permute-start(bf16[64,2048]{1,0:T(8,128)(2,1)} %param.5), channel_id=1, source_target_pairs={{0,96},{32,0},{64,32},{96,64},{1,97},{33,1},{65,33},{97,65},{2,98}... | collective-permute-start | bytes 786440 | tf_op jit(solution)/shard_map/ppermute | solution.py:30
  22.3 2.9 %collective-permute-start.9 = (bf16[1792,128]{1,0:T(8,128)(2,1)S(1)}, bf16[1792,128]{1,0:T(8,128)(2,1)S(1)}, u32[]{:S(2)}, u32[]{:S(2)}) collective-permute-start(bf16[1792,128]{1,0:T(8,128)(2,1)S(1)} %bitcast.75), channel_id=1, source_target_pairs={{0,3},{1,0},{2,1},{3,2},{4,7},{5,4},{6,5},{7,6},{8,11},{9,8},{10,9... | collective-permute-start | bytes 1376264 | tf_op jit(solution)/shard_map/ppermute | solution.py:30
  29.5 9.5 %convolution_convert_fusion = bf16[256,3584]{1,0:T(8,128)(2,1)S(1)} fusion(bf16[256,2048]{1,0:T(8,128)(2,1)} %constant_dynamic-update-slice_fusion, bf16[2048,3584]{1,0:T(8,128)(2,1)} %param.6), kind=kOutput, calls=%fused_computation | convolution fusion | flops 3759013888 | bytes 17563648 | tf_op jit(solution)/shard_map/dot_general | solution.py:165
  40.0 2.9 %collective-permute-start.16 = (bf16[256,512]{1,0:T(8,128)(2,1)S(1)}, bf16[256,512]{1,0:T(8,128)(2,1)}, u32[]{:S(2)}, u32[]{:S(2)}) collective-permute-start(bf16[256,512]{1,0:T(8,128)(2,1)S(1)} %get-tuple-element.26.b0), channel_id=1, source_target_pairs={{0,64},{32,96},{64,0},{96,32},{1,65},{33,97},{65,1},{97,33},{2,66}... | collective-permute-start | bytes 786440 | tf_op jit(solution)/shard_map/ppermute | solution.py:30
  45.5 10.5 %convolution_convert_fusion.1 = bf16[256,2048]{1,0:T(8,128)(2,1)} fusion(bf16[2048,3584]{1,0:T(8,128)(2,1)} %param.6, bf16[128,3584]{1,0:T(8,128)(2,1)} %copy-done.5, bf16[128,3584]{1,0:T(8,128)(2,1)S(1)} %get-tuple-element.5), kind=kOutput, calls=%fused_computation.2 | convolution fusion | flops 3762290688 | bytes 17563648 | tf_op jit(solution)/shard_map/dot_general | solution.py:170
  58.3 3.1 %fusion.4 = bf16[128,3584]{1,0:T(8,128)(2,1)} fusion(bf16[128,3584]{1,0:T(8,128)(2,1)} %collective-permute-done.3, bf16[256,3584]{1,0:T(8,128)(2,1)} %copy-done.2), kind=kLoop, calls=%fused_computation.7 | loop fusion | flops 5505024 | bytes 2752512 | tf_op jit(solution)/shard_map/convert_element_type | solution.py:167
  62.6 2.6 %collective-permute-start.27 = (bf16[256,512]{1,0:T(8,128)(2,1)S(1)}, bf16[256,512]{1,0:T(8,128)(2,1)S(1)}, u32[]{:S(2)}, u32[]{:S(2)}) collective-permute-start(bf16[256,512]{1,0:T(8,128)(2,1)S(1)} %get-tuple-element.27.b0), channel_id=1, source_target_pairs={{0,32},{32,64},{64,96},{96,0},{1,33},{33,65},{65,97},{97,1},{2,34}... | collective-permute-start | bytes 786440 | tf_op jit(solution)/shard_map/ppermute | solution.py:30
  67.2 4.9 %shard_map.77 = bf16[1792,512]{1,0:T(8,128)(2,1)S(1)} custom-call(s32[2]{0:T(128)S(1)} %pad_add_fusion.place_ref, bf16[1792,512]{1,0:T(8,128)(2,1)S(1)} %pad_maximum_fusion.own_ref, bf16[1792,512]{1,0:T(8,128)(2,1)S(1)} %collective-permute-done.11.oth_ref, bf16[256,512]{1,0:T(8,128)(2,1)S(1)} %get-tuple-element.26.b0, ...), custom_call_target="tpu_custom_call" | custom-call | flops 1879048192 | bytes 5505024 | tf_op jit(solution)/shard_map/pallas_call | solution.py:81
  72.2 2.9 %collective-permute-start.7 = (bf16[64,2048]{1,0:T(8,128)(2,1)S(1)}, bf16[64,2048]{1,0:T(8,128)(2,1)S(1)}, u32[]{:S(2)}, u32[]{:S(2)}) collective-permute-start(bf16[64,2048]{1,0:T(8,128)(2,1)S(1)} %get-tuple-element.20), channel_id=1, source_target_pairs={{0,64},{32,96},{64,0},{96,32},{1,65},{33,97},{65,1},{97,33},{2,66}... | collective-permute-start | bytes 786440 | tf_op jit(solution)/shard_map/ppermute | solution.py:30
  75.1 2.3 %collective-permute-start.18 = (bf16[224,512]{1,0:T(8,128)(2,1)S(1)}, bf16[224,512]{1,0:T(8,128)(2,1)S(1)}, u32[]{:S(2)}, u32[]{:S(2)}) collective-permute-start(bf16[224,512]{1,0:T(8,128)(2,1)S(1)} %get-tuple-element.11), channel_id=1, source_target_pairs={{0,4},{4,8},{8,12},{12,16},{16,20},{20,24},{24,28},{28,0},{1,5},{5... | collective-permute-start | bytes 688136 | tf_op jit(solution)/shard_map/ppermute | solution.py:30
  77.3 5.8 %collective-permute-start.22 = (bf16[224,512]{1,0:T(8,128)(2,1)S(1)}, bf16[224,512]{1,0:T(8,128)(2,1)S(1)}, u32[]{:S(2)}, u32[]{:S(2)}) collective-permute-start(bf16[224,512]{1,0:T(8,128)(2,1)S(1)} %get-tuple-element.12), channel_id=1, source_target_pairs={{0,28},{4,0},{8,4},{12,8},{16,12},{20,16},{24,20},{28,24},{1,29},{... | collective-permute-start | bytes 688136 | tf_op jit(solution)/shard_map/ppermute | solution.py:30
  83.2 3.8 %shard_map.78 = bf16[1792,512]{1,0:T(8,128)(2,1)S(1)} custom-call(s32[2]{0:T(128)S(1)} %pad_add_fusion.place_ref, bf16[1792,512]{1,0:T(8,128)(2,1)S(1)} %pad_maximum_fusion.own_ref, bf16[1792,512]{1,0:T(8,128)(2,1)S(1)} %collective-permute-done.11.oth_ref, bf16[256,512]{1,0:T(8,128)(2,1)S(1)} %get-tuple-element.27.b0, ...), custom_call_target="tpu_custom_call" | custom-call | flops 1879048192 | bytes 5505024 | tf_op jit(solution)/shard_map/pallas_call | solution.py:81
  88.1 5.0 %collective-permute-done.28 = bf16[224,512]{1,0:T(8,128)(2,1)S(1)} collective-permute-done((bf16[224,512]{1,0:T(8,128)(2,1)S(1)}, bf16[224,512]{1,0:T(8,128)(2,1)S(1)}, u32[]{:S(2)}, u32[]{:S(2)}) %collective-permute-start.28) | collective-permute-done | bytes 229408 | tf_op jit(solution)/shard_map/ppermute | solution.py:30
  93.3 7.6 %collective-permute-done.19 = bf16[224,512]{1,0:T(8,128)(2,1)S(1)} collective-permute-done((bf16[224,512]{1,0:T(8,128)(2,1)S(1)}, bf16[224,512]{1,0:T(8,128)(2,1)S(1)}, u32[]{:S(2)}, u32[]{:S(2)}) %collective-permute-start.19) | collective-permute-done | bytes 229408 | tf_op jit(solution)/shard_map/ppermute | solution.py:30
  103.8 4.9 %collective-permute-done.29 = bf16[224,512]{1,0:T(8,128)(2,1)S(1)} collective-permute-done((bf16[224,512]{1,0:T(8,128)(2,1)S(1)}, bf16[224,512]{1,0:T(8,128)(2,1)S(1)}, u32[]{:S(2)}, u32[]{:S(2)}) %collective-permute-start.29) | collective-permute-done | bytes 229408 | tf_op jit(solution)/shard_map/ppermute | solution.py:30
  108.7 3.6 %collective-permute-start.23 = (bf16[224,512]{1,0:T(8,128)(2,1)S(1)}, bf16[224,512]{1,0:T(8,128)(2,1)S(1)}, u32[]{:S(2)}, u32[]{:S(2)}) collective-permute-start(bf16[224,512]{1,0:T(8,128)(2,1)S(1)} %get-tuple-element.10), channel_id=1, source_target_pairs={{0,28},{4,0},{8,4},{12,8},{16,12},{20,16},{24,20},{28,24},{1,29},{... | collective-permute-start | bytes 688136 | tf_op jit(solution)/shard_map/ppermute | solution.py:30
  112.5 3.4 %collective-permute-done.23 = bf16[224,512]{1,0:T(8,128)(2,1)S(1)} collective-permute-done((bf16[224,512]{1,0:T(8,128)(2,1)S(1)}, bf16[224,512]{1,0:T(8,128)(2,1)S(1)}, u32[]{:S(2)}, u32[]{:S(2)}) %collective-permute-start.23) | collective-permute-done | bytes 229408 | tf_op jit(solution)/shard_map/ppermute | solution.py:30
  115.9 2.9 %collective-permute-done.30 = bf16[224,512]{1,0:T(8,128)(2,1)S(1)} collective-permute-done((bf16[224,512]{1,0:T(8,128)(2,1)S(1)}, bf16[224,512]{1,0:T(8,128)(2,1)S(1)}, u32[]{:S(2)}, u32[]{:S(2)}) %collective-permute-start.30) | collective-permute-done | bytes 229408 | tf_op jit(solution)/shard_map/ppermute | solution.py:30
  118.9 4.7 %collective-permute-done.33 = bf16[224,512]{1,0:T(8,128)(2,1)S(1)} collective-permute-done((bf16[224,512]{1,0:T(8,128)(2,1)S(1)}, bf16[224,512]{1,0:T(8,128)(2,1)S(1)}, u32[]{:S(2)}, u32[]{:S(2)}) %collective-permute-start.33) | collective-permute-done | bytes 229408 | tf_op jit(solution)/shard_map/ppermute | solution.py:30
  125.6 2.3 %collective-permute-done.21 = bf16[224,512]{1,0:T(8,128)(2,1)S(1)} collective-permute-done((bf16[224,512]{1,0:T(8,128)(2,1)S(1)}, bf16[224,512]{1,0:T(8,128)(2,1)S(1)}, u32[]{:S(2)}, u32[]{:S(2)}) %collective-permute-start.21) | collective-permute-done | bytes 229408 | tf_op jit(solution)/shard_map/ppermute | solution.py:30
  127.9 2.3 %collective-permute-start.31 = (bf16[224,512]{1,0:T(8,128)(2,1)S(1)}, bf16[224,512]{1,0:T(8,128)(2,1)S(1)}, u32[]{:S(2)}, u32[]{:S(2)}) collective-permute-start(bf16[224,512]{1,0:T(8,128)(2,1)S(1)} %get-tuple-element.13), channel_id=1, source_target_pairs={{0,28},{4,0},{8,4},{12,8},{16,12},{20,16},{24,20},{28,24},{1,29},{... | collective-permute-start | bytes 688136 | tf_op jit(solution)/shard_map/ppermute | solution.py:30
  130.4 3.6 %collective-permute-done.31 = bf16[224,512]{1,0:T(8,128)(2,1)S(1)} collective-permute-done((bf16[224,512]{1,0:T(8,128)(2,1)S(1)}, bf16[224,512]{1,0:T(8,128)(2,1)S(1)}, u32[]{:S(2)}, u32[]{:S(2)}) %collective-permute-start.31) | collective-permute-done | bytes 229408 | tf_op jit(solution)/shard_map/ppermute | solution.py:30
  134.0 3.6 %collective-permute-done.34 = bf16[224,512]{1,0:T(8,128)(2,1)S(1)} collective-permute-done((bf16[224,512]{1,0:T(8,128)(2,1)S(1)}, bf16[224,512]{1,0:T(8,128)(2,1)S(1)}, u32[]{:S(2)}, u32[]{:S(2)}) %collective-permute-start.34) | collective-permute-done | bytes 229408 | tf_op jit(solution)/shard_map/ppermute | solution.py:30
  139.7 4.1 %collective-permute-done.35 = bf16[112,1024]{1,0:T(8,128)(2,1)S(1)} collective-permute-done((bf16[112,1024]{1,0:T(8,128)(2,1)S(1)}, bf16[112,1024]{1,0:T(8,128)(2,1)S(1)}, u32[]{:S(2)}, u32[]{:S(2)}) %collective-permute-start.35) | collective-permute-done | bytes 229408 | tf_op jit(solution)/shard_map/ppermute | solution.py:154
  (95 shorter events, 42.5 us)
Async XLA Ops:
  1.7 15.7 %collective-permute-start.12 = (bf16[64,1024]{1,0:T(8,128)(2,1)S(1)}, bf16[64,1024]{1,0:T(8,128)(2,1)S(1)}, u32[]{:S(2)}, u32[]{:S(2)}) collective-permute-start(bf16[64,1024]{1,0:T(8,128)(2,1)S(1)} %get-tuple-element.28), channel_id=1, source_target_pairs={{0,1},{1,2},{2,3},{3,0},{4,5},{5,6},{6,7},{7,4},{8,9},{9,10},{10,1... | collective-permute-start | bytes 393224 | tf_op jit(solution)/shard_map/ppermute | solution.py:30
  3.4 15.9 %collective-permute-start.13 = (bf16[64,1024]{1,0:T(8,128)(2,1)S(1)}, bf16[64,1024]{1,0:T(8,128)(2,1)}, u32[]{:S(2)}, u32[]{:S(2)}) collective-permute-start(bf16[64,1024]{1,0:T(8,128)(2,1)S(1)} %get-tuple-element.28), channel_id=1, source_target_pairs={{0,3},{1,0},{2,1},{3,2},{4,7},{5,4},{6,5},{7,6},{8,11},{9,8},{10,9... | collective-permute-start | bytes 393224 | tf_op jit(solution)/shard_map/ppermute | solution.py:30
  5.0 17.3 %collective-permute-start = (bf16[64,2048]{1,0:T(8,128)(2,1)}, bf16[64,2048]{1,0:T(8,128)(2,1)}, u32[]{:S(2)}, u32[]{:S(2)}) collective-permute-start(bf16[64,2048]{1,0:T(8,128)(2,1)} %param.5), channel_id=1, source_target_pairs={{0,96},{32,0},{64,32},{96,64},{1,97},{33,1},{65,33},{97,65},{2,98}... | collective-permute-start | bytes 786440 | tf_op jit(solution)/shard_map/ppermute | solution.py:30
  7.3 19.6 %collective-permute-start.1 = (bf16[64,2048]{1,0:T(8,128)(2,1)}, bf16[64,2048]{1,0:T(8,128)(2,1)}, u32[]{:S(2)}, u32[]{:S(2)}) collective-permute-start(bf16[64,2048]{1,0:T(8,128)(2,1)} %param.5), channel_id=1, source_target_pairs={{0,64},{32,96},{64,0},{96,32},{1,65},{33,97},{65,1},{97,33},{2,66}... | collective-permute-start | bytes 786440 | tf_op jit(solution)/shard_map/ppermute | solution.py:30
  8.0 12.8 %collective-permute-start.14 = (bf16[64,1024]{1,0:T(8,128)(2,1)S(1)}, bf16[64,1024]{1,0:T(8,128)(2,1)}, u32[]{:S(2)}, u32[]{:S(2)}) collective-permute-start(bf16[64,1024]{1,0:T(8,128)(2,1)S(1)} %get-tuple-element.29), channel_id=1, source_target_pairs={{0,2},{1,3},{2,0},{3,1},{4,6},{5,7},{6,4},{7,5},{8,10},{9,11},{10,... | collective-permute-start | bytes 393224 | tf_op jit(solution)/shard_map/ppermute | solution.py:30
  17.4 11.2 %collective-permute-start.2 = (bf16[64,2048]{1,0:T(8,128)(2,1)S(1)}, bf16[64,2048]{1,0:T(8,128)(2,1)S(1)}, u32[]{:S(2)}, u32[]{:S(2)}) collective-permute-start(bf16[64,2048]{1,0:T(8,128)(2,1)S(1)} %copy-done.3), channel_id=1, source_target_pairs={{0,32},{32,64},{64,96},{96,0},{1,33},{33,65},{65,97},{97,1},{2,34}... | collective-permute-start | bytes 786440 | tf_op jit(solution)/shard_map/ppermute | solution.py:30
  19.2 20.8 %collective-permute-start.10 = (bf16[1792,128]{1,0:T(8,128)(2,1)}, bf16[1792,128]{1,0:T(8,128)(2,1)S(1)}, u32[]{:S(2)}, u32[]{:S(2)}) collective-permute-start(bf16[1792,128]{1,0:T(8,128)(2,1)} %bitcast.77), channel_id=1, source_target_pairs={{0,2},{1,3},{2,0},{3,1},{4,6},{5,7},{6,4},{7,5},{8,10},{9,11},{10,... | collective-permute-start | bytes 1376264 | tf_op jit(solution)/shard_map/ppermute | solution.py:30
  20.8 22.1 %collective-permute-start.8 = (bf16[1792,128]{1,0:T(8,128)(2,1)}, bf16[1792,128]{1,0:T(8,128)(2,1)S(1)}, u32[]{:S(2)}, u32[]{:S(2)}) collective-permute-start(bf16[1792,128]{1,0:T(8,128)(2,1)} %bitcast.76), channel_id=1, source_target_pairs={{0,1},{1,2},{2,3},{3,0},{4,5},{5,6},{6,7},{7,4},{8,9},{9,10},{10,1... | collective-permute-start | bytes 1376264 | tf_op jit(solution)/shard_map/ppermute | solution.py:30
  22.3 21.6 %collective-permute-start.9 = (bf16[1792,128]{1,0:T(8,128)(2,1)S(1)}, bf16[1792,128]{1,0:T(8,128)(2,1)S(1)}, u32[]{:S(2)}, u32[]{:S(2)}) collective-permute-start(bf16[1792,128]{1,0:T(8,128)(2,1)S(1)} %bitcast.75), channel_id=1, source_target_pairs={{0,3},{1,0},{2,1},{3,2},{4,7},{5,4},{6,5},{7,6},{8,11},{9,8},{10,9... | collective-permute-start | bytes 1376264 | tf_op jit(solution)/shard_map/ppermute | solution.py:30
  26.9 17.2 %collective-permute-start.4 = (bf16[128,3584]{1,0:T(8,128)(2,1)S(1)}, bf16[128,3584]{1,0:T(8,128)(2,1)S(1)}, u32[]{:S(2)}, u32[]{:S(2)}) collective-permute-start(bf16[128,3584]{1,0:T(8,128)(2,1)S(1)} %get-tuple-element.5), channel_id=1, source_target_pairs={{0,128},{128,0},{1,129},{129,1},{2,130},{130,2},{3,131},{131,3},{4... | collective-permute-start | bytes 2752520 | tf_op jit(solution)/shard_map/ppermute | solution.py:30
  28.6 32.9 %collective-permute-start.15 = (bf16[256,512]{1,0:T(8,128)(2,1)S(1)}, bf16[256,512]{1,0:T(8,128)(2,1)}, u32[]{:S(2)}, u32[]{:S(2)}) collective-permute-start(bf16[256,512]{1,0:T(8,128)(2,1)S(1)} %get-tuple-element.26.b0), channel_id=1, source_target_pairs={{0,96},{32,0},{64,32},{96,64},{1,97},{33,1},{65,33},{97,65},{2,98}... | collective-permute-start | bytes 786440 | tf_op jit(solution)/shard_map/ppermute | solution.py:30
  40.0 22.5 %collective-permute-start.16 = (bf16[256,512]{1,0:T(8,128)(2,1)S(1)}, bf16[256,512]{1,0:T(8,128)(2,1)}, u32[]{:S(2)}, u32[]{:S(2)}) collective-permute-start(bf16[256,512]{1,0:T(8,128)(2,1)S(1)} %get-tuple-element.26.b0), channel_id=1, source_target_pairs={{0,64},{32,96},{64,0},{96,32},{1,65},{33,97},{65,1},{97,33},{2,66}... | collective-permute-start | bytes 786440 | tf_op jit(solution)/shard_map/ppermute | solution.py:30
  42.9 22.3 %collective-permute-start.17 = (bf16[256,512]{1,0:T(8,128)(2,1)S(1)}, bf16[256,512]{1,0:T(8,128)(2,1)}, u32[]{:S(2)}, u32[]{:S(2)}) collective-permute-start(bf16[256,512]{1,0:T(8,128)(2,1)S(1)} %get-tuple-element.26.b0), channel_id=1, source_target_pairs={{0,32},{32,64},{64,96},{96,0},{1,33},{33,65},{65,97},{97,1},{2,34}... | collective-permute-start | bytes 786440 | tf_op jit(solution)/shard_map/ppermute | solution.py:30
  43.8 13.3 %collective-permute-start.3 = (bf16[128,3584]{1,0:T(8,128)(2,1)}, bf16[128,3584]{1,0:T(8,128)(2,1)}, u32[]{:S(2)}, u32[]{:S(2)}) collective-permute-start(bf16[128,3584]{1,0:T(8,128)(2,1)} %slice.17), channel_id=1, source_target_pairs={{0,128},{128,0},{1,129},{129,1},{2,130},{130,2},{3,131},{131,3},{4... | collective-permute-start | bytes 2752520 | tf_op jit(solution)/shard_map/ppermute | solution.py:30
  45.0 20.5 %collective-permute-start.11 = (bf16[1792,512]{1,0:T(8,128)(2,1)S(1)}, bf16[1792,512]{1,0:T(8,128)(2,1)S(1)}, u32[]{:S(2)}, u32[]{:S(2)}) collective-permute-start(bf16[1792,512]{1,0:T(8,128)(2,1)S(1)} %pad_maximum_fusion.own_ref), channel_id=1, source_target_pairs={{0,128},{128,0},{1,129},{129,1},{2,130},{130,2},{3,131},{131,3},{4... | collective-permute-start | bytes 5505032 | tf_op jit(solution)/shard_map/ppermute | solution.py:30
  57.2 15.0 %collective-permute-start.25 = (bf16[256,512]{1,0:T(8,128)(2,1)S(1)}, bf16[256,512]{1,0:T(8,128)(2,1)S(1)}, u32[]{:S(2)}, u32[]{:S(2)}) collective-permute-start(bf16[256,512]{1,0:T(8,128)(2,1)S(1)} %get-tuple-element.27.b0), channel_id=1, source_target_pairs={{0,96},{32,0},{64,32},{96,64},{1,97},{33,1},{65,33},{97,65},{2,98}... | collective-permute-start | bytes 786440 | tf_op jit(solution)/shard_map/ppermute | solution.py:30
  61.5 13.6 %collective-permute-start.26 = (bf16[256,512]{1,0:T(8,128)(2,1)S(1)}, bf16[256,512]{1,0:T(8,128)(2,1)S(1)}, u32[]{:S(2)}, u32[]{:S(2)}) collective-permute-start(bf16[256,512]{1,0:T(8,128)(2,1)S(1)} %get-tuple-element.27.b0), channel_id=1, source_target_pairs={{0,64},{32,96},{64,0},{96,32},{1,65},{33,97},{65,1},{97,33},{2,66}... | collective-permute-start | bytes 786440 | tf_op jit(solution)/shard_map/ppermute | solution.py:30
  62.6 14.8 %collective-permute-start.27 = (bf16[256,512]{1,0:T(8,128)(2,1)S(1)}, bf16[256,512]{1,0:T(8,128)(2,1)S(1)}, u32[]{:S(2)}, u32[]{:S(2)}) collective-permute-start(bf16[256,512]{1,0:T(8,128)(2,1)S(1)} %get-tuple-element.27.b0), channel_id=1, source_target_pairs={{0,32},{32,64},{64,96},{96,0},{1,33},{33,65},{65,97},{97,1},{2,34}... | collective-permute-start | bytes 786440 | tf_op jit(solution)/shard_map/ppermute | solution.py:30
  65.2 72.7 %collective-permute-start.5 = (bf16[64,2048]{1,0:T(8,128)(2,1)S(1)}, bf16[64,2048]{1,0:T(8,128)(2,1)S(1)}, u32[]{:S(2)}, u32[]{:S(2)}) collective-permute-start(bf16[64,2048]{1,0:T(8,128)(2,1)S(1)} %get-tuple-element.19), channel_id=1, source_target_pairs={{0,32},{32,64},{64,96},{96,0},{1,33},{33,65},{65,97},{97,1},{2,34}... | collective-permute-start | bytes 786440 | tf_op jit(solution)/shard_map/ppermute | solution.py:30
  65.6 72.3 %collective-permute-start.6 = (bf16[64,2048]{1,0:T(8,128)(2,1)S(1)}, bf16[64,2048]{1,0:T(8,128)(2,1)S(1)}, u32[]{:S(2)}, u32[]{:S(2)}) collective-permute-start(bf16[64,2048]{1,0:T(8,128)(2,1)S(1)} %get-tuple-element.21), channel_id=1, source_target_pairs={{0,96},{32,0},{64,32},{96,64},{1,97},{33,1},{65,33},{97,65},{2,98}... | collective-permute-start | bytes 786440 | tf_op jit(solution)/shard_map/ppermute | solution.py:30
  72.2 65.7 %collective-permute-start.7 = (bf16[64,2048]{1,0:T(8,128)(2,1)S(1)}, bf16[64,2048]{1,0:T(8,128)(2,1)S(1)}, u32[]{:S(2)}, u32[]{:S(2)}) collective-permute-start(bf16[64,2048]{1,0:T(8,128)(2,1)S(1)} %get-tuple-element.20), channel_id=1, source_target_pairs={{0,64},{32,96},{64,0},{96,32},{1,65},{33,97},{65,1},{97,33},{2,66}... | collective-permute-start | bytes 786440 | tf_op jit(solution)/shard_map/ppermute | solution.py:30
  75.1 11.9 %collective-permute-start.18 = (bf16[224,512]{1,0:T(8,128)(2,1)S(1)}, bf16[224,512]{1,0:T(8,128)(2,1)S(1)}, u32[]{:S(2)}, u32[]{:S(2)}) collective-permute-start(bf16[224,512]{1,0:T(8,128)(2,1)S(1)} %get-tuple-element.11), channel_id=1, source_target_pairs={{0,4},{4,8},{8,12},{12,16},{16,20},{20,24},{24,28},{28,0},{1,5},{5... | collective-permute-start | bytes 688136 | tf_op jit(solution)/shard_map/ppermute | solution.py:30
  77.3 15.8 %collective-permute-start.22 = (bf16[224,512]{1,0:T(8,128)(2,1)S(1)}, bf16[224,512]{1,0:T(8,128)(2,1)S(1)}, u32[]{:S(2)}, u32[]{:S(2)}) collective-permute-start(bf16[224,512]{1,0:T(8,128)(2,1)S(1)} %get-tuple-element.12), channel_id=1, source_target_pairs={{0,28},{4,0},{8,4},{12,8},{16,12},{20,16},{24,20},{28,24},{1,29},{... | collective-permute-start | bytes 688136 | tf_op jit(solution)/shard_map/ppermute | solution.py:30
  93.1 10.6 %collective-permute-start.32 = (bf16[224,512]{1,0:T(8,128)(2,1)S(1)}, bf16[224,512]{1,0:T(8,128)(2,1)S(1)}, u32[]{:S(2)}, u32[]{:S(2)}) collective-permute-start(bf16[224,512]{1,0:T(8,128)(2,1)S(1)} %get-tuple-element.18), channel_id=1, source_target_pairs={{0,4},{4,8},{8,12},{12,16},{16,20},{20,24},{24,28},{28,0},{1,5},{5... | collective-permute-start | bytes 688136 | tf_op jit(solution)/shard_map/ppermute | solution.py:30
  (18 other events, 113.5 us)

commit v2 on v0

v2 whole, which is shorter than its diff:
```python
import functools
import math

import jax
import jax.numpy as jnp
from jax import lax
from jax.experimental import pallas as pl
from jax.experimental.pallas import tpu as pltpu
from jax.sharding import Mesh, PartitionSpec as P

coeff = math.sqrt(2.0 / math.pi)
BF = jnp.bfloat16
F32 = jnp.float32
SIZES = {"row": 2, "col": 4, "z": 8, "y": 4}


def gelu_value(v):
    inner = coeff * (v + 0.044715 * v * v * v)
    return 0.5 * v * (1.0 + jnp.tanh(inner))


def gelu_slope(v):
    tanh_part = jnp.tanh(coeff * (v + 0.044715 * v * v * v))
    return 0.5 * (1.0 + tanh_part) + 0.5 * v * (1.0 - tanh_part * tanh_part) * coeff * (
        1.0 + 3.0 * 0.044715 * v * v
    )


def send(value, axis, step):
    n = SIZES[axis]
    return lax.ppermute(value, axis, [(i, (i + step) % n) for i in range(n)])


def together(*values):
    return lax.optimization_barrier(values)


VMEM = pl.BlockSpec(memory_space=pltpu.VMEM)
SMEM = pl.BlockSpec(memory_space=pltpu.SMEM)


def params(mib):
    return pltpu.CompilerParams(vmem_limit_bytes=mib * 2**20)


def grad_kernel(pre_ref, grad_ref, flip_ref, parts_ref):
    g = grad_ref[...].astype(F32) * gelu_slope(pre_ref[...].astype(F32))
    flip = g.T.astype(BF)
    flip_ref[...] = flip
    for k in range(2):
        for q in range(4):
            block = flip[k * 448 + q * 112 : k * 448 + q * 112 + 112]
            parts_ref[q ^ 1, 0, k * 112 : k * 112 + 112] = block
            parts_ref[q, 1, k * 112 : k * 112 + 112] = block


def grad_pre_flipped(pre, grad):
    rows, cols = pre.shape
    tile = 896
    return pl.pallas_call(
        grad_kernel,
        grid=(cols // tile,),
        in_specs=[pl.BlockSpec((rows, tile), lambda i: (0, i))] * 2,
        out_specs=[
            pl.BlockSpec((tile, rows), lambda i: (i, 0)),
            pl.BlockSpec((4, 2, tile // 4, rows), lambda i: (0, 0, i, 0)),
        ],
        out_shape=[
            jax.ShapeDtypeStruct((cols, rows), BF),
            jax.ShapeDtypeStruct((4, 2, cols // 4, rows), BF),
        ],
        compiler_params=params(60),
        cost_estimate=pl.CostEstimate(
            flops=30 * rows * cols, bytes_accessed=10 * rows * cols, transcendentals=rows * cols
        ),
    )(pre, grad)


def copy_acts(place_ref, blocks, acts, sems):
    x, r, y = place_ref[0], place_ref[1], place_ref[2]
    copies = []
    for d, block in enumerate(blocks):
        at = lax.rem(x + d, 4)
        start = ((at // 2) ^ r) * 512 + lax.rem(at, 2) * 64
        for j, turn in enumerate((0, 3, 1, 2)):
            row = pl.multiple_of(start + lax.rem(y + turn, 4) * 128, 64)
            copies.append((block.at[pl.ds(j * 64, 64), :], acts.at[pl.ds(row, 64), :]))
    return [pltpu.make_async_copy(a, b, sems.at[n]) for n, (a, b) in enumerate(copies)]


def first_kernel(wanted, place_ref, own_ref, oth_ref, b0, b1, b2, b3, *rest):
    outs, (acts, lhs, sems) = rest[:-3], rest[-3:]
    z = place_ref[3]
    copies = copy_acts(place_ref, (b0, b1, b2, b3), acts, sems)
    for i, (which, offset) in enumerate(wanted):
        rows = pl.ds(pl.multiple_of(lax.rem(z + offset, 8) * 112, 16), 112)
        for h, ref in enumerate((own_ref, oth_ref)):
            for k in range(4):
                to = lhs.at[pl.ds(i * 112, 112), pl.ds(h * 512 + k * 128, 128)]
                sem = sems.at[len(copies)]
                copies.append(pltpu.make_async_copy(ref.at[k, which, rows, :], to, sem))
    for copy in copies:
        copy.start()
    for copy in copies:
        copy.wait()
    part = jnp.dot(lhs[...], acts[...], preferred_element_type=F32)
    for i, out in enumerate(outs):
        out[...] = part[i * 112 : i * 112 + 112].astype(BF)


def rest_kernel(wanted, place_ref, own_ref, oth_ref, b0, b1, b2, b3, *rest):
    outs, (acts, lhs, sems) = rest[:-3], rest[-3:]
    z = place_ref[3]
    copies = copy_acts(place_ref, (b0, b1, b2, b3), acts, sems)
    for which in range(2):
        for h, ref in enumerate((own_ref, oth_ref)):
            for k in range(4):
                to = lhs.at[which, :, pl.ds(h * 512 + k * 128, 128)]
                copies.append(pltpu.make_async_copy(ref.at[k, which], to, sems.at[len(copies)]))
    for copy in copies:
        copy.start()
    for copy in copies:
        copy.wait()
    for i in range(0, len(wanted), 4):
        rows = [
            lhs[which, pl.ds(pl.multiple_of(lax.rem(z + offset, 8) * 112, 16), 112), :]
            for which, offset in wanted[i : i + 4]
        ]
        part = jnp.dot(jnp.concatenate(rows, axis=0), acts[...], preferred_element_type=F32)
        for k in range(4):
            outs[i + k][...] = part[k * 112 : k * 112 + 112].astype(BF)


def weight_parts(place, own, oth, blocks, wanted, first):
    anywhere = pl.BlockSpec(memory_space=pl.ANY)
    n = len(wanted)
    return pl.pallas_call(
        functools.partial(first_kernel if first else rest_kernel, wanted),
        grid=(1,),
        in_specs=[SMEM] + [anywhere] * 6,
        out_specs=[pl.BlockSpec((112, 1024), lambda i: (0, 0))] * n,
        scratch_shapes=[
            pltpu.VMEM((1024, 1024), BF),
            pltpu.VMEM((112 * n, 1024) if first else (2, 896, 1024), BF),
            pltpu.SemaphoreType.DMA((16 + (8 * n if first else 16),)),
        ],
        out_shape=[jax.ShapeDtypeStruct((112, 1024), BF)] * n,
        compiler_params=params(60),
        cost_estimate=pl.CostEstimate(flops=2**20, bytes_accessed=2**20, transcendentals=0),
    )(place, own, oth, *blocks)


def both_kernel(place_ref, f0, f1, f2, f3, own_ref, oth_ref, w_ref, keep_ref, give_ref, o0, o1, o2, o3, rows_ref, acc):
    step, last = pl.program_id(0), pl.num_programs(0) - 1
    x, r = place_ref[0], place_ref[1]

    @pl.when(step == 0)
    def _():
        for d, ref in enumerate((f0, f1, f2, f3)):
            at = lax.rem(x + d, 4)
            row = ((at // 2) ^ r) * 128 + lax.rem(at, 2) * 64
            rows_ref[pl.ds(pl.multiple_of(row, 64), 64), :] = ref[...]

    w = w_ref[...]
    part = jnp.dot(rows_ref[...], w, preferred_element_type=F32).astype(BF)
    keep_ref[...] = part[:128]
    give_ref[...] = part[128:]
    both = jnp.concatenate([own_ref[...], oth_ref[...]], axis=1)
    more = jnp.dot(w, both, preferred_element_type=F32)

    @pl.when(step == 0)
    def _():
        acc[...] = more

    @pl.when(step > 0)
    def _():
        acc[...] += more

    @pl.when(step == last)
    def _():
        flat = acc[...].T.astype(BF)
        rows_ref[...] = flat
        for d, out in enumerate((o0, o1, o2, o3)):
            at = lax.rem(x + d, 4)
            row = ((at // 2) ^ r) * 128 + lax.rem(at, 2) * 64
            out[...] = rows_ref[pl.ds(pl.multiple_of(row, 64), 64), :]


def both_products(place, fwd, own, oth, weight):
    feats, hidden = weight.shape
    tile = 512
    return pl.pallas_call(
        both_kernel,
        grid=(hidden // tile,),
        in_specs=[SMEM]
        + [pl.BlockSpec((64, feats), lambda i: (0, 0))] * 4
        + [pl.BlockSpec((tile, 128), lambda i: (i, 0))] * 2
        + [pl.BlockSpec((feats, tile), lambda i: (0, i))],
        out_specs=[pl.BlockSpec((128, tile), lambda i: (0, i))] * 2
        + [pl.BlockSpec((64, feats), lambda i: (0, 0))] * 4,
        out_shape=[jax.ShapeDtypeStruct((128, hidden), BF)] * 2
        + [jax.ShapeDtypeStruct((64, feats), BF)] * 4,
        scratch_shapes=[pltpu.VMEM((256, feats), BF), pltpu.VMEM((feats, 256), F32)],
        compiler_params=params(60),
        cost_estimate=pl.CostEstimate(
            flops=4 * 256 * 2048 * hidden, bytes_accessed=2 * 2048 * hidden, transcendentals=0
        ),
    )(place, *fwd, own, oth, weight)


def reduce_z(piece, step):
    far, near = piece[4], piece[-3 * step % 8]
    for hop in (3, 2, 1, 0):
        far = send(far, "z", step)
        if hop >= 1:
            near = send(near, "z", -step)
            far = far + piece[hop * step % 8]
            if hop > 1:
                near = near + piece[-(hop - 1) * step % 8]
    return piece[0].astype(F32) + far.astype(F32) + near.astype(F32)


def on_device(act_forward, weight, act_backward, pre_backward, grad_backward):
    r, x, z, y = (lax.axis_index(name) for name in ("row", "col", "z", "y"))
    ym = y % 2
    place = jnp.stack([x, r, y, z]).astype(jnp.int32)

    left, right = send(act_forward, "col", 1), send(act_forward, "col", -1)

    same = lax.dynamic_slice(act_backward, (0, ym * 1024), (64, 1024))
    other = lax.dynamic_slice(act_backward, (0, (1 - ym) * 1024), (64, 1024))
    acts = jnp.concatenate(
        [same, send(other, "y", 1), send(other, "y", -1), send(same, "y", 2)], axis=0
    )
    flipped, halves = grad_pre_flipped(pre_backward, grad_backward)

    acts, halves, left, right, act_forward = together(acts, halves, left, right, act_forward)
    far = send(act_forward, "col", 2)
    b1, b2, b3 = send(acts, "col", -1), send(acts, "col", 2), send(acts, "col", 1)
    flipped_other = send(flipped, "row", 1)
    grads_own = lax.all_to_all(halves, "y", 0, 0)
    keep, give, mine, to_right, to_far, to_left = both_products(
        place, (act_forward, right, far, left), flipped, flipped_other, weight
    )

    grads_own, give, b1, b2, b3 = together(grads_own, give, b1, b2, b3)
    pre_forward = keep.astype(F32) + send(give, "row", 1).astype(F32)
    hidden_forward = gelu_value(pre_forward).astype(BF)
    grads_other, hidden_forward = together(send(grads_own, "row", 1), hidden_forward)
    parts = {}
    first = [(0, 4), (0, 5), (1, 4), (1, 3)]
    others = [(w, o) for w in range(2) for o in range(8) if (w, o) not in first]
    for wanted in (first, others):
        got = weight_parts(
            place, grads_own, grads_other, (acts, b1, b2, b3), wanted, wanted is first
        )
        parts.update(zip(wanted, got))
    given, kept = ([parts[w, o] for o in range(8)] for w in range(2))
    given = reduce_z(given, 1).astype(BF)
    kept = reduce_z(kept, -1)
    grad_inputs = (
        mine.astype(F32)
        + send(to_right, "col", 1).astype(F32)
        + send(to_left, "col", -1).astype(F32)
        + send(to_far, "col", 2).astype(F32)
    ).astype(BF)
    got = lax.ppermute(given, "y", [(0, 1), (1, 0), (2, 3), (3, 2)]).astype(F32)
    grad_weight = jnp.where(
        ym == 0, jnp.concatenate([kept, got], axis=1), jnp.concatenate([got, kept], axis=1)
    ).T
    return hidden_forward, grad_inputs, grad_weight


def solution(mesh):
    fine = Mesh(mesh.devices.reshape(2, 4, 8, 4), ("row", "col", "z", "y"))
    in_specs = (
        P(("z", "y", "col"), "row"),
        P("row", "col"),
        P(("z", "y", "col"), "row"),
        P(("z", "y", "row"), "col"),
        P(("z", "y", "row"), "col"),
    )
    out_specs = (
        P(("z", "y", "row"), "col"),
        P(("z", "y", "col"), "row"),
        P("row", ("col", "z", "y")),
    )
    return jax.shard_map(
        on_device, mesh=fine, in_specs=in_specs, out_specs=out_specs, check_vma=False
    )
```

time: 386 us -> 119 us (0.31)
  waiting for transfers between devices: 329 us -> 27.6 us
  starting transfers between devices: 0.24 us -> 46 us
  Pallas kernels: 0 us -> 31.9 us
  matrix products: 30.9 us -> 0 us
  between operations: 14.1 us -> 1.03 us
    reduce_scatter x3 -> x0, waiting for transfers between devices: 265 us -> none  [the longest x1 241 us: on_device(): lax.psum_scatter(lax.dot_general(grad_full, gathered_back, (((0,), (0,)),...]
    all_gather x3 -> x0, waiting for transfers between devices: 63.1 us -> none  [the longest x1 26 us: on_device(): lax.all_gather(act_forward, 'col', axis=0, tiled=True)]
    ppermute x0 -> x30, starting transfers between devices: none -> 42.4 us  [the longest x29 40.6 us: send(): return lax.ppermute(value, axis, [(i, (i + step) % n) for i in range(n)])]
    pallas_call x0 -> x4, Pallas kernels: none -> 31.9 us  [the longest x1 14.8 us: both_products(): pl.pallas_call(both_kernel, grid=(hidden // tile,), in_specs=[SMEM] + [pl...]
    dot_general x3 -> x0, matrix products: 30.9 us -> none  [the longest x1 11 us: on_device(): lax.dot_general(grad_full, gathered_back, (((0,), (0,)), ((), ())), prefe...]
    ppermute x0 -> x30, waiting for transfers between devices: none -> 27.6 us  [the longest x29 24.2 us: send(): return lax.ppermute(value, axis, [(i, (i + step) % n) for i in range(n)])]
  transfers between devices with their start and end apart: 6 -> 31, of which waited for: 5 -> 13; matrix products, arithmetic and copies ran while one was open for 10% -> 7% of each run, Pallas kernels for 0% -> 23%
where the time goes in v2:
time: 119 us; the launch traced here: 117 us
  starting transfers between devices  46 us (39%)
  Pallas kernels  31.9 us (27%)
  waiting for transfers between devices  27.6 us (23%)
  other arithmetic  8.99 us (8%)
  local copies, waits for them, and re-layouts  1.87 us (2%)
    ppermute x29, starting transfers between devices, send(): return lax.ppermute(value, axis, [(i, (i + step) % n) for i in range(n)])  40.6 us
    ppermute x29, waiting for transfers between devices, send(): return lax.ppermute(value, axis, [(i, (i + step) % n) for i in range(n)])  24.2 us
    pallas_call x1, Pallas kernels, both_products(): pl.pallas_call(both_kernel, grid=(hidden // tile,), in_specs=[SMEM] + [pl...  14.8 us
    pallas_call x2, Pallas kernels, weight_parts(): pl.pallas_call(functools.partial(first_kernel if first else rest_kernel,...  12.4 us
    pallas_call x1, Pallas kernels, grad_pre_flipped(): pl.pallas_call(grad_kernel, grid=(cols // tile,), in_specs=[pl.BlockSpec(...  4.68 us
    all_to_all x1, starting transfers between devices, on_device(): grads_own = lax.all_to_all(halves, 'y', 0, 0)  3.58 us
    ppermute x1, waiting for transfers between devices, on_device(): got = lax.ppermute(given, 'y', [(0, 1), (1, 0), (2, 3), (3, 2)]).astype(F32)  3.48 us
    convert_element_type x1, other arithmetic, on_device(): hidden_forward = gelu_value(pre_forward).astype(BF)  2.84 us
  transfers between devices with their start and end apart: 31, of which 13 were waited for; matrix products, arithmetic and copies ran while one was open for 7% of the time, Pallas kernels for 23%

profile of v2, /device:TPU:2, one launch (start us, length us, event | category | flops | bytes accessed | tf_op | source)
XLA Modules:
  0.0 117.3 jit_solution(12983889481438266940)
XLA Ops:
  1.6 3.1 %collective-permute-start.1 = (bf16[64,1024]{1,0:T(8,128)(2,1)S(1)}, bf16[64,1024]{1,0:T(8,128)(2,1)S(1)}, u32[]{:S(2)}, u32[]{:S(2)}) collective-permute-start(bf16[64,1024]{1,0:T(8,128)(2,1)S(1)} %get-tuple-element.75), channel_id=1, source_target_pairs={{0,3},{1,0},{2,1},{3,2},{4,7},{5,4},{6,5},{7,6},{8,11},{9,8},{10,9... | collective-permute-start | bytes 393224 | tf_op jit(solution)/shard_map/ppermute | solution.py:31
  6.8 2.2 %collective-permute-start.2 = (bf16[64,1024]{1,0:T(8,128)(2,1)S(1)}, bf16[64,1024]{1,0:T(8,128)(2,1)S(1)}, u32[]{:S(2)}, u32[]{:S(2)}) collective-permute-start(bf16[64,1024]{1,0:T(8,128)(2,1)S(1)} %get-tuple-element.76), channel_id=1, source_target_pairs={{0,2},{1,3},{2,0},{3,1},{4,6},{5,7},{6,4},{7,5},{8,10},{9,11},{10,... | collective-permute-start | bytes 393224 | tf_op jit(solution)/shard_map/ppermute | solution.py:31
  9.0 4.7 %shard_map.76 = (bf16[3584,128]{1,0:T(8,128)(2,1)}, bf16[4,2,896,128]{3,2,1,0:T(8,128)(2,1)}) custom-call(bf16[128,3584]{1,0:T(8,128)(2,1)} %pre_ref.1, bf16[128,3584]{1,0:T(8,128)(2,1)} %grad_ref.1), custom_call_target="tpu_custom_call" | custom-call | flops 13762560 | bytes 4587520 | tf_op jit(solution)/shard_map/pallas_call | solution.py:60
  16.1 3.6 %all-to-all-start = ((bf16[4,2,896,128]{3,2,1,0:T(8,128)(2,1)}), bf16[4,2,896,128]{3,2,1,0:T(8,128)(2,1)S(1)}, u32[]{:S(2)}, u32[]{:S(2)}) async-start(bf16[4,2,896,128]{3,2,1,0:T(8,128)(2,1)} %get-tuple-element.40), calls=%async_computation | async-start | bytes 3670016 | tf_op jit(solution)/shard_map/all_to_all | solution.py:241
  19.7 2.2 %collective-permute-start.5 = (bf16[64,2048]{1,0:T(8,128)(2,1)}, bf16[64,2048]{1,0:T(8,128)(2,1)}, u32[]{:S(2)}, u32[]{:S(2)}) collective-permute-start(bf16[64,2048]{1,0:T(8,128)(2,1)} %f0), channel_id=1, source_target_pairs={{0,64},{32,96},{64,0},{96,32},{1,65},{33,97},{65,1},{97,33},{2,66}... | collective-permute-start | bytes 786440 | tf_op jit(solution)/shard_map/ppermute | solution.py:31
  23.6 2.4 %collective-permute-start.8 = (bf16[256,1024]{1,0:T(8,128)(2,1)S(1)}, bf16[256,1024]{1,0:T(8,128)(2,1)S(1)}, u32[]{:S(2)}, u32[]{:S(2)}) collective-permute-start(bf16[256,1024]{1,0:T(8,128)(2,1)S(1)} %pad_maximum_fusion.b0), channel_id=1, source_target_pairs={{0,64},{32,96},{64,0},{96,32},{1,65},{33,97},{65,1},{97,33},{2,66}... | collective-permute-start | bytes 1572872 | tf_op jit(solution)/shard_map/ppermute | solution.py:31
  26.5 4.4 %collective-permute-done.5.f2 = bf16[64,2048]{1,0:T(8,128)(2,1)} collective-permute-done((bf16[64,2048]{1,0:T(8,128)(2,1)}, bf16[64,2048]{1,0:T(8,128)(2,1)}, u32[]{:S(2)}, u32[]{:S(2)}) %collective-permute-start.5) | collective-permute-done | bytes 262176 | tf_op jit(solution)/shard_map/ppermute | solution.py:31
  30.9 14.8 %shard_map.77 = (bf16[128,3584]{1,0:T(8,128)(2,1)}, bf16[128,3584]{1,0:T(8,128)(2,1)}, bf16[64,2048]{1,0:T(8,128)(2,1)}, bf16[64,2048]{1,0:T(8,128)(2,1)}, bf16[...) custom-call(s32[4]{0:T(128)} %pad_add_fusion.place_ref, bf16[64,2048]{1,0:T(8,128)(2,1)} %f0, bf16[64,2048]{1,0:T(8,128)(2,1)} %copy-done.15, ...), custom_call_target="tpu_custom_call" | custom-call | flops 7516192768 | bytes 14680064 | tf_op jit(solution)/shard_map/pallas_call | solution.py:192
  45.8 5.7 %collective-permute-done.7.b1 = bf16[256,1024]{1,0:T(8,128)(2,1)} collective-permute-done((bf16[256,1024]{1,0:T(8,128)(2,1)S(1)}, bf16[256,1024]{1,0:T(8,128)(2,1)}, u32[]{:S(2)}, u32[]{:S(2)}) %collective-permute-start.7) | collective-permute-done | bytes 524320 | tf_op jit(solution)/shard_map/ppermute | solution.py:31
  52.0 2.2 %collective-permute-done.11 = bf16[128,3584]{1,0:T(8,128)(2,1)S(1)} collective-permute-done((bf16[128,3584]{1,0:T(8,128)(2,1)}, bf16[128,3584]{1,0:T(8,128)(2,1)S(1)}, u32[]{:S(2)}, u32[]{:S(2)}) %collective-permute-start.11) | collective-permute-done | bytes 917536 | tf_op jit(solution)/shard_map/ppermute | solution.py:31
  54.2 2.8 %fusion.4 = bf16[128,3584]{1,0:T(8,128)(2,1)} fusion(bf16[128,3584]{1,0:T(8,128)(2,1)S(1)} %collective-permute-done.11, bf16[128,3584]{1,0:T(8,128)(2,1)} %get-tuple-element.48), kind=kLoop, calls=%fused_computation.5 | loop fusion | flops 5505024 | bytes 2752512 | tf_op jit(solution)/shard_map/convert_element_type | solution.py:248
  57.0 4.8 %shard_map.79 = (bf16[112,1024]{1,0:T(8,128)(2,1)}, bf16[112,1024]{1,0:T(8,128)(2,1)}, bf16[112,1024]{1,0:T(8,128)(2,1)}, bf16[112,1024]{1,0:T(8,128)(2,1)}) custom-call(s32[4]{0:T(128)} %pad_add_fusion.place_ref, bf16[4,2,896,128]{3,2,1,0:T(8,128)(2,1)} %copy-done, bf16[4,2,896,128]{3,2,1,0:T(8,128)(2,1)} %collective-permute-done.10.oth_ref, ...), custom_call_target="tpu_custom_call" | custom-call | flops 1048576 | bytes 1048576 | tf_op jit(solution)/shard_map/pallas_call | solution.py:137
  63.8 4.0 %collective-permute-start.15 = (bf16[112,1024]{1,0:T(8,128)(2,1)}, bf16[112,1024]{1,0:T(8,128)(2,1)S(1)}, u32[]{:S(2)}, u32[]{:S(2)}) collective-permute-start(bf16[112,1024]{1,0:T(8,128)(2,1)} %get-tuple-element.60), channel_id=1, source_target_pairs={{0,28},{4,0},{8,4},{12,8},{16,12},{20,16},{24,20},{28,24},{1,29},{... | collective-permute-start | bytes 688136 | tf_op jit(solution)/shard_map/ppermute | solution.py:31
  67.9 3.2 %collective-permute-start.26 = (bf16[112,1024]{1,0:T(8,128)(2,1)}, bf16[112,1024]{1,0:T(8,128)(2,1)S(1)}, u32[]{:S(2)}, u32[]{:S(2)}) collective-permute-start(bf16[112,1024]{1,0:T(8,128)(2,1)} %get-tuple-element.72), channel_id=1, source_target_pairs={{0,28},{4,0},{8,4},{12,8},{16,12},{20,16},{24,20},{28,24},{1,29},{... | collective-permute-start | bytes 688136 | tf_op jit(solution)/shard_map/ppermute | solution.py:31
  71.1 7.5 %shard_map.78 = (bf16[112,1024]{1,0:T(8,128)(2,1)}, bf16[112,1024]{1,0:T(8,128)(2,1)}, bf16[112,1024]{1,0:T(8,128)(2,1)}, bf16[112,1024]{1,0:T(8,128)(2,1)}, bf1...) custom-call(s32[4]{0:T(128)} %pad_add_fusion.place_ref, ...), custom_call_target="tpu_custom_call" | custom-call | flops 1048576 | bytes 1048576 | tf_op jit(solution)/shard_map/pallas_call | solution.py:137
  80.9 3.3 %collective-permute-start.16 = (bf16[112,1024]{1,0:T(8,128)(2,1)S(1)}, bf16[112,1024]{1,0:T(8,128)(2,1)S(1)}, u32[]{:S(2)}, u32[]{:S(2)}) collective-permute-start(bf16[112,1024]{1,0:T(8,128)(2,1)S(1)} %add.83), channel_id=1, source_target_pairs={{0,28},{4,0},{8,4},{12,8},{16,12},{20,16},{24,20},{28,24},{1,29},{... | collective-permute-start | bytes 688136 | tf_op jit(solution)/shard_map/ppermute | solution.py:31
  86.2 2.1 %collective-permute-start.14 = (bf16[64,2048]{1,0:T(8,128)(2,1)}, bf16[64,2048]{1,0:T(8,128)(2,1)S(1)}, u32[]{:S(2)}, u32[]{:S(2)}) collective-permute-start(bf16[64,2048]{1,0:T(8,128)(2,1)} %get-tuple-element.54), channel_id=1, source_target_pairs={{0,64},{32,96},{64,0},{96,32},{1,65},{33,97},{65,1},{97,33},{2,66}... | collective-permute-start | bytes 786440 | tf_op jit(solution)/shard_map/ppermute | solution.py:31
  89.6 2.2 %collective-permute-start.24 = (bf16[112,1024]{1,0:T(8,128)(2,1)S(1)}, bf16[112,1024]{1,0:T(8,128)(2,1)S(1)}, u32[]{:S(2)}, u32[]{:S(2)}) collective-permute-start(bf16[112,1024]{1,0:T(8,128)(2,1)S(1)} %add.91), channel_id=1, source_target_pairs={{0,4},{4,8},{8,12},{12,16},{16,20},{20,24},{24,28},{28,0},{1,5},{5... | collective-permute-start | bytes 688136 | tf_op jit(solution)/shard_map/ppermute | solution.py:31
  92.0 3.5 %collective-permute-done.27 = bf16[112,1024]{1,0:T(8,128)(2,1)S(1)} collective-permute-done((bf16[112,1024]{1,0:T(8,128)(2,1)S(1)}, bf16[112,1024]{1,0:T(8,128)(2,1)S(1)}, u32[]{:S(2)}, u32[]{:S(2)}) %collective-permute-start.27) | collective-permute-done | bytes 229408 | tf_op jit(solution)/shard_map/ppermute | solution.py:31
  95.5 2.3 %collective-permute-done.24 = bf16[112,1024]{1,0:T(8,128)(2,1)S(1)} collective-permute-done((bf16[112,1024]{1,0:T(8,128)(2,1)S(1)}, bf16[112,1024]{1,0:T(8,128)(2,1)S(1)}, u32[]{:S(2)}, u32[]{:S(2)}) %collective-permute-start.24) | collective-permute-done | bytes 229408 | tf_op jit(solution)/shard_map/ppermute | solution.py:31
  99.4 2.6 %collective-permute-start.28 = (bf16[112,1024]{1,0:T(8,128)(2,1)S(1)}, bf16[112,1024]{1,0:T(8,128)(2,1)S(1)}, u32[]{:S(2)}, u32[]{:S(2)}) collective-permute-start(bf16[112,1024]{1,0:T(8,128)(2,1)S(1)} %add.95), channel_id=1, source_target_pairs={{0,28},{4,0},{8,4},{12,8},{16,12},{20,16},{24,20},{28,24},{1,29},{... | collective-permute-start | bytes 688136 | tf_op jit(solution)/shard_map/ppermute | solution.py:31
  102.8 2.4 %collective-permute-done.20 = bf16[112,1024]{1,0:T(8,128)(2,1)S(1)} collective-permute-done((bf16[112,1024]{1,0:T(8,128)(2,1)S(1)}, bf16[112,1024]{1,0:T(8,128)(2,1)S(1)}, u32[]{:S(2)}, u32[]{:S(2)}) %collective-permute-start.20) | collective-permute-done | bytes 229408 | tf_op jit(solution)/shard_map/ppermute | solution.py:31
  105.5 3.2 %collective-permute-start.18 = (bf16[112,1024]{1,0:T(8,128)(2,1)S(1)}, bf16[112,1024]{1,0:T(8,128)(2,1)S(1)}, u32[]{:S(2)}, u32[]{:S(2)}) collective-permute-start(bf16[112,1024]{1,0:T(8,128)(2,1)S(1)} %add.85), channel_id=1, source_target_pairs={{0,28},{4,0},{8,4},{12,8},{16,12},{20,16},{24,20},{28,24},{1,29},{... | collective-permute-start | bytes 688136 | tf_op jit(solution)/shard_map/ppermute | solution.py:31
  112.8 3.5 %collective-permute-done.29 = bf16[112,1024]{1,0:T(8,128)(2,1)S(1)} collective-permute-done((bf16[112,1024]{1,0:T(8,128)(2,1)S(1)}, bf16[112,1024]{1,0:T(8,128)(2,1)S(1)}, u32[]{:S(2)}, u32[]{:S(2)}) %collective-permute-start.29) | collective-permute-done | bytes 229408 | tf_op jit(solution)/shard_map/ppermute | solution.py:267
  (93 shorter events, 23.6 us)
Async XLA Ops:
  1.6 12.0 %collective-permute-start.1 = (bf16[64,1024]{1,0:T(8,128)(2,1)S(1)}, bf16[64,1024]{1,0:T(8,128)(2,1)S(1)}, u32[]{:S(2)}, u32[]{:S(2)}) collective-permute-start(bf16[64,1024]{1,0:T(8,128)(2,1)S(1)} %get-tuple-element.75), channel_id=1, source_target_pairs={{0,3},{1,0},{2,1},{3,2},{4,7},{5,4},{6,5},{7,6},{8,11},{9,8},{10,9... | collective-permute-start | bytes 393224 | tf_op jit(solution)/shard_map/ppermute | solution.py:31
  4.7 10.5 %collective-permute-start.3 = (bf16[64,2048]{1,0:T(8,128)(2,1)}, bf16[64,2048]{1,0:T(8,128)(2,1)S(1)}, u32[]{:S(2)}, u32[]{:S(2)}) collective-permute-start(bf16[64,2048]{1,0:T(8,128)(2,1)} %f0), channel_id=1, source_target_pairs={{0,32},{32,64},{64,96},{96,0},{1,33},{33,65},{65,97},{97,1},{2,34}... | collective-permute-start | bytes 786440 | tf_op jit(solution)/shard_map/ppermute | solution.py:31
  6.2 9.0 %collective-permute-start.4 = (bf16[64,2048]{1,0:T(8,128)(2,1)}, bf16[64,2048]{1,0:T(8,128)(2,1)S(1)}, u32[]{:S(2)}, u32[]{:S(2)}) collective-permute-start(bf16[64,2048]{1,0:T(8,128)(2,1)} %f0), channel_id=1, source_target_pairs={{0,96},{32,0},{64,32},{96,64},{1,97},{33,1},{65,33},{97,65},{2,98}... | collective-permute-start | bytes 786440 | tf_op jit(solution)/shard_map/ppermute | solution.py:31
  6.8 8.4 %collective-permute-start = (bf16[64,1024]{1,0:T(8,128)(2,1)S(1)}, bf16[64,1024]{1,0:T(8,128)(2,1)S(1)}, u32[]{:S(2)}, u32[]{:S(2)}) collective-permute-start(bf16[64,1024]{1,0:T(8,128)(2,1)S(1)} %get-tuple-element.75), channel_id=1, source_target_pairs={{0,1},{1,2},{2,3},{3,0},{4,5},{5,6},{6,7},{7,4},{8,9},{9,10},{10,1... | collective-permute-start | bytes 393224 | tf_op jit(solution)/shard_map/ppermute | solution.py:31
  6.8 8.4 %collective-permute-start.2 = (bf16[64,1024]{1,0:T(8,128)(2,1)S(1)}, bf16[64,1024]{1,0:T(8,128)(2,1)S(1)}, u32[]{:S(2)}, u32[]{:S(2)}) collective-permute-start(bf16[64,1024]{1,0:T(8,128)(2,1)S(1)} %get-tuple-element.76), channel_id=1, source_target_pairs={{0,2},{1,3},{2,0},{3,1},{4,6},{5,7},{6,4},{7,5},{8,10},{9,11},{10,... | collective-permute-start | bytes 393224 | tf_op jit(solution)/shard_map/ppermute | solution.py:31
  13.7 17.3 %collective-permute-start.6 = (bf16[3584,128]{1,0:T(8,128)(2,1)}, bf16[3584,128]{1,0:T(8,128)(2,1)}, u32[]{:S(2)}, u32[]{:S(2)}) collective-permute-start(bf16[3584,128]{1,0:T(8,128)(2,1)} %get-tuple-element.44.own_ref), channel_id=1, source_target_pairs={{0,128},{128,0},{1,129},{129,1},{2,130},{130,2},{3,131},{131,3},{4... | collective-permute-start | bytes 2752520 | tf_op jit(solution)/shard_map/ppermute | solution.py:31
  16.1 35.4 %all-to-all-start = ((bf16[4,2,896,128]{3,2,1,0:T(8,128)(2,1)}), bf16[4,2,896,128]{3,2,1,0:T(8,128)(2,1)S(1)}, u32[]{:S(2)}, u32[]{:S(2)}) async-start(bf16[4,2,896,128]{3,2,1,0:T(8,128)(2,1)} %get-tuple-element.40), calls=%async_computation | async-start | bytes 3670016 | tf_op jit(solution)/shard_map/all_to_all | solution.py:241
  19.7 11.2 %collective-permute-start.5 = (bf16[64,2048]{1,0:T(8,128)(2,1)}, bf16[64,2048]{1,0:T(8,128)(2,1)}, u32[]{:S(2)}, u32[]{:S(2)}) collective-permute-start(bf16[64,2048]{1,0:T(8,128)(2,1)} %f0), channel_id=1, source_target_pairs={{0,64},{32,96},{64,0},{96,32},{1,65},{33,97},{65,1},{97,33},{2,66}... | collective-permute-start | bytes 786440 | tf_op jit(solution)/shard_map/ppermute | solution.py:31
  22.5 23.3 %collective-permute-start.9 = (bf16[256,1024]{1,0:T(8,128)(2,1)S(1)}, bf16[256,1024]{1,0:T(8,128)(2,1)S(1)}, u32[]{:S(2)}, u32[]{:S(2)}) collective-permute-start(bf16[256,1024]{1,0:T(8,128)(2,1)S(1)} %pad_maximum_fusion.b0), channel_id=1, source_target_pairs={{0,32},{32,64},{64,96},{96,0},{1,33},{33,65},{65,97},{97,1},{2,34}... | collective-permute-start | bytes 1572872 | tf_op jit(solution)/shard_map/ppermute | solution.py:31
  23.6 22.2 %collective-permute-start.8 = (bf16[256,1024]{1,0:T(8,128)(2,1)S(1)}, bf16[256,1024]{1,0:T(8,128)(2,1)S(1)}, u32[]{:S(2)}, u32[]{:S(2)}) collective-permute-start(bf16[256,1024]{1,0:T(8,128)(2,1)S(1)} %pad_maximum_fusion.b0), channel_id=1, source_target_pairs={{0,64},{32,96},{64,0},{96,32},{1,65},{33,97},{65,1},{97,33},{2,66}... | collective-permute-start | bytes 1572872 | tf_op jit(solution)/shard_map/ppermute | solution.py:31
  26.0 25.5 %collective-permute-start.7 = (bf16[256,1024]{1,0:T(8,128)(2,1)S(1)}, bf16[256,1024]{1,0:T(8,128)(2,1)}, u32[]{:S(2)}, u32[]{:S(2)}) collective-permute-start(bf16[256,1024]{1,0:T(8,128)(2,1)S(1)} %pad_maximum_fusion.b0), channel_id=1, source_target_pairs={{0,96},{32,0},{64,32},{96,64},{1,97},{33,1},{65,33},{97,65},{2,98}... | collective-permute-start | bytes 1572872 | tf_op jit(solution)/shard_map/ppermute | solution.py:31
  61.8 16.8 %collective-permute-start.22 = (bf16[112,1024]{1,0:T(8,128)(2,1)}, bf16[112,1024]{1,0:T(8,128)(2,1)S(1)}, u32[]{:S(2)}, u32[]{:S(2)}) collective-permute-start(bf16[112,1024]{1,0:T(8,128)(2,1)} %get-tuple-element.68), channel_id=1, source_target_pairs={{0,4},{4,8},{8,12},{12,16},{16,20},{20,24},{24,28},{28,0},{1,5},{5... | collective-permute-start | bytes 688136 | tf_op jit(solution)/shard_map/ppermute | solution.py:31
  63.8 16.0 %collective-permute-start.15 = (bf16[112,1024]{1,0:T(8,128)(2,1)}, bf16[112,1024]{1,0:T(8,128)(2,1)S(1)}, u32[]{:S(2)}, u32[]{:S(2)}) collective-permute-start(bf16[112,1024]{1,0:T(8,128)(2,1)} %get-tuple-element.60), channel_id=1, source_target_pairs={{0,28},{4,0},{8,4},{12,8},{16,12},{20,16},{24,20},{28,24},{1,29},{... | collective-permute-start | bytes 688136 | tf_op jit(solution)/shard_map/ppermute | solution.py:31
  67.9 17.8 %collective-permute-start.19 = (bf16[112,1024]{1,0:T(8,128)(2,1)}, bf16[112,1024]{1,0:T(8,128)(2,1)S(1)}, u32[]{:S(2)}, u32[]{:S(2)}) collective-permute-start(bf16[112,1024]{1,0:T(8,128)(2,1)} %get-tuple-element.64), channel_id=1, source_target_pairs={{0,4},{4,8},{8,12},{12,16},{16,20},{20,24},{24,28},{28,0},{1,5},{5... | collective-permute-start | bytes 688136 | tf_op jit(solution)/shard_map/ppermute | solution.py:31
  67.9 18.3 %collective-permute-start.26 = (bf16[112,1024]{1,0:T(8,128)(2,1)}, bf16[112,1024]{1,0:T(8,128)(2,1)S(1)}, u32[]{:S(2)}, u32[]{:S(2)}) collective-permute-start(bf16[112,1024]{1,0:T(8,128)(2,1)} %get-tuple-element.72), channel_id=1, source_target_pairs={{0,28},{4,0},{8,4},{12,8},{16,12},{20,16},{24,20},{28,24},{1,29},{... | collective-permute-start | bytes 688136 | tf_op jit(solution)/shard_map/ppermute | solution.py:31
  79.8 9.6 %collective-permute-start.23 = (bf16[112,1024]{1,0:T(8,128)(2,1)S(1)}, bf16[112,1024]{1,0:T(8,128)(2,1)S(1)}, u32[]{:S(2)}, u32[]{:S(2)}) collective-permute-start(bf16[112,1024]{1,0:T(8,128)(2,1)S(1)} %add.90), channel_id=1, source_target_pairs={{0,4},{4,8},{8,12},{12,16},{16,20},{20,24},{24,28},{28,0},{1,5},{5... | collective-permute-start | bytes 688136 | tf_op jit(solution)/shard_map/ppermute | solution.py:31
  80.9 8.7 %collective-permute-start.16 = (bf16[112,1024]{1,0:T(8,128)(2,1)S(1)}, bf16[112,1024]{1,0:T(8,128)(2,1)S(1)}, u32[]{:S(2)}, u32[]{:S(2)}) collective-permute-start(bf16[112,1024]{1,0:T(8,128)(2,1)S(1)} %add.83), channel_id=1, source_target_pairs={{0,28},{4,0},{8,4},{12,8},{16,12},{20,16},{24,20},{28,24},{1,29},{... | collective-permute-start | bytes 688136 | tf_op jit(solution)/shard_map/ppermute | solution.py:31
  84.2 15.2 %collective-permute-start.12 = (bf16[64,2048]{1,0:T(8,128)(2,1)}, bf16[64,2048]{1,0:T(8,128)(2,1)S(1)}, u32[]{:S(2)}, u32[]{:S(2)}) collective-permute-start(bf16[64,2048]{1,0:T(8,128)(2,1)} %get-tuple-element.52), channel_id=1, source_target_pairs={{0,32},{32,64},{64,96},{96,0},{1,33},{33,65},{65,97},{97,1},{2,34}... | collective-permute-start | bytes 786440 | tf_op jit(solution)/shard_map/ppermute | solution.py:31
  85.7 16.2 %collective-permute-start.13 = (bf16[64,2048]{1,0:T(8,128)(2,1)}, bf16[64,2048]{1,0:T(8,128)(2,1)S(1)}, u32[]{:S(2)}, u32[]{:S(2)}) collective-permute-start(bf16[64,2048]{1,0:T(8,128)(2,1)} %get-tuple-element.53), channel_id=1, source_target_pairs={{0,96},{32,0},{64,32},{96,64},{1,97},{33,1},{65,33},{97,65},{2,98}... | collective-permute-start | bytes 786440 | tf_op jit(solution)/shard_map/ppermute | solution.py:31
  86.2 15.7 %collective-permute-start.14 = (bf16[64,2048]{1,0:T(8,128)(2,1)}, bf16[64,2048]{1,0:T(8,128)(2,1)S(1)}, u32[]{:S(2)}, u32[]{:S(2)}) collective-permute-start(bf16[64,2048]{1,0:T(8,128)(2,1)} %get-tuple-element.54), channel_id=1, source_target_pairs={{0,64},{32,96},{64,0},{96,32},{1,65},{33,97},{65,1},{97,33},{2,66}... | collective-permute-start | bytes 786440 | tf_op jit(solution)/shard_map/ppermute | solution.py:31
  89.6 8.2 %collective-permute-start.24 = (bf16[112,1024]{1,0:T(8,128)(2,1)S(1)}, bf16[112,1024]{1,0:T(8,128)(2,1)S(1)}, u32[]{:S(2)}, u32[]{:S(2)}) collective-permute-start(bf16[112,1024]{1,0:T(8,128)(2,1)S(1)} %add.91), channel_id=1, source_target_pairs={{0,4},{4,8},{8,12},{12,16},{16,20},{20,24},{24,28},{28,0},{1,5},{5... | collective-permute-start | bytes 688136 | tf_op jit(solution)/shard_map/ppermute | solution.py:31
  95.5 9.7 %collective-permute-start.20 = (bf16[112,1024]{1,0:T(8,128)(2,1)S(1)}, bf16[112,1024]{1,0:T(8,128)(2,1)S(1)}, u32[]{:S(2)}, u32[]{:S(2)}) collective-permute-start(bf16[112,1024]{1,0:T(8,128)(2,1)S(1)} %add.87), channel_id=1, source_target_pairs={{0,4},{4,8},{8,12},{12,16},{16,20},{20,24},{24,28},{28,0},{1,5},{5... | collective-permute-start | bytes 688136 | tf_op jit(solution)/shard_map/ppermute | solution.py:31
  99.4 9.8 %collective-permute-start.28 = (bf16[112,1024]{1,0:T(8,128)(2,1)S(1)}, bf16[112,1024]{1,0:T(8,128)(2,1)S(1)}, u32[]{:S(2)}, u32[]{:S(2)}) collective-permute-start(bf16[112,1024]{1,0:T(8,128)(2,1)S(1)} %add.95), channel_id=1, source_target_pairs={{0,28},{4,0},{8,4},{12,8},{16,12},{20,16},{24,20},{28,24},{1,29},{... | collective-permute-start | bytes 688136 | tf_op jit(solution)/shard_map/ppermute | solution.py:31
  101.9 8.1 %collective-permute-start.25 = (bf16[112,1024]{1,0:T(8,128)(2,1)S(1)}, bf16[112,1024]{1,0:T(8,128)(2,1)S(1)}, u32[]{:S(2)}, u32[]{:S(2)}) collective-permute-start(bf16[112,1024]{1,0:T(8,128)(2,1)S(1)} %add.92), channel_id=1, source_target_pairs={{0,4},{4,8},{8,12},{12,16},{16,20},{20,24},{24,28},{28,0},{1,5},{5... | collective-permute-start | bytes 688136 | tf_op jit(solution)/shard_map/ppermute | solution.py:31
  (23 other events, 221.4 us)

commit v3 on v2

--- a/solution.py
+++ b/solution.py
@@ -77,7 +77,7 @@
 
 
 def copy_acts(place_ref, blocks, acts, sems):
-    x, r, y = place_ref[0], place_ref[1], place_ref[2]
+    x, r, y = (lax.axis_index(n) for n in ("col", "row", "y"))
     copies = []
     for d, block in enumerate(blocks):
         at = lax.rem(x + d, 4)
@@ -90,7 +90,7 @@
 
 def first_kernel(wanted, place_ref, own_ref, oth_ref, b0, b1, b2, b3, *rest):
     outs, (acts, lhs, sems) = rest[:-3], rest[-3:]
-    z = place_ref[3]
+    z = lax.axis_index("z")
     copies = copy_acts(place_ref, (b0, b1, b2, b3), acts, sems)
     for i, (which, offset) in enumerate(wanted):
         rows = pl.ds(pl.multiple_of(lax.rem(z + offset, 8) * 112, 16), 112)
@@ -110,7 +110,7 @@
 
 def rest_kernel(wanted, place_ref, own_ref, oth_ref, b0, b1, b2, b3, *rest):
     outs, (acts, lhs, sems) = rest[:-3], rest[-3:]
-    z = place_ref[3]
+    z = lax.axis_index("z")
     copies = copy_acts(place_ref, (b0, b1, b2, b3), acts, sems)
     for which in range(2):
         for h, ref in enumerate((own_ref, oth_ref)):
@@ -131,13 +131,13 @@
             outs[i + k][...] = part[k * 112 : k * 112 + 112].astype(BF)
 
 
-def weight_parts(place, own, oth, blocks, wanted, first):
+def weight_parts(place, own, oth, blocks, wanted, first, late=()):
     anywhere = pl.BlockSpec(memory_space=pl.ANY)
     n = len(wanted)
     return pl.pallas_call(
         functools.partial(first_kernel if first else rest_kernel, wanted),
         grid=(1,),
-        in_specs=[SMEM] + [anywhere] * 6,
+        in_specs=[SMEM] + [anywhere] * (6 + len(late)),
         out_specs=[pl.BlockSpec((112, 1024), lambda i: (0, 0))] * n,
         scratch_shapes=[
             pltpu.VMEM((1024, 1024), BF),
@@ -147,12 +147,13 @@
         out_shape=[jax.ShapeDtypeStruct((112, 1024), BF)] * n,
         compiler_params=params(60),
         cost_estimate=pl.CostEstimate(flops=2**20, bytes_accessed=2**20, transcendentals=0),
-    )(place, own, oth, *blocks)
-
-
-def both_kernel(place_ref, f0, f1, f2, f3, own_ref, oth_ref, w_ref, keep_ref, give_ref, o0, o1, o2, o3, rows_ref, acc):
+    )(place, own, oth, *blocks, *late)
+
+
+def both_kernel(place_ref, f0, f1, f2, f3, own_ref, oth_ref, w_ref, keep_ref, out_ref, *rest):
+    gives, rows_ref, acc = rest[:-2], rest[-2], rest[-1]
     step, last = pl.program_id(0), pl.num_programs(0) - 1
-    x, r = place_ref[0], place_ref[1]
+    x, r = lax.axis_index("col"), lax.axis_index("row")
 
     @pl.when(step == 0)
     def _():
@@ -164,7 +165,8 @@
     w = w_ref[...]
     part = jnp.dot(rows_ref[...], w, preferred_element_type=F32).astype(BF)
     keep_ref[...] = part[:128]
-    give_ref[...] = part[128:]
+    for k, give in enumerate(gives):
+        give[...] = part[128 + 64 * k : 192 + 64 * k]
     both = jnp.concatenate([own_ref[...], oth_ref[...]], axis=1)
     more = jnp.dot(w, both, preferred_element_type=F32)
 
@@ -179,11 +181,10 @@
     @pl.when(step == last)
     def _():
         flat = acc[...].T.astype(BF)
-        rows_ref[...] = flat
-        for d, out in enumerate((o0, o1, o2, o3)):
-            at = lax.rem(x + d, 4)
-            row = ((at // 2) ^ r) * 128 + lax.rem(at, 2) * 64
-            out[...] = rows_ref[pl.ds(pl.multiple_of(row, 64), 64), :]
+        for half in range(2):
+            for k in range(2):
+                at = (half ^ r) * 2 + k
+                out_ref[at] = flat[half * 128 + k * 64 : half * 128 + k * 64 + 64]
 
 
 def both_products(place, fwd, own, oth, weight):
@@ -196,28 +197,65 @@
         + [pl.BlockSpec((64, feats), lambda i: (0, 0))] * 4
         + [pl.BlockSpec((tile, 128), lambda i: (i, 0))] * 2
         + [pl.BlockSpec((feats, tile), lambda i: (0, i))],
-        out_specs=[pl.BlockSpec((128, tile), lambda i: (0, i))] * 2
-        + [pl.BlockSpec((64, feats), lambda i: (0, 0))] * 4,
-        out_shape=[jax.ShapeDtypeStruct((128, hidden), BF)] * 2
-        + [jax.ShapeDtypeStruct((64, feats), BF)] * 4,
+        out_specs=[
+            pl.BlockSpec((128, tile), lambda i: (0, i)),
+            pl.BlockSpec((4, 64, feats), lambda i: (0, 0, 0)),
+        ]
+        + [pl.BlockSpec((64, tile), lambda i: (0, i))] * 2,
+        out_shape=[
+            jax.ShapeDtypeStruct((128, hidden), BF),
+            jax.ShapeDtypeStruct((4, 64, feats), BF),
+        ]
+        + [jax.ShapeDtypeStruct((64, hidden), BF)] * 2,
         scratch_shapes=[pltpu.VMEM((256, feats), BF), pltpu.VMEM((feats, 256), F32)],
         compiler_params=params(60),
         cost_estimate=pl.CostEstimate(
-            flops=4 * 256 * 2048 * hidden, bytes_accessed=2 * 2048 * hidden, transcendentals=0
+            flops=12 * 256 * 2048 * hidden, bytes_accessed=2 * 2048 * hidden, transcendentals=0
         ),
     )(place, *fwd, own, oth, weight)
 
 
-def reduce_z(piece, step):
+def gelu_kernel(keep_ref, *refs):
+    out_ref, rows = refs[-1], refs[0].shape[0]
+    for k, got in enumerate(refs[:-1]):
+        at = pl.ds(k * rows, rows)
+        v = keep_ref[at, :].astype(F32) + got[...].astype(F32)
+        out_ref[at, :] = gelu_value(v).astype(BF)
+
+
+def gelu_rows(keep, got):
+    rows, cols = keep.shape
+    tile = 896
+    whole = pl.BlockSpec((rows, tile), lambda i: (0, i))
+    return pl.pallas_call(
+        gelu_kernel,
+        grid=(cols // tile,),
+        in_specs=[whole] + [pl.BlockSpec((rows // len(got), tile), lambda i: (0, i))] * len(got),
+        out_specs=whole,
+        out_shape=jax.ShapeDtypeStruct((rows, cols), BF),
+        compiler_params=params(60),
+        cost_estimate=pl.CostEstimate(flops=2**18, bytes_accessed=2**18, transcendentals=0),
+    )(keep, *got)
+
+
+def reduce_z(piece, step, swap, late=None):
+    partner = [(k, k ^ 1) for k in range(4)]
     far, near = piece[4], piece[-3 * step % 8]
-    for hop in (3, 2, 1, 0):
+    for hop in (3, 2, 1):
         far = send(far, "z", step)
-        if hop >= 1:
-            near = send(near, "z", -step)
-            far = far + piece[hop * step % 8]
-            if hop > 1:
-                near = near + piece[-(hop - 1) * step % 8]
-    return piece[0].astype(F32) + far.astype(F32) + near.astype(F32)
+        if hop == 3 and late is not None:
+            far, late = together(far, late)
+        near = send(near, "z", -step)
+        far = far + piece[hop * step % 8]
+        if hop > 1:
+            near = near + piece[-(hop - 1) * step % 8]
+    if swap:
+        near = lax.ppermute(near + piece[0], "y", partner)
+        steps = [(k * 4 + a, (k + step) % 8 * 4 + b) for k in range(8) for a, b in partner]
+        far = lax.ppermute(far, ("z", "y"), steps)
+        return near.astype(F32) + far.astype(F32), late
+    far = send(far, "z", step)
+    return piece[0].astype(F32) + far.astype(F32) + near.astype(F32), late
 
 
 def on_device(act_forward, weight, act_backward, pre_backward, grad_backward):
@@ -234,37 +272,35 @@
     )
     flipped, halves = grad_pre_flipped(pre_backward, grad_backward)
 
-    acts, halves, left, right, act_forward = together(acts, halves, left, right, act_forward)
+    acts, halves, flipped, left, right, act_forward = together(
+        acts, halves, flipped, left, right, act_forward
+    )
     far = send(act_forward, "col", 2)
     b1, b2, b3 = send(acts, "col", -1), send(acts, "col", 2), send(acts, "col", 1)
     flipped_other = send(flipped, "row", 1)
     grads_own = lax.all_to_all(halves, "y", 0, 0)
-    keep, give, mine, to_right, to_far, to_left = both_products(
+    keep, packed, *gives = both_products(
         place, (act_forward, right, far, left), flipped, flipped_other, weight
     )
 
-    grads_own, give, b1, b2, b3 = together(grads_own, give, b1, b2, b3)
-    pre_forward = keep.astype(F32) + send(give, "row", 1).astype(F32)
-    hidden_forward = gelu_value(pre_forward).astype(BF)
-    grads_other, hidden_forward = together(send(grads_own, "row", 1), hidden_forward)
+    hidden_forward = gelu_rows(keep, [send(give, "row", 1) for give in gives])
+    grads_own, hidden_forward, packed, b1, b2, b3 = together(
+        grads_own, hidden_forward, packed, b1, b2, b3
+    )
+    grads_other = send(grads_own, "row", 1)
+    packed = lax.all_to_all(packed, "col", 0, 0)
     parts = {}
-    first = [(0, 4), (0, 5), (1, 4), (1, 3)]
+    first = [(0, 4), (0, 3), (1, 4), (1, 5)]
     others = [(w, o) for w in range(2) for o in range(8) if (w, o) not in first]
-    for wanted in (first, others):
+    for wanted, late in ((first, ()), (others, ())):
         got = weight_parts(
-            place, grads_own, grads_other, (acts, b1, b2, b3), wanted, wanted is first
+            place, grads_own, grads_other, (acts, b1, b2, b3), wanted, wanted is first, late
         )
         parts.update(zip(wanted, got))
     given, kept = ([parts[w, o] for o in range(8)] for w in range(2))
-    given = reduce_z(given, 1).astype(BF)
-    kept = reduce_z(kept, -1)
-    grad_inputs = (
-        mine.astype(F32)
-        + send(to_right, "col", 1).astype(F32)
-        + send(to_left, "col", -1).astype(F32)
-        + send(to_far, "col", 2).astype(F32)
-    ).astype(BF)
-    got = lax.ppermute(given, "y", [(0, 1), (1, 0), (2, 3), (3, 2)]).astype(F32)
+    got, _ = reduce_z(given, -1, True)
+    kept, packed = reduce_z(kept, 1, False, packed)
+    grad_inputs = packed.astype(F32).sum(axis=0).astype(BF)
     grad_weight = jnp.where(
         ym == 0, jnp.concatenate([kept, got], axis=1), jnp.concatenate([got, kept], axis=1)
     ).T

time: 119 us -> 110 us (0.924)
  waiting for transfers between devices: 27.6 us -> 13.4 us
  Pallas kernels: 31.9 us -> 35.8 us
  starting transfers between devices: 46 us -> 49.7 us
  other arithmetic: 8.99 us -> 7.8 us
    ppermute x29 -> x26, waiting for transfers between devices: 24.2 us -> 9.86 us  [send(): return lax.ppermute(value, axis, [(i, (i + step) % n) for i in range(n)])]
    all_to_all x0 -> x1, starting transfers between devices: none -> 5.61 us  [on_device(): packed = lax.all_to_all(packed, 'col', 0, 0)]
    ppermute x29 -> x26, starting transfers between devices: 40.6 us -> 35.6 us  [send(): return lax.ppermute(value, axis, [(i, (i + step) % n) for i in range(n)])]
    pallas_call x0 -> x1, Pallas kernels: none -> 3.91 us  [gelu_rows(): pl.pallas_call(gelu_kernel, grid=(cols // tile,), in_specs=[whole] + [pl....]
    convert_element_type x4 -> x0, other arithmetic: 3.81 us -> none  [the longest x1 2.84 us: on_device(): hidden_forward = gelu_value(pre_forward).astype(BF)]
    ppermute x1 -> x2, starting transfers between devices: 1.77 us -> 4.95 us  [the longest x1 4.33 us: reduce_z(): far = lax.ppermute(far, ('z', 'y'), steps)]
    ppermute x1 -> x2, waiting for transfers between devices: 3.48 us -> 3.01 us  [the longest x1 2.49 us: reduce_z(): near = lax.ppermute(near + piece[0], 'y', partner)]
  transfers between devices with their start and end apart: 31 -> 30, of which waited for: 13 -> 15; matrix products, arithmetic and copies ran while one was open for 7% -> 7% of each run, Pallas kernels for 23% -> 33%
where the time goes in v3:
time: 110 us; the launch traced here: 109 us
  starting transfers between devices  49.7 us (45%)
  Pallas kernels  35.8 us (33%)
  waiting for transfers between devices  13.4 us (12%)
  other arithmetic  7.8 us (7%)
  local copies, waits for them, and re-layouts  1.12 us (1%)
    ppermute x26, starting transfers between devices, send(): return lax.ppermute(value, axis, [(i, (i + step) % n) for i in range(n)])  35.6 us
    pallas_call x1, Pallas kernels, both_products(): pl.pallas_call(both_kernel, grid=(hidden // tile,), in_specs=[SMEM] + [pl...  14.8 us
    pallas_call x2, Pallas kernels, weight_parts(): pl.pallas_call(functools.partial(first_kernel if first else rest_kernel,...  12.4 us
    ppermute x26, waiting for transfers between devices, send(): return lax.ppermute(value, axis, [(i, (i + step) % n) for i in range(n)])  9.86 us
    all_to_all x1, starting transfers between devices, on_device(): packed = lax.all_to_all(packed, 'col', 0, 0)  5.61 us
    pallas_call x1, Pallas kernels, grad_pre_flipped(): pl.pallas_call(grad_kernel, grid=(cols // tile,), in_specs=[pl.BlockSpec(...  4.71 us
    ppermute x1, starting transfers between devices, reduce_z(): far = lax.ppermute(far, ('z', 'y'), steps)  4.33 us
    pallas_call x1, Pallas kernels, gelu_rows(): pl.pallas_call(gelu_kernel, grid=(cols // tile,), in_specs=[whole] + [pl....  3.91 us
  transfers between devices with their start and end apart: 30, of which 15 were waited for; matrix products, arithmetic and copies ran while one was open for 7% of the time, Pallas kernels for 33%

profile of v3, /device:TPU:2, one launch (start us, length us, event | category | flops | bytes accessed | tf_op | source)
XLA Modules:
  0.0 108.9 jit_solution(4617129611818631789)
XLA Ops:
  0.6 1.6 %collective-permute-start.3 = (bf16[64,2048]{1,0:T(8,128)(2,1)}, bf16[64,2048]{1,0:T(8,128)(2,1)S(1)}, u32[]{:S(2)}, u32[]{:S(2)}) collective-permute-start(bf16[64,2048]{1,0:T(8,128)(2,1)} %f0), channel_id=1, source_target_pairs={{0,32},{32,64},{64,96},{96,0},{1,33},{33,65},{65,97},{97,1},{2,34}... | collective-permute-start | bytes 786440 | tf_op jit(solution)/shard_map/ppermute | solution.py:31
  4.1 2.9 %collective-permute-start.2 = (bf16[64,1024]{1,0:T(8,128)(2,1)S(1)}, bf16[64,1024]{1,0:T(8,128)(2,1)S(1)}, u32[]{:S(2)}, u32[]{:S(2)}) collective-permute-start(bf16[64,1024]{1,0:T(8,128)(2,1)S(1)} %get-tuple-element.76), channel_id=1, source_target_pairs={{0,2},{1,3},{2,0},{3,1},{4,6},{5,7},{6,4},{7,5},{8,10},{9,11},{10,... | collective-permute-start | bytes 393224 | tf_op jit(solution)/shard_map/ppermute | solution.py:31
  7.0 1.1 collective-permute-start.1
  9.0 4.7 %shard_map.76 = (bf16[3584,128]{1,0:T(8,128)(2,1)}, bf16[4,2,896,128]{3,2,1,0:T(8,128)(2,1)}) custom-call(bf16[128,3584]{1,0:T(8,128)(2,1)} %pre_ref.1, bf16[128,3584]{1,0:T(8,128)(2,1)} %grad_ref.1), custom_call_target="tpu_custom_call" | custom-call | flops 13762560 | bytes 4587520 | tf_op jit(solution)/shard_map/pallas_call | solution.py:60
  14.4 2.2 %collective-permute-start.5 = (bf16[64,2048]{1,0:T(8,128)(2,1)}, bf16[64,2048]{1,0:T(8,128)(2,1)}, u32[]{:S(2)}, u32[]{:S(2)}) collective-permute-start(bf16[64,2048]{1,0:T(8,128)(2,1)} %f0), channel_id=1, source_target_pairs={{0,64},{32,96},{64,0},{96,32},{1,65},{33,97},{65,1},{97,33},{2,66}... | collective-permute-start | bytes 786440 | tf_op jit(solution)/shard_map/ppermute | solution.py:31
  17.2 1.4 %collective-permute-start.9 = (bf16[256,1024]{1,0:T(8,128)(2,1)S(1)}, bf16[256,1024]{1,0:T(8,128)(2,1)S(1)}, u32[]{:S(2)}, u32[]{:S(2)}) collective-permute-start(bf16[256,1024]{1,0:T(8,128)(2,1)S(1)} %pad_maximum_fusion.b0), channel_id=1, source_target_pairs={{0,96},{32,0},{64,32},{96,64},{1,97},{33,1},{65,33},{97,65},{2,98}... | collective-permute-start | bytes 1572872 | tf_op jit(solution)/shard_map/ppermute | solution.py:31
  18.7 1.7 %collective-permute-start.10 = (bf16[256,1024]{1,0:T(8,128)(2,1)S(1)}, bf16[256,1024]{1,0:T(8,128)(2,1)S(1)}, u32[]{:S(2)}, u32[]{:S(2)}) collective-permute-start(bf16[256,1024]{1,0:T(8,128)(2,1)S(1)} %pad_maximum_fusion.b0), channel_id=1, source_target_pairs={{0,64},{32,96},{64,0},{96,32},{1,65},{33,97},{65,1},{97,33},{2,66}... | collective-permute-start | bytes 1572872 | tf_op jit(solution)/shard_map/ppermute | solution.py:31
  21.3 3.6 %all-to-all-start = ((bf16[4,2,896,128]{3,2,1,0:T(8,128)(2,1)}), bf16[4,2,896,128]{3,2,1,0:T(8,128)(2,1)S(1)}, u32[]{:S(2)}, u32[]{:S(2)}) async-start(bf16[4,2,896,128]{3,2,1,0:T(8,128)(2,1)} %get-tuple-element.41), calls=%async_computation | async-start | bytes 3670016 | tf_op jit(solution)/shard_map/all_to_all | solution.py:281
  25.5 14.8 %shard_map.77 = (bf16[128,3584]{1,0:T(8,128)(2,1)}, bf16[4,64,2048]{2,1,0:T(8,128)(2,1)}, bf16[64,3584]{1,0:T(8,128)(2,1)}, bf16[64,3584]{1,0:T(8,128)(2,1)}) custom-call(s32[4]{0:T(128)} %pad_add_fusion.place_ref, bf16[64,2048]{1,0:T(8,128)(2,1)} %f0, bf16[64,2048]{1,0:T(8,128)(2,1)} %copy-done.15, bf16[64,2048]{1,0:T(8,128)(2,1)} %collective-permute-done.5.f2, ...), custom_call_target="tpu_custom_call" | custom-call | flops 22548578304 | bytes 14680064 | tf_op jit(solution)/shard_map/pallas_call | solution.py:193
  40.9 1.5 %collective-permute-done.7.refs_0_ = bf16[64,3584]{1,0:T(8,128)(2,1)S(1)} collective-permute-done((bf16[64,3584]{1,0:T(8,128)(2,1)}, bf16[64,3584]{1,0:T(8,128)(2,1)S(1)}, u32[]{:S(2)}, u32[]{:S(2)}) %collective-permute-start.7) | collective-permute-done | bytes 458784 | tf_op jit(solution)/shard_map/ppermute | solution.py:31
  43.2 3.9 %shard_map.78 = bf16[128,3584]{1,0:T(8,128)(2,1)} custom-call(bf16[128,3584]{1,0:T(8,128)(2,1)} %get-tuple-element.46.keep_ref, bf16[64,3584]{1,0:T(8,128)(2,1)} %copy-done.4, bf16[64,3584]{1,0:T(8,128)(2,1)} %collective-permute-done.8.refs_1_), custom_call_target="tpu_custom_call" | custom-call | flops 262144 | bytes 262144 | tf_op jit(solution)/shard_map/pallas_call | solution.py:230
  48.2 5.6 %all-to-all-start.1 = ((bf16[4,64,2048]{2,1,0:T(8,128)(2,1)}), bf16[4,64,2048]{2,1,0:T(8,128)(2,1)S(1)}, u32[]{:S(2)}, u32[]{:S(2)}) async-start(bf16[4,64,2048]{2,1,0:T(8,128)(2,1)} %get-tuple-element.57), calls=%async_computation.1 | async-start | bytes 2097152 | tf_op jit(solution)/shard_map/all_to_all | solution.py:291
  53.8 4.8 %shard_map.79 = (bf16[112,1024]{1,0:T(8,128)(2,1)}, bf16[112,1024]{1,0:T(8,128)(2,1)}, bf16[112,1024]{1,0:T(8,128)(2,1)}, bf16[112,1024]{1,0:T(8,128)(2,1)}) custom-call(s32[4]{0:T(128)} %pad_add_fusion.place_ref, bf16[4,2,896,128]{3,2,1,0:T(8,128)(2,1)} %copy-done, bf16[4,2,896,128]{3,2,1,0:T(8,128)(2,1)} %collective-permute-done.12.oth_ref, ...), custom_call_target="tpu_custom_call" | custom-call | flops 1048576 | bytes 1048576 | tf_op jit(solution)/shard_map/pallas_call | solution.py:137
  58.6 5.4 %collective-permute-start.24 = (bf16[112,1024]{1,0:T(8,128)(2,1)}, bf16[112,1024]{1,0:T(8,128)(2,1)S(1)}, u32[]{:S(2)}, u32[]{:S(2)}) collective-permute-start(bf16[112,1024]{1,0:T(8,128)(2,1)} %get-tuple-element.71), channel_id=1, source_target_pairs={{0,28},{4,0},{8,4},{12,8},{16,12},{20,16},{24,20},{28,24},{1,29},{... | collective-permute-start | bytes 688136 | tf_op jit(solution)/shard_map/ppermute | solution.py:31
  64.0 7.6 %shard_map.80 = (bf16[112,1024]{1,0:T(8,128)(2,1)}, bf16[112,1024]{1,0:T(8,128)(2,1)}, bf16[112,1024]{1,0:T(8,128)(2,1)}, bf16[112,1024]{1,0:T(8,128)(2,1)}, bf1...) custom-call(s32[4]{0:T(128)} %pad_add_fusion.place_ref, ...), custom_call_target="tpu_custom_call" | custom-call | flops 1048576 | bytes 1048576 | tf_op jit(solution)/shard_map/pallas_call | solution.py:137
  71.7 1.1 add.65
  72.7 3.3 %collective-permute-start.25 = (bf16[112,1024]{1,0:T(8,128)(2,1)S(1)}, bf16[112,1024]{1,0:T(8,128)(2,1)S(1)}, u32[]{:S(2)}, u32[]{:S(2)}) collective-permute-start(bf16[112,1024]{1,0:T(8,128)(2,1)S(1)} %add.65), channel_id=1, source_target_pairs={{0,28},{4,0},{8,4},{12,8},{16,12},{20,16},{24,20},{28,24},{1,29},{... | collective-permute-start | bytes 688136 | tf_op jit(solution)/shard_map/ppermute | solution.py:31
  77.2 3.2 %collective-permute-start.17 = (bf16[112,1024]{1,0:T(8,128)(2,1)}, bf16[112,1024]{1,0:T(8,128)(2,1)S(1)}, u32[]{:S(2)}, u32[]{:S(2)}) collective-permute-start(bf16[112,1024]{1,0:T(8,128)(2,1)} %get-tuple-element.64), channel_id=1, source_target_pairs={{0,28},{4,0},{8,4},{12,8},{16,12},{20,16},{24,20},{28,24},{1,29},{... | collective-permute-start | bytes 688136 | tf_op jit(solution)/shard_map/ppermute | solution.py:31
  81.6 3.5 %collective-permute-start.26 = (bf16[112,1024]{1,0:T(8,128)(2,1)S(1)}, bf16[112,1024]{1,0:T(8,128)(2,1)S(1)}, u32[]{:S(2)}, u32[]{:S(2)}) collective-permute-start(bf16[112,1024]{1,0:T(8,128)(2,1)S(1)} %add.66), channel_id=1, source_target_pairs={{0,28},{4,0},{8,4},{12,8},{16,12},{20,16},{24,20},{28,24},{1,29},{... | collective-permute-start | bytes 688136 | tf_op jit(solution)/shard_map/ppermute | solution.py:31
  87.3 3.3 %collective-permute-start.18 = (bf16[112,1024]{1,0:T(8,128)(2,1)S(1)}, bf16[112,1024]{1,0:T(8,128)(2,1)S(1)}, u32[]{:S(2)}, u32[]{:S(2)}) collective-permute-start(bf16[112,1024]{1,0:T(8,128)(2,1)S(1)} %add.59), channel_id=1, source_target_pairs={{0,28},{4,0},{8,4},{12,8},{16,12},{20,16},{24,20},{28,24},{1,29},{... | collective-permute-start | bytes 688136 | tf_op jit(solution)/shard_map/ppermute | solution.py:31
  91.7 4.3 %collective-permute-start.27 = (bf16[112,1024]{1,0:T(8,128)(2,1)S(1)}, bf16[112,1024]{1,0:T(8,128)(2,1)S(1)}, u32[]{:S(2)}, u32[]{:S(2)}) collective-permute-start(bf16[112,1024]{1,0:T(8,128)(2,1)S(1)} %add.67), channel_id=1, source_target_pairs={{0,29},{1,28},{2,31},{3,30},{4,1},{5,0},{6,3},{7,2},{8,5},{9,4},{1... | collective-permute-start | bytes 688136 | tf_op jit(solution)/shard_map/ppermute | solution.py:255
  99.3 1.2 %collective-permute-start.19 = (bf16[112,1024]{1,0:T(8,128)(2,1)S(1)}, bf16[112,1024]{1,0:T(8,128)(2,1)S(1)}, u32[]{:S(2)}, u32[]{:S(2)}) collective-permute-start(bf16[112,1024]{1,0:T(8,128)(2,1)S(1)} %add.60), channel_id=1, source_target_pairs={{0,28},{4,0},{8,4},{12,8},{16,12},{20,16},{24,20},{28,24},{1,29},{... | collective-permute-start | bytes 688136 | tf_op jit(solution)/shard_map/ppermute | solution.py:31
  102.1 2.5 %collective-permute-done.23 = bf16[112,1024]{1,0:T(8,128)(2,1)S(1)} collective-permute-done((bf16[112,1024]{1,0:T(8,128)(2,1)}, bf16[112,1024]{1,0:T(8,128)(2,1)S(1)}, u32[]{:S(2)}, u32[]{:S(2)}) %collective-permute-start.23) | collective-permute-done | bytes 229408 | tf_op jit(solution)/shard_map/ppermute | solution.py:253
  105.4 2.4 %collective-permute-done.16 = bf16[112,1024]{1,0:T(8,128)(2,1)S(1)} collective-permute-done((bf16[112,1024]{1,0:T(8,128)(2,1)S(1)}, bf16[112,1024]{1,0:T(8,128)(2,1)S(1)}, u32[]{:S(2)}, u32[]{:S(2)}) %collective-permute-start.16) | collective-permute-done | bytes 229408 | tf_op jit(solution)/shard_map/ppermute | solution.py:31
  (91 shorter events, 20.3 us)
Async XLA Ops:
  0.6 13.7 %collective-permute-start.3 = (bf16[64,2048]{1,0:T(8,128)(2,1)}, bf16[64,2048]{1,0:T(8,128)(2,1)S(1)}, u32[]{:S(2)}, u32[]{:S(2)}) collective-permute-start(bf16[64,2048]{1,0:T(8,128)(2,1)} %f0), channel_id=1, source_target_pairs={{0,32},{32,64},{64,96},{96,0},{1,33},{33,65},{65,97},{97,1},{2,34}... | collective-permute-start | bytes 786440 | tf_op jit(solution)/shard_map/ppermute | solution.py:31
  2.2 12.1 %collective-permute-start.4 = (bf16[64,2048]{1,0:T(8,128)(2,1)}, bf16[64,2048]{1,0:T(8,128)(2,1)S(1)}, u32[]{:S(2)}, u32[]{:S(2)}) collective-permute-start(bf16[64,2048]{1,0:T(8,128)(2,1)} %f0), channel_id=1, source_target_pairs={{0,96},{32,0},{64,32},{96,64},{1,97},{33,1},{65,33},{97,65},{2,98}... | collective-permute-start | bytes 786440 | tf_op jit(solution)/shard_map/ppermute | solution.py:31
  4.1 9.7 %collective-permute-start.2 = (bf16[64,1024]{1,0:T(8,128)(2,1)S(1)}, bf16[64,1024]{1,0:T(8,128)(2,1)S(1)}, u32[]{:S(2)}, u32[]{:S(2)}) collective-permute-start(bf16[64,1024]{1,0:T(8,128)(2,1)S(1)} %get-tuple-element.76), channel_id=1, source_target_pairs={{0,2},{1,3},{2,0},{3,1},{4,6},{5,7},{6,4},{7,5},{8,10},{9,11},{10,... | collective-permute-start | bytes 393224 | tf_op jit(solution)/shard_map/ppermute | solution.py:31
  14.3 11.2 %collective-permute-start.6 = (bf16[3584,128]{1,0:T(8,128)(2,1)}, bf16[3584,128]{1,0:T(8,128)(2,1)}, u32[]{:S(2)}, u32[]{:S(2)}) collective-permute-start(bf16[3584,128]{1,0:T(8,128)(2,1)} %get-tuple-element.45.own_ref), channel_id=1, source_target_pairs={{0,128},{128,0},{1,129},{129,1},{2,130},{130,2},{3,131},{131,3},{4... | collective-permute-start | bytes 2752520 | tf_op jit(solution)/shard_map/ppermute | solution.py:31
  14.4 11.1 %collective-permute-start.5 = (bf16[64,2048]{1,0:T(8,128)(2,1)}, bf16[64,2048]{1,0:T(8,128)(2,1)}, u32[]{:S(2)}, u32[]{:S(2)}) collective-permute-start(bf16[64,2048]{1,0:T(8,128)(2,1)} %f0), channel_id=1, source_target_pairs={{0,64},{32,96},{64,0},{96,32},{1,65},{33,97},{65,1},{97,33},{2,66}... | collective-permute-start | bytes 786440 | tf_op jit(solution)/shard_map/ppermute | solution.py:31
  17.2 29.9 %collective-permute-start.9 = (bf16[256,1024]{1,0:T(8,128)(2,1)S(1)}, bf16[256,1024]{1,0:T(8,128)(2,1)S(1)}, u32[]{:S(2)}, u32[]{:S(2)}) collective-permute-start(bf16[256,1024]{1,0:T(8,128)(2,1)S(1)} %pad_maximum_fusion.b0), channel_id=1, source_target_pairs={{0,96},{32,0},{64,32},{96,64},{1,97},{33,1},{65,33},{97,65},{2,98}... | collective-permute-start | bytes 1572872 | tf_op jit(solution)/shard_map/ppermute | solution.py:31
  18.7 28.7 %collective-permute-start.10 = (bf16[256,1024]{1,0:T(8,128)(2,1)S(1)}, bf16[256,1024]{1,0:T(8,128)(2,1)S(1)}, u32[]{:S(2)}, u32[]{:S(2)}) collective-permute-start(bf16[256,1024]{1,0:T(8,128)(2,1)S(1)} %pad_maximum_fusion.b0), channel_id=1, source_target_pairs={{0,64},{32,96},{64,0},{96,32},{1,65},{33,97},{65,1},{97,33},{2,66}... | collective-permute-start | bytes 1572872 | tf_op jit(solution)/shard_map/ppermute | solution.py:31
  20.3 27.2 %collective-permute-start.11 = (bf16[256,1024]{1,0:T(8,128)(2,1)S(1)}, bf16[256,1024]{1,0:T(8,128)(2,1)}, u32[]{:S(2)}, u32[]{:S(2)}) collective-permute-start(bf16[256,1024]{1,0:T(8,128)(2,1)S(1)} %pad_maximum_fusion.b0), channel_id=1, source_target_pairs={{0,32},{32,64},{64,96},{96,0},{1,33},{33,65},{65,97},{97,1},{2,34}... | collective-permute-start | bytes 1572872 | tf_op jit(solution)/shard_map/ppermute | solution.py:31
  21.3 26.8 %all-to-all-start = ((bf16[4,2,896,128]{3,2,1,0:T(8,128)(2,1)}), bf16[4,2,896,128]{3,2,1,0:T(8,128)(2,1)S(1)}, u32[]{:S(2)}, u32[]{:S(2)}) async-start(bf16[4,2,896,128]{3,2,1,0:T(8,128)(2,1)} %get-tuple-element.41), calls=%async_computation | async-start | bytes 3670016 | tf_op jit(solution)/shard_map/all_to_all | solution.py:281
  48.2 32.2 %all-to-all-start.1 = ((bf16[4,64,2048]{2,1,0:T(8,128)(2,1)}), bf16[4,64,2048]{2,1,0:T(8,128)(2,1)S(1)}, u32[]{:S(2)}, u32[]{:S(2)}) async-start(bf16[4,64,2048]{2,1,0:T(8,128)(2,1)} %get-tuple-element.57), calls=%async_computation.1 | async-start | bytes 2097152 | tf_op jit(solution)/shard_map/all_to_all | solution.py:291
  58.6 13.0 %collective-permute-start.24 = (bf16[112,1024]{1,0:T(8,128)(2,1)}, bf16[112,1024]{1,0:T(8,128)(2,1)S(1)}, u32[]{:S(2)}, u32[]{:S(2)}) collective-permute-start(bf16[112,1024]{1,0:T(8,128)(2,1)} %get-tuple-element.71), channel_id=1, source_target_pairs={{0,28},{4,0},{8,4},{12,8},{16,12},{20,16},{24,20},{28,24},{1,29},{... | collective-permute-start | bytes 688136 | tf_op jit(solution)/shard_map/ppermute | solution.py:31
  64.0 12.1 %collective-permute-start.20 = (bf16[112,1024]{1,0:T(8,128)(2,1)}, bf16[112,1024]{1,0:T(8,128)(2,1)S(1)}, u32[]{:S(2)}, u32[]{:S(2)}) collective-permute-start(bf16[112,1024]{1,0:T(8,128)(2,1)} %get-tuple-element.67), channel_id=1, source_target_pairs={{0,4},{4,8},{8,12},{12,16},{16,20},{20,24},{24,28},{28,0},{1,5},{5... | collective-permute-start | bytes 688136 | tf_op jit(solution)/shard_map/ppermute | solution.py:31
  64.0 16.4 %collective-permute-start.13 = (bf16[112,1024]{1,0:T(8,128)(2,1)}, bf16[112,1024]{1,0:T(8,128)(2,1)S(1)}, u32[]{:S(2)}, u32[]{:S(2)}) collective-permute-start(bf16[112,1024]{1,0:T(8,128)(2,1)} %get-tuple-element.56), channel_id=1, source_target_pairs={{0,4},{4,8},{8,12},{12,16},{16,20},{20,24},{24,28},{28,0},{1,5},{5... | collective-permute-start | bytes 688136 | tf_op jit(solution)/shard_map/ppermute | solution.py:31
  72.7 8.8 %collective-permute-start.25 = (bf16[112,1024]{1,0:T(8,128)(2,1)S(1)}, bf16[112,1024]{1,0:T(8,128)(2,1)S(1)}, u32[]{:S(2)}, u32[]{:S(2)}) collective-permute-start(bf16[112,1024]{1,0:T(8,128)(2,1)S(1)} %add.65), channel_id=1, source_target_pairs={{0,28},{4,0},{8,4},{12,8},{16,12},{20,16},{24,20},{28,24},{1,29},{... | collective-permute-start | bytes 688136 | tf_op jit(solution)/shard_map/ppermute | solution.py:31
  77.1 9.0 %collective-permute-start.21 = (bf16[112,1024]{1,0:T(8,128)(2,1)S(1)}, bf16[112,1024]{1,0:T(8,128)(2,1)}, u32[]{:S(2)}, u32[]{:S(2)}) collective-permute-start(bf16[112,1024]{1,0:T(8,128)(2,1)S(1)} %add.62), channel_id=1, source_target_pairs={{0,4},{4,8},{8,12},{12,16},{16,20},{20,24},{24,28},{28,0},{1,5},{5... | collective-permute-start | bytes 688136 | tf_op jit(solution)/shard_map/ppermute | solution.py:31
  77.2 10.0 %collective-permute-start.17 = (bf16[112,1024]{1,0:T(8,128)(2,1)}, bf16[112,1024]{1,0:T(8,128)(2,1)S(1)}, u32[]{:S(2)}, u32[]{:S(2)}) collective-permute-start(bf16[112,1024]{1,0:T(8,128)(2,1)} %get-tuple-element.64), channel_id=1, source_target_pairs={{0,28},{4,0},{8,4},{12,8},{16,12},{20,16},{24,20},{28,24},{1,29},{... | collective-permute-start | bytes 688136 | tf_op jit(solution)/shard_map/ppermute | solution.py:31
  81.4 9.8 %collective-permute-start.14 = (bf16[112,1024]{1,0:T(8,128)(2,1)S(1)}, bf16[112,1024]{1,0:T(8,128)(2,1)S(1)}, u32[]{:S(2)}, u32[]{:S(2)}) collective-permute-start(bf16[112,1024]{1,0:T(8,128)(2,1)S(1)} %add.55), channel_id=1, source_target_pairs={{0,4},{4,8},{8,12},{12,16},{16,20},{20,24},{24,28},{28,0},{1,5},{5... | collective-permute-start | bytes 688136 | tf_op jit(solution)/shard_map/ppermute | solution.py:31
  81.6 10.0 %collective-permute-start.26 = (bf16[112,1024]{1,0:T(8,128)(2,1)S(1)}, bf16[112,1024]{1,0:T(8,128)(2,1)S(1)}, u32[]{:S(2)}, u32[]{:S(2)}) collective-permute-start(bf16[112,1024]{1,0:T(8,128)(2,1)S(1)} %add.66), channel_id=1, source_target_pairs={{0,28},{4,0},{8,4},{12,8},{16,12},{20,16},{24,20},{28,24},{1,29},{... | collective-permute-start | bytes 688136 | tf_op jit(solution)/shard_map/ppermute | solution.py:31
  87.1 9.8 %collective-permute-start.22 = (bf16[112,1024]{1,0:T(8,128)(2,1)S(1)}, bf16[112,1024]{1,0:T(8,128)(2,1)S(1)}, u32[]{:S(2)}, u32[]{:S(2)}) collective-permute-start(bf16[112,1024]{1,0:T(8,128)(2,1)S(1)} %add.63), channel_id=1, source_target_pairs={{0,4},{4,8},{8,12},{12,16},{16,20},{20,24},{24,28},{28,0},{1,5},{5... | collective-permute-start | bytes 688136 | tf_op jit(solution)/shard_map/ppermute | solution.py:31
  87.3 11.9 %collective-permute-start.18 = (bf16[112,1024]{1,0:T(8,128)(2,1)S(1)}, bf16[112,1024]{1,0:T(8,128)(2,1)S(1)}, u32[]{:S(2)}, u32[]{:S(2)}) collective-permute-start(bf16[112,1024]{1,0:T(8,128)(2,1)S(1)} %add.59), channel_id=1, source_target_pairs={{0,28},{4,0},{8,4},{12,8},{16,12},{20,16},{24,20},{28,24},{1,29},{... | collective-permute-start | bytes 688136 | tf_op jit(solution)/shard_map/ppermute | solution.py:31
  91.3 9.1 %collective-permute-start.15 = (bf16[112,1024]{1,0:T(8,128)(2,1)S(1)}, bf16[112,1024]{1,0:T(8,128)(2,1)S(1)}, u32[]{:S(2)}, u32[]{:S(2)}) collective-permute-start(bf16[112,1024]{1,0:T(8,128)(2,1)S(1)} %add.56), channel_id=1, source_target_pairs={{0,4},{4,8},{8,12},{12,16},{16,20},{20,24},{24,28},{28,0},{1,5},{5... | collective-permute-start | bytes 688136 | tf_op jit(solution)/shard_map/ppermute | solution.py:31
  91.7 10.4 %collective-permute-start.27 = (bf16[112,1024]{1,0:T(8,128)(2,1)S(1)}, bf16[112,1024]{1,0:T(8,128)(2,1)S(1)}, u32[]{:S(2)}, u32[]{:S(2)}) collective-permute-start(bf16[112,1024]{1,0:T(8,128)(2,1)S(1)} %add.67), channel_id=1, source_target_pairs={{0,29},{1,28},{2,31},{3,30},{4,1},{5,0},{6,3},{7,2},{8,5},{9,4},{1... | collective-permute-start | bytes 688136 | tf_op jit(solution)/shard_map/ppermute | solution.py:255
  97.7 6.9 %collective-permute-start.23 = (bf16[112,1024]{1,0:T(8,128)(2,1)}, bf16[112,1024]{1,0:T(8,128)(2,1)S(1)}, u32[]{:S(2)}, u32[]{:S(2)}) collective-permute-start(bf16[112,1024]{1,0:T(8,128)(2,1)} %add.64), channel_id=1, source_target_pairs={{0,1},{1,0},{2,3},{3,2},{4,5},{5,4},{6,7},{7,6},{8,9},{9,8},{10,11... | collective-permute-start | bytes 688136 | tf_op jit(solution)/shard_map/ppermute | solution.py:253
  100.5 7.3 %collective-permute-start.16 = (bf16[112,1024]{1,0:T(8,128)(2,1)S(1)}, bf16[112,1024]{1,0:T(8,128)(2,1)S(1)}, u32[]{:S(2)}, u32[]{:S(2)}) collective-permute-start(bf16[112,1024]{1,0:T(8,128)(2,1)S(1)} %add.57), channel_id=1, source_target_pairs={{0,4},{4,8},{8,12},{12,16},{16,20},{20,24},{24,28},{28,0},{1,5},{5... | collective-permute-start | bytes 688136 | tf_op jit(solution)/shard_map/ppermute | solution.py:31
  (22 other events, 175.6 us)

commit v4 on v3

--- a/solution.py
+++ b/solution.py
@@ -47,7 +47,7 @@
     g = grad_ref[...].astype(F32) * gelu_slope(pre_ref[...].astype(F32))
     flip = g.T.astype(BF)
     flip_ref[...] = flip
-    for k in range(2):
+    for k in range(4):
         for q in range(4):
             block = flip[k * 448 + q * 112 : k * 448 + q * 112 + 112]
             parts_ref[q ^ 1, 0, k * 112 : k * 112 + 112] = block
@@ -56,7 +56,7 @@
 
 def grad_pre_flipped(pre, grad):
     rows, cols = pre.shape
-    tile = 896
+    tile = 1792
     return pl.pallas_call(
         grad_kernel,
         grid=(cols // tile,),
@@ -76,81 +76,93 @@
     )(pre, grad)
 
 
-def copy_acts(place_ref, blocks, acts, sems):
-    x, r, y = (lax.axis_index(n) for n in ("col", "row", "y"))
+def copy_acts(blocks, acts, sems):
+    x, r, y = (lax.axis_index(name) for name in ("col", "row", "y"))
     copies = []
     for d, block in enumerate(blocks):
         at = lax.rem(x + d, 4)
-        start = ((at // 2) ^ r) * 512 + lax.rem(at, 2) * 64
         for j, turn in enumerate((0, 3, 1, 2)):
-            row = pl.multiple_of(start + lax.rem(y + turn, 4) * 128, 64)
-            copies.append((block.at[pl.ds(j * 64, 64), :], acts.at[pl.ds(row, 64), :]))
-    return [pltpu.make_async_copy(a, b, sems.at[n]) for n, (a, b) in enumerate(copies)]
-
-
-def first_kernel(wanted, place_ref, own_ref, oth_ref, b0, b1, b2, b3, *rest):
+            to = acts.at[(at // 2) ^ r, lax.rem(y + turn, 4), lax.rem(at, 2)]
+            copies.append(pltpu.make_async_copy(block.at[j], to, sems.at[len(copies)]))
+    return copies
+
+
+def first_kernel(wanted, own_ref, oth_ref, b0, b1, b2, b3, *rest):
     outs, (acts, lhs, sems) = rest[:-3], rest[-3:]
     z = lax.axis_index("z")
-    copies = copy_acts(place_ref, (b0, b1, b2, b3), acts, sems)
+    copies = copy_acts((b0, b1, b2, b3), acts, sems)
     for i, (which, offset) in enumerate(wanted):
         rows = pl.ds(pl.multiple_of(lax.rem(z + offset, 8) * 112, 16), 112)
         for h, ref in enumerate((own_ref, oth_ref)):
-            for k in range(4):
-                to = lhs.at[pl.ds(i * 112, 112), pl.ds(h * 512 + k * 128, 128)]
-                sem = sems.at[len(copies)]
-                copies.append(pltpu.make_async_copy(ref.at[k, which, rows, :], to, sem))
+            to = lhs.at[pl.ds(h * 4, 4), pl.ds(i * 112, 112), :]
+            sem = sems.at[len(copies)]
+            copies.append(pltpu.make_async_copy(ref.at[:, which, rows, :], to, sem))
     for copy in copies:
         copy.start()
     for copy in copies:
         copy.wait()
-    part = jnp.dot(lhs[...], acts[...], preferred_element_type=F32)
+    both = jnp.concatenate([lhs[k] for k in range(8)], axis=1)
+    part = jnp.dot(both, acts[...].reshape(1024, 1024), preferred_element_type=F32)
     for i, out in enumerate(outs):
         out[...] = part[i * 112 : i * 112 + 112].astype(BF)
 
 
-def rest_kernel(wanted, place_ref, own_ref, oth_ref, b0, b1, b2, b3, *rest):
-    outs, (acts, lhs, sems) = rest[:-3], rest[-3:]
+def rest_kernel(wanted, own_ref, oth_ref, b0, b1, b2, b3, *rest):
+    outs, (acts, lhs, done, sems) = rest[:-4], rest[-4:]
     z = lax.axis_index("z")
-    copies = copy_acts(place_ref, (b0, b1, b2, b3), acts, sems)
+    copies = copy_acts((b0, b1, b2, b3), acts, sems)
     for which in range(2):
         for h, ref in enumerate((own_ref, oth_ref)):
-            for k in range(4):
-                to = lhs.at[which, :, pl.ds(h * 512 + k * 128, 128)]
-                copies.append(pltpu.make_async_copy(ref.at[k, which], to, sems.at[len(copies)]))
+            to = lhs.at[which, pl.ds(h * 4, 4)]
+            copies.append(pltpu.make_async_copy(ref.at[:, which], to, sems.at[len(copies)]))
     for copy in copies:
         copy.start()
-    for copy in copies:
+    for copy in copies[:18]:
         copy.wait()
-    for i in range(0, len(wanted), 4):
-        rows = [
-            lhs[which, pl.ds(pl.multiple_of(lax.rem(z + offset, 8) * 112, 16), 112), :]
-            for which, offset in wanted[i : i + 4]
-        ]
-        part = jnp.dot(jnp.concatenate(rows, axis=0), acts[...], preferred_element_type=F32)
-        for k in range(4):
-            outs[i + k][...] = part[k * 112 : k * 112 + 112].astype(BF)
-
-
-def weight_parts(place, own, oth, blocks, wanted, first, late=()):
+    sent = []
+    for which in range(2):
+        if which == 1:
+            for copy in copies[18:]:
+                copy.wait()
+        mine = [(i, offset) for i, (w, offset) in enumerate(wanted) if w == which]
+        pieces = []
+        for _, offset in mine:
+            rows = pl.ds(pl.multiple_of(lax.rem(z + offset, 8) * 112, 16), 112)
+            pieces.append(jnp.concatenate([lhs[which, k, rows, :] for k in range(8)], axis=1))
+        both = jnp.concatenate(pieces, axis=0)
+        part = jnp.dot(both, acts[...].reshape(1024, 1024), preferred_element_type=F32)
+        for k, (i, _) in enumerate(mine):
+            done[i] = part[k * 112 : k * 112 + 112].astype(BF)
+            sent.append(pltpu.make_async_copy(done.at[i], outs[i], sems.at[20 + i]))
+            sent[-1].start()
+    for copy in sent:
+        copy.wait()
+
+
+def weight_parts(own, oth, blocks, wanted, first):
     anywhere = pl.BlockSpec(memory_space=pl.ANY)
     n = len(wanted)
+    if first:
+        scratch = [pltpu.VMEM((8, 112 * n, 128), BF), pltpu.SemaphoreType.DMA((16 + 2 * n,))]
+    else:
+        scratch = [
+            pltpu.VMEM((2, 8, 896, 128), BF),
+            pltpu.VMEM((n, 112, 1024), BF),
+            pltpu.SemaphoreType.DMA((20 + n,)),
+        ]
     return pl.pallas_call(
         functools.partial(first_kernel if first else rest_kernel, wanted),
         grid=(1,),
-        in_specs=[SMEM] + [anywhere] * (6 + len(late)),
-        out_specs=[pl.BlockSpec((112, 1024), lambda i: (0, 0))] * n,
-        scratch_shapes=[
-            pltpu.VMEM((1024, 1024), BF),
-            pltpu.VMEM((112 * n, 1024) if first else (2, 896, 1024), BF),
-            pltpu.SemaphoreType.DMA((16 + (8 * n if first else 16),)),
-        ],
+        in_specs=[anywhere] * 6,
+        out_specs=[pl.BlockSpec((112, 1024), lambda i: (0, 0)) if first else anywhere] * n,
+        scratch_shapes=[pltpu.VMEM((2, 4, 2, 64, 1024), BF)] + scratch,
         out_shape=[jax.ShapeDtypeStruct((112, 1024), BF)] * n,
         compiler_params=params(60),
         cost_estimate=pl.CostEstimate(flops=2**20, bytes_accessed=2**20, transcendentals=0),
-    )(place, own, oth, *blocks, *late)
-
-
-def both_kernel(place_ref, f0, f1, f2, f3, own_ref, oth_ref, w_ref, keep_ref, out_ref, *rest):
+    )(own, oth, *(block.reshape(4, 64, 1024) for block in blocks))
+
+
+def both_kernel(f0, f1, f2, f3, own_ref, oth_ref, w_ref, keep_ref, out_ref, *rest):
     gives, rows_ref, acc = rest[:-2], rest[-2], rest[-1]
     step, last = pl.program_id(0), pl.num_programs(0) - 1
     x, r = lax.axis_index("col"), lax.axis_index("row")
@@ -187,14 +199,13 @@
                 out_ref[at] = flat[half * 128 + k * 64 : half * 128 + k * 64 + 64]
 
 
-def both_products(place, fwd, own, oth, weight):
+def both_products(fwd, own, oth, weight):
     feats, hidden = weight.shape
     tile = 512
     return pl.pallas_call(
         both_kernel,
         grid=(hidden // tile,),
-        in_specs=[SMEM]
-        + [pl.BlockSpec((64, feats), lambda i: (0, 0))] * 4
+        in_specs=[pl.BlockSpec((64, feats), lambda i: (0, 0))] * 4
         + [pl.BlockSpec((tile, 128), lambda i: (i, 0))] * 2
         + [pl.BlockSpec((feats, tile), lambda i: (0, i))],
         out_specs=[
@@ -212,7 +223,7 @@
         cost_estimate=pl.CostEstimate(
             flops=12 * 256 * 2048 * hidden, bytes_accessed=2 * 2048 * hidden, transcendentals=0
         ),
-    )(place, *fwd, own, oth, weight)
+    )(*fwd, own, oth, weight)
 
 
 def gelu_kernel(keep_ref, *refs):
@@ -225,7 +236,7 @@
 
 def gelu_rows(keep, got):
     rows, cols = keep.shape
-    tile = 896
+    tile = 1792
     whole = pl.BlockSpec((rows, tile), lambda i: (0, i))
     return pl.pallas_call(
         gelu_kernel,
@@ -238,30 +249,32 @@
     )(keep, *got)
 
 
+def send_z(value, step, swap=False):
+    pairs = []
+    for k in range(8):
+        for y in range(4):
+            pairs.append((k * 4 + y, (k + step) % 8 * 4 + (y ^ 1 if swap else y)))
+    return lax.ppermute(value, ("z", "y"), pairs)
+
+
 def reduce_z(piece, step, swap, late=None):
-    partner = [(k, k ^ 1) for k in range(4)]
     far, near = piece[4], piece[-3 * step % 8]
     for hop in (3, 2, 1):
-        far = send(far, "z", step)
+        far = send_z(far, step)
         if hop == 3 and late is not None:
             far, late = together(far, late)
-        near = send(near, "z", -step)
+        near = send_z(near, -step, swap and hop == 1)
         far = far + piece[hop * step % 8]
         if hop > 1:
             near = near + piece[-(hop - 1) * step % 8]
-    if swap:
-        near = lax.ppermute(near + piece[0], "y", partner)
-        steps = [(k * 4 + a, (k + step) % 8 * 4 + b) for k in range(8) for a, b in partner]
-        far = lax.ppermute(far, ("z", "y"), steps)
-        return near.astype(F32) + far.astype(F32), late
-    far = send(far, "z", step)
-    return piece[0].astype(F32) + far.astype(F32) + near.astype(F32), late
+    own = lax.ppermute(piece[0], "y", [(k, k ^ 1) for k in range(4)]) if swap else piece[0]
+    far = send_z(far, step, swap)
+    return own.astype(F32) + near.astype(F32) + far.astype(F32), late
 
 
 def on_device(act_forward, weight, act_backward, pre_backward, grad_backward):
     r, x, z, y = (lax.axis_index(name) for name in ("row", "col", "z", "y"))
     ym = y % 2
-    place = jnp.stack([x, r, y, z]).astype(jnp.int32)
 
     left, right = send(act_forward, "col", 1), send(act_forward, "col", -1)
 
@@ -272,15 +285,13 @@
     )
     flipped, halves = grad_pre_flipped(pre_backward, grad_backward)
 
-    acts, halves, flipped, left, right, act_forward = together(
-        acts, halves, flipped, left, right, act_forward
-    )
+    acts, halves, flipped, left, right = together(acts, halves, flipped, left, right)
     far = send(act_forward, "col", 2)
     b1, b2, b3 = send(acts, "col", -1), send(acts, "col", 2), send(acts, "col", 1)
     flipped_other = send(flipped, "row", 1)
     grads_own = lax.all_to_all(halves, "y", 0, 0)
     keep, packed, *gives = both_products(
-        place, (act_forward, right, far, left), flipped, flipped_other, weight
+        (act_forward, right, far, left), flipped, flipped_other, weight
     )
 
     hidden_forward = gelu_rows(keep, [send(give, "row", 1) for give in gives])
@@ -290,16 +301,16 @@
     grads_other = send(grads_own, "row", 1)
     packed = lax.all_to_all(packed, "col", 0, 0)
     parts = {}
-    first = [(0, 4), (0, 3), (1, 4), (1, 5)]
+    first = [(0, 4), (1, 4)]
     others = [(w, o) for w in range(2) for o in range(8) if (w, o) not in first]
-    for wanted, late in ((first, ()), (others, ())):
+    for wanted in (first, others):
         got = weight_parts(
-            place, grads_own, grads_other, (acts, b1, b2, b3), wanted, wanted is first, late
+            grads_own, grads_other, (acts, b1, b2, b3), wanted, wanted is first
         )
         parts.update(zip(wanted, got))
     given, kept = ([parts[w, o] for o in range(8)] for w in range(2))
-    got, _ = reduce_z(given, -1, True)
-    kept, packed = reduce_z(kept, 1, False, packed)
+    got, _ = reduce_z(given, 1, True)
+    kept, packed = reduce_z(kept, -1, False, packed)
     grad_inputs = packed.astype(F32).sum(axis=0).astype(BF)
     grad_weight = jnp.where(
         ym == 0, jnp.concatenate([kept, got], axis=1), jnp.concatenate([got, kept], axis=1)

time: 110 us -> 107 us (0.973)
  waiting for transfers between devices: 13.4 us -> 18.7 us
  starting transfers between devices: 49.7 us -> 45.3 us
  Pallas kernels: 35.8 us -> 31.7 us
  local copies, waits for them, and re-layouts: 1.12 us -> 2.36 us
    ppermute x26 -> x13, starting transfers between devices: 35.6 us -> 14.3 us  [send(): return lax.ppermute(value, axis, [(i, (i + step) % n) for i in range(n)])]
    ppermute x2 -> x15, starting transfers between devices: 4.95 us -> 22.3 us  [the longest x14 22 us: send_z(): return lax.ppermute(value, ('z', 'y'), pairs)]
    ppermute x2 -> x15, waiting for transfers between devices: 3.01 us -> 12.7 us  [the longest x14 12.7 us: send_z(): return lax.ppermute(value, ('z', 'y'), pairs)]
    ppermute x26 -> x13, waiting for transfers between devices: 9.86 us -> 5.98 us  [send(): return lax.ppermute(value, axis, [(i, (i + step) % n) for i in range(n)])]
    pallas_call x2, Pallas kernels: 12.4 us -> 10.4 us  [weight_parts(): pl.pallas_call(functools.partial(first_kernel if first else rest_kernel,...]
    unnamed x32 -> x30, local copies, waits for them, and re-layouts: 0.14 us -> 1.37 us
    pallas_call x1, Pallas kernels: 3.91 us -> 2.75 us  [gelu_rows(): pl.pallas_call(gelu_kernel, grid=(cols // tile,), in_specs=[whole] + [pl....]
  transfers between devices with their start and end apart: 30 -> 30, of which waited for: 15 -> 15; matrix products, arithmetic and copies ran while one was open for 7% -> 7% of each run, Pallas kernels for 33% -> 30%
where the time goes in v4:
time: 107 us; the launch traced here: 106 us
  starting transfers between devices  45.3 us (42%)
  Pallas kernels  31.7 us (30%)
  waiting for transfers between devices  18.7 us (17%)
  other arithmetic  7.17 us (7%)
  local copies, waits for them, and re-layouts  2.36 us (2%)
    ppermute x14, starting transfers between devices, send_z(): return lax.ppermute(value, ('z', 'y'), pairs)  22 us
    pallas_call x1, Pallas kernels, both_products(): pl.pallas_call(both_kernel, grid=(hidden // tile,), in_specs=[pl.BlockSpe...  14.7 us
    ppermute x13, starting transfers between devices, send(): return lax.ppermute(value, axis, [(i, (i + step) % n) for i in range(n)])  14.3 us
    ppermute x14, waiting for transfers between devices, send_z(): return lax.ppermute(value, ('z', 'y'), pairs)  12.7 us
    pallas_call x2, Pallas kernels, weight_parts(): pl.pallas_call(functools.partial(first_kernel if first else rest_kernel,...  10.4 us
    ppermute x13, waiting for transfers between devices, send(): return lax.ppermute(value, axis, [(i, (i + step) % n) for i in range(n)])  5.98 us
    all_to_all x1, starting transfers between devices, on_device(): packed = lax.all_to_all(packed, 'col', 0, 0)  5.07 us
    pallas_call x1, Pallas kernels, grad_pre_flipped(): pl.pallas_call(grad_kernel, grid=(cols // tile,), in_specs=[pl.BlockSpec(...  3.78 us
  transfers between devices with their start and end apart: 30, of which 15 were waited for; matrix products, arithmetic and copies ran while one was open for 7% of the time, Pallas kernels for 30%

profile of v4, /device:TPU:2, one launch (start us, length us, event | category | flops | bytes accessed | tf_op | source)
XLA Modules:
  0.0 106.1 jit_solution(11635616630863171400)
XLA Ops:
  0.6 1.6 %collective-permute-start.3 = (bf16[64,2048]{1,0:T(8,128)(2,1)}, bf16[64,2048]{1,0:T(8,128)(2,1)S(1)}, u32[]{:S(2)}, u32[]{:S(2)}) collective-permute-start(bf16[64,2048]{1,0:T(8,128)(2,1)} %f0.1), channel_id=1, source_target_pairs={{0,32},{32,64},{64,96},{96,0},{1,33},{33,65},{65,97},{97,1},{2,34}... | collective-permute-start | bytes 786440 | tf_op jit(solution)/shard_map/ppermute | solution.py:31
  4.1 2.9 %collective-permute-start.2 = (bf16[64,1024]{1,0:T(8,128)(2,1)S(1)}, bf16[64,1024]{1,0:T(8,128)(2,1)S(1)}, u32[]{:S(2)}, u32[]{:S(2)}) collective-permute-start(bf16[64,1024]{1,0:T(8,128)(2,1)S(1)} %get-tuple-element.74), channel_id=1, source_target_pairs={{0,2},{1,3},{2,0},{3,1},{4,6},{5,7},{6,4},{7,5},{8,10},{9,11},{10,... | collective-permute-start | bytes 393224 | tf_op jit(solution)/shard_map/ppermute | solution.py:31
  9.0 3.8 %shard_map.76 = (bf16[3584,128]{1,0:T(8,128)(2,1)}, bf16[4,2,896,128]{3,2,1,0:T(8,128)(2,1)}) custom-call(bf16[128,3584]{1,0:T(8,128)(2,1)} %pre_ref.1, bf16[128,3584]{1,0:T(8,128)(2,1)} %grad_ref.1), custom_call_target="tpu_custom_call" | custom-call | flops 13762560 | bytes 4587520 | tf_op jit(solution)/shard_map/pallas_call | solution.py:60
  15.1 2.1 %collective-permute-start.5 = (bf16[64,2048]{1,0:T(8,128)(2,1)}, bf16[64,2048]{1,0:T(8,128)(2,1)}, u32[]{:S(2)}, u32[]{:S(2)}) collective-permute-start(bf16[64,2048]{1,0:T(8,128)(2,1)} %f0.1), channel_id=1, source_target_pairs={{0,64},{32,96},{64,0},{96,32},{1,65},{33,97},{65,1},{97,33},{2,66}... | collective-permute-start | bytes 786440 | tf_op jit(solution)/shard_map/ppermute | solution.py:31
  17.2 1.4 %collective-permute-start.9 = (bf16[256,1024]{1,0:T(8,128)(2,1)S(1)}, bf16[256,1024]{1,0:T(8,128)(2,1)S(1)}, u32[]{:S(2)}, u32[]{:S(2)}) collective-permute-start(bf16[256,1024]{1,0:T(8,128)(2,1)S(1)} %pad_maximum_fusion), channel_id=1, source_target_pairs={{0,96},{32,0},{64,32},{96,64},{1,97},{33,1},{65,33},{97,65},{2,98}... | collective-permute-start | bytes 1572872 | tf_op jit(solution)/shard_map/ppermute | solution.py:31
  18.6 1.7 %collective-permute-start.10 = (bf16[256,1024]{1,0:T(8,128)(2,1)S(1)}, bf16[256,1024]{1,0:T(8,128)(2,1)S(1)}, u32[]{:S(2)}, u32[]{:S(2)}) collective-permute-start(bf16[256,1024]{1,0:T(8,128)(2,1)S(1)} %pad_maximum_fusion), channel_id=1, source_target_pairs={{0,64},{32,96},{64,0},{96,32},{1,65},{33,97},{65,1},{97,33},{2,66}... | collective-permute-start | bytes 1572872 | tf_op jit(solution)/shard_map/ppermute | solution.py:31
  21.3 3.6 %all-to-all-start = ((bf16[4,2,896,128]{3,2,1,0:T(8,128)(2,1)}), bf16[4,2,896,128]{3,2,1,0:T(8,128)(2,1)S(1)}, u32[]{:S(2)}, u32[]{:S(2)}) async-start(bf16[4,2,896,128]{3,2,1,0:T(8,128)(2,1)} %get-tuple-element.40), calls=%async_computation | async-start | bytes 3670016 | tf_op jit(solution)/shard_map/all_to_all | solution.py:292
  26.1 14.7 %shard_map.77 = (bf16[128,3584]{1,0:T(8,128)(2,1)}, bf16[4,64,2048]{2,1,0:T(8,128)(2,1)}, bf16[64,3584]{1,0:T(8,128)(2,1)}, bf16[64,3584]{1,0:T(8,128)(2,1)}) custom-call(bf16[64,2048]{1,0:T(8,128)(2,1)} %f0.1, bf16[64,2048]{1,0:T(8,128)(2,1)} %copy-done.14, bf16[64,2048]{1,0:T(8,128)(2,1)} %collective-permute-done.5.f2, bf16[64,2048]{1,0:T(8,128)(2,1)} %copy-done.13, ...), custom_call_target="tpu_custom_call" | custom-call | flops 22548578304 | bytes 14680064 | tf_op jit(solution)/shard_map/pallas_call | solution.py:205
  41.5 1.5 %collective-permute-done.7.refs_0_ = bf16[64,3584]{1,0:T(8,128)(2,1)S(1)} collective-permute-done((bf16[64,3584]{1,0:T(8,128)(2,1)}, bf16[64,3584]{1,0:T(8,128)(2,1)S(1)}, u32[]{:S(2)}, u32[]{:S(2)}) %collective-permute-start.7) | collective-permute-done | bytes 458784 | tf_op jit(solution)/shard_map/ppermute | solution.py:31
  43.8 2.7 %shard_map.78 = bf16[128,3584]{1,0:T(8,128)(2,1)} custom-call(bf16[128,3584]{1,0:T(8,128)(2,1)} %get-tuple-element.44.keep_ref, bf16[64,3584]{1,0:T(8,128)(2,1)} %copy-done.4, bf16[64,3584]{1,0:T(8,128)(2,1)} %collective-permute-done.8.refs_1_), custom_call_target="tpu_custom_call" | custom-call | flops 262144 | bytes 262144 | tf_op jit(solution)/shard_map/pallas_call | solution.py:241
  48.2 5.1 %all-to-all-start.1 = ((bf16[4,64,2048]{2,1,0:T(8,128)(2,1)}), bf16[4,64,2048]{2,1,0:T(8,128)(2,1)S(1)}, u32[]{:S(2)}, u32[]{:S(2)}) async-start(bf16[4,64,2048]{2,1,0:T(8,128)(2,1)} %get-tuple-element.55), calls=%async_computation.1 | async-start | bytes 2097152 | tf_op jit(solution)/shard_map/all_to_all | solution.py:302
  53.3 3.3 %shard_map.79 = (bf16[112,1024]{1,0:T(8,128)(2,1)}, bf16[112,1024]{1,0:T(8,128)(2,1)}) custom-call(bf16[4,2,896,128]{3,2,1,0:T(8,128)(2,1)} %copy-done, bf16[4,2,896,128]{3,2,1,0:T(8,128)(2,1)} %collective-permute-done.12.oth_ref, bf16[4,64,1024]{2,1,0:T(8,128)(2,1)} %bitcast.6, bf16[4,64,1024]{2,1,0:T(8,128)(2,1)} %bitcast.8, ...), custom_call_target="tpu_custom_call" | custom-call | flops 1048576 | bytes 1048576 | tf_op jit(solution)/shard_map/pallas_call | solution.py:153
  56.6 1.5 %collective-permute-start.24 = (bf16[112,1024]{1,0:T(8,128)(2,1)}, bf16[112,1024]{1,0:T(8,128)(2,1)S(1)}, u32[]{:S(2)}, u32[]{:S(2)}) collective-permute-start(bf16[112,1024]{1,0:T(8,128)(2,1)} %get-tuple-element.69), channel_id=1, source_target_pairs={{0,4},{1,5},{2,6},{3,7},{4,8},{5,9},{6,10},{7,11},{8,12},{9,13},{1... | collective-permute-start | bytes 688136 | tf_op jit(solution)/shard_map/ppermute | solution.py:257
  58.1 4.0 %collective-permute-start.13 = (bf16[112,1024]{1,0:T(8,128)(2,1)}, bf16[112,1024]{1,0:T(8,128)(2,1)S(1)}, u32[]{:S(2)}, u32[]{:S(2)}) collective-permute-start(bf16[112,1024]{1,0:T(8,128)(2,1)} %get-tuple-element.54), channel_id=1, source_target_pairs={{0,28},{1,29},{2,30},{3,31},{4,0},{5,1},{6,2},{7,3},{8,4},{9,5},{1... | collective-permute-start | bytes 688136 | tf_op jit(solution)/shard_map/ppermute | solution.py:257
  62.1 7.1 %shard_map.80 = (bf16[112,1024]{1,0:T(8,128)(2,1)}, bf16[112,1024]{1,0:T(8,128)(2,1)}, bf16[112,1024]{1,0:T(8,128)(2,1)}, bf16[112,1024]{1,0:T(8,128)(2,1)}, bf1...) custom-call(bf16[4,2,896,128]{3,2,1,0:T(8,128)(2,1)} %copy-done, ...), custom_call_target="tpu_custom_call" | custom-call | flops 1048576 | bytes 1048576 | tf_op jit(solution)/shard_map/pallas_call | solution.py:153
  69.3 2.0 %collective-permute-start.21 = (bf16[112,1024]{1,0:T(8,128)(2,1)}, bf16[112,1024]{1,0:T(8,128)(2,1)S(1)}, u32[]{:S(2)}, u32[]{:S(2)}) collective-permute-start(bf16[112,1024]{1,0:T(8,128)(2,1)} %get-tuple-element.66), channel_id=1, source_target_pairs={{0,28},{1,29},{2,30},{3,31},{4,0},{5,1},{6,2},{7,3},{8,4},{9,5},{1... | collective-permute-start | bytes 688136 | tf_op jit(solution)/shard_map/ppermute | solution.py:257
  73.6 3.2 %collective-permute-start.17 = (bf16[112,1024]{1,0:T(8,128)(2,1)S(1)}, bf16[112,1024]{1,0:T(8,128)(2,1)S(1)}, u32[]{:S(2)}, u32[]{:S(2)}) collective-permute-start(bf16[112,1024]{1,0:T(8,128)(2,1)S(1)} %add.58), channel_id=1, source_target_pairs={{0,28},{1,29},{2,30},{3,31},{4,0},{5,1},{6,2},{7,3},{8,4},{9,5},{1... | collective-permute-start | bytes 688136 | tf_op jit(solution)/shard_map/ppermute | solution.py:257
  79.0 2.0 %collective-permute-start.22 = (bf16[112,1024]{1,0:T(8,128)(2,1)S(1)}, bf16[112,1024]{1,0:T(8,128)(2,1)S(1)}, u32[]{:S(2)}, u32[]{:S(2)}) collective-permute-start(bf16[112,1024]{1,0:T(8,128)(2,1)S(1)} %add.62), channel_id=1, source_target_pairs={{0,28},{1,29},{2,30},{3,31},{4,0},{5,1},{6,2},{7,3},{8,4},{9,5},{1... | collective-permute-start | bytes 688136 | tf_op jit(solution)/shard_map/ppermute | solution.py:257
  82.7 4.4 %collective-permute-done.14 = bf16[112,1024]{1,0:T(8,128)(2,1)S(1)} collective-permute-done((bf16[112,1024]{1,0:T(8,128)(2,1)}, bf16[112,1024]{1,0:T(8,128)(2,1)S(1)}, u32[]{:S(2)}, u32[]{:S(2)}) %collective-permute-start.14) | collective-permute-done | bytes 229408 | tf_op jit(solution)/shard_map/ppermute | solution.py:257
  87.3 3.3 %collective-permute-start.18 = (bf16[112,1024]{1,0:T(8,128)(2,1)S(1)}, bf16[112,1024]{1,0:T(8,128)(2,1)S(1)}, u32[]{:S(2)}, u32[]{:S(2)}) collective-permute-start(bf16[112,1024]{1,0:T(8,128)(2,1)S(1)} %add.59), channel_id=1, source_target_pairs={{0,28},{1,29},{2,30},{3,31},{4,0},{5,1},{6,2},{7,3},{8,4},{9,5},{1... | collective-permute-start | bytes 688136 | tf_op jit(solution)/shard_map/ppermute | solution.py:257
  92.8 1.9 %collective-permute-start.27 = (bf16[112,1024]{1,0:T(8,128)(2,1)}, bf16[112,1024]{1,0:T(8,128)(2,1)}, u32[]{:S(2)}, u32[]{:S(2)}) collective-permute-start(bf16[112,1024]{1,0:T(8,128)(2,1)} %add.67), channel_id=1, source_target_pairs={{0,5},{1,4},{2,7},{3,6},{4,9},{5,8},{6,11},{7,10},{8,13},{9,12},{1... | collective-permute-start | bytes 688136 | tf_op jit(solution)/shard_map/ppermute | solution.py:257
  96.3 3.3 %collective-permute-start.19 = (bf16[112,1024]{1,0:T(8,128)(2,1)S(1)}, bf16[112,1024]{1,0:T(8,128)(2,1)S(1)}, u32[]{:S(2)}, u32[]{:S(2)}) collective-permute-start(bf16[112,1024]{1,0:T(8,128)(2,1)S(1)} %add.60), channel_id=1, source_target_pairs={{0,28},{1,29},{2,30},{3,31},{4,0},{5,1},{6,2},{7,3},{8,4},{9,5},{1... | collective-permute-start | bytes 688136 | tf_op jit(solution)/shard_map/ppermute | solution.py:257
  100.4 2.0 %collective-permute-done.27 = bf16[112,1024]{1,0:T(8,128)(2,1)} collective-permute-done((bf16[112,1024]{1,0:T(8,128)(2,1)}, bf16[112,1024]{1,0:T(8,128)(2,1)}, u32[]{:S(2)}, u32[]{:S(2)}) %collective-permute-start.27) | collective-permute-done | bytes 229408 | tf_op jit(solution)/shard_map/ppermute | solution.py:257
  103.4 1.6 %collective-permute-done.16 = bf16[112,1024]{1,0:T(8,128)(2,1)S(1)} collective-permute-done((bf16[112,1024]{1,0:T(8,128)(2,1)S(1)}, bf16[112,1024]{1,0:T(8,128)(2,1)S(1)}, u32[]{:S(2)}, u32[]{:S(2)}) %collective-permute-start.16) | collective-permute-done | bytes 229408 | tf_op jit(solution)/shard_map/ppermute | solution.py:257
  (87 shorter events, 24.5 us)
Async XLA Ops:
  0.6 13.7 %collective-permute-start.3 = (bf16[64,2048]{1,0:T(8,128)(2,1)}, bf16[64,2048]{1,0:T(8,128)(2,1)S(1)}, u32[]{:S(2)}, u32[]{:S(2)}) collective-permute-start(bf16[64,2048]{1,0:T(8,128)(2,1)} %f0.1), channel_id=1, source_target_pairs={{0,32},{32,64},{64,96},{96,0},{1,33},{33,65},{65,97},{97,1},{2,34}... | collective-permute-start | bytes 786440 | tf_op jit(solution)/shard_map/ppermute | solution.py:31
  2.2 12.1 %collective-permute-start.4 = (bf16[64,2048]{1,0:T(8,128)(2,1)}, bf16[64,2048]{1,0:T(8,128)(2,1)S(1)}, u32[]{:S(2)}, u32[]{:S(2)}) collective-permute-start(bf16[64,2048]{1,0:T(8,128)(2,1)} %f0.1), channel_id=1, source_target_pairs={{0,96},{32,0},{64,32},{96,64},{1,97},{33,1},{65,33},{97,65},{2,98}... | collective-permute-start | bytes 786440 | tf_op jit(solution)/shard_map/ppermute | solution.py:31
  4.1 8.8 %collective-permute-start.2 = (bf16[64,1024]{1,0:T(8,128)(2,1)S(1)}, bf16[64,1024]{1,0:T(8,128)(2,1)S(1)}, u32[]{:S(2)}, u32[]{:S(2)}) collective-permute-start(bf16[64,1024]{1,0:T(8,128)(2,1)S(1)} %get-tuple-element.74), channel_id=1, source_target_pairs={{0,2},{1,3},{2,0},{3,1},{4,6},{5,7},{6,4},{7,5},{8,10},{9,11},{10,... | collective-permute-start | bytes 393224 | tf_op jit(solution)/shard_map/ppermute | solution.py:31
  14.3 11.8 %collective-permute-start.6 = (bf16[3584,128]{1,0:T(8,128)(2,1)}, bf16[3584,128]{1,0:T(8,128)(2,1)}, u32[]{:S(2)}, u32[]{:S(2)}) collective-permute-start(bf16[3584,128]{1,0:T(8,128)(2,1)} %get-tuple-element.43.own_ref), channel_id=1, source_target_pairs={{0,128},{128,0},{1,129},{129,1},{2,130},{130,2},{3,131},{131,3},{4... | collective-permute-start | bytes 2752520 | tf_op jit(solution)/shard_map/ppermute | solution.py:31
  15.1 11.1 %collective-permute-start.5 = (bf16[64,2048]{1,0:T(8,128)(2,1)}, bf16[64,2048]{1,0:T(8,128)(2,1)}, u32[]{:S(2)}, u32[]{:S(2)}) collective-permute-start(bf16[64,2048]{1,0:T(8,128)(2,1)} %f0.1), channel_id=1, source_target_pairs={{0,64},{32,96},{64,0},{96,32},{1,65},{33,97},{65,1},{97,33},{2,66}... | collective-permute-start | bytes 786440 | tf_op jit(solution)/shard_map/ppermute | solution.py:31
  17.2 29.3 %collective-permute-start.9 = (bf16[256,1024]{1,0:T(8,128)(2,1)S(1)}, bf16[256,1024]{1,0:T(8,128)(2,1)S(1)}, u32[]{:S(2)}, u32[]{:S(2)}) collective-permute-start(bf16[256,1024]{1,0:T(8,128)(2,1)S(1)} %pad_maximum_fusion), channel_id=1, source_target_pairs={{0,96},{32,0},{64,32},{96,64},{1,97},{33,1},{65,33},{97,65},{2,98}... | collective-permute-start | bytes 1572872 | tf_op jit(solution)/shard_map/ppermute | solution.py:31
  18.6 28.7 %collective-permute-start.10 = (bf16[256,1024]{1,0:T(8,128)(2,1)S(1)}, bf16[256,1024]{1,0:T(8,128)(2,1)S(1)}, u32[]{:S(2)}, u32[]{:S(2)}) collective-permute-start(bf16[256,1024]{1,0:T(8,128)(2,1)S(1)} %pad_maximum_fusion), channel_id=1, source_target_pairs={{0,64},{32,96},{64,0},{96,32},{1,65},{33,97},{65,1},{97,33},{2,66}... | collective-permute-start | bytes 1572872 | tf_op jit(solution)/shard_map/ppermute | solution.py:31
  20.3 27.2 %collective-permute-start.11 = (bf16[256,1024]{1,0:T(8,128)(2,1)S(1)}, bf16[256,1024]{1,0:T(8,128)(2,1)}, u32[]{:S(2)}, u32[]{:S(2)}) collective-permute-start(bf16[256,1024]{1,0:T(8,128)(2,1)S(1)} %pad_maximum_fusion), channel_id=1, source_target_pairs={{0,32},{32,64},{64,96},{96,0},{1,33},{33,65},{65,97},{97,1},{2,34}... | collective-permute-start | bytes 1572872 | tf_op jit(solution)/shard_map/ppermute | solution.py:31
  21.3 26.3 %all-to-all-start = ((bf16[4,2,896,128]{3,2,1,0:T(8,128)(2,1)}), bf16[4,2,896,128]{3,2,1,0:T(8,128)(2,1)S(1)}, u32[]{:S(2)}, u32[]{:S(2)}) async-start(bf16[4,2,896,128]{3,2,1,0:T(8,128)(2,1)} %get-tuple-element.40), calls=%async_computation | async-start | bytes 3670016 | tf_op jit(solution)/shard_map/all_to_all | solution.py:292
  48.2 24.4 %all-to-all-start.1 = ((bf16[4,64,2048]{2,1,0:T(8,128)(2,1)}), bf16[4,64,2048]{2,1,0:T(8,128)(2,1)S(1)}, u32[]{:S(2)}, u32[]{:S(2)}) async-start(bf16[4,64,2048]{2,1,0:T(8,128)(2,1)} %get-tuple-element.55), calls=%async_computation.1 | async-start | bytes 2097152 | tf_op jit(solution)/shard_map/all_to_all | solution.py:302
  56.6 14.7 %collective-permute-start.24 = (bf16[112,1024]{1,0:T(8,128)(2,1)}, bf16[112,1024]{1,0:T(8,128)(2,1)S(1)}, u32[]{:S(2)}, u32[]{:S(2)}) collective-permute-start(bf16[112,1024]{1,0:T(8,128)(2,1)} %get-tuple-element.69), channel_id=1, source_target_pairs={{0,4},{1,5},{2,6},{3,7},{4,8},{5,9},{6,10},{7,11},{8,12},{9,13},{1... | collective-permute-start | bytes 688136 | tf_op jit(solution)/shard_map/ppermute | solution.py:257
  58.1 14.5 %collective-permute-start.13 = (bf16[112,1024]{1,0:T(8,128)(2,1)}, bf16[112,1024]{1,0:T(8,128)(2,1)S(1)}, u32[]{:S(2)}, u32[]{:S(2)}) collective-permute-start(bf16[112,1024]{1,0:T(8,128)(2,1)} %get-tuple-element.54), channel_id=1, source_target_pairs={{0,28},{1,29},{2,30},{3,31},{4,0},{5,1},{6,2},{7,3},{8,4},{9,5},{1... | collective-permute-start | bytes 688136 | tf_op jit(solution)/shard_map/ppermute | solution.py:257
  69.3 8.8 %collective-permute-start.21 = (bf16[112,1024]{1,0:T(8,128)(2,1)}, bf16[112,1024]{1,0:T(8,128)(2,1)S(1)}, u32[]{:S(2)}, u32[]{:S(2)}) collective-permute-start(bf16[112,1024]{1,0:T(8,128)(2,1)} %get-tuple-element.66), channel_id=1, source_target_pairs={{0,28},{1,29},{2,30},{3,31},{4,0},{5,1},{6,2},{7,3},{8,4},{9,5},{1... | collective-permute-start | bytes 688136 | tf_op jit(solution)/shard_map/ppermute | solution.py:257
  72.3 9.8 %collective-permute-start.25 = (bf16[112,1024]{1,0:T(8,128)(2,1)S(1)}, bf16[112,1024]{1,0:T(8,128)(2,1)S(1)}, u32[]{:S(2)}, u32[]{:S(2)}) collective-permute-start(bf16[112,1024]{1,0:T(8,128)(2,1)S(1)} %add.65), channel_id=1, source_target_pairs={{0,4},{1,5},{2,6},{3,7},{4,8},{5,9},{6,10},{7,11},{8,12},{9,13},{1... | collective-permute-start | bytes 688136 | tf_op jit(solution)/shard_map/ppermute | solution.py:257
  72.4 14.6 %collective-permute-start.14 = (bf16[112,1024]{1,0:T(8,128)(2,1)}, bf16[112,1024]{1,0:T(8,128)(2,1)S(1)}, u32[]{:S(2)}, u32[]{:S(2)}) collective-permute-start(bf16[112,1024]{1,0:T(8,128)(2,1)} %get-tuple-element.58), channel_id=1, source_target_pairs={{0,4},{1,5},{2,6},{3,7},{4,8},{5,9},{6,10},{7,11},{8,12},{9,13},{1... | collective-permute-start | bytes 688136 | tf_op jit(solution)/shard_map/ppermute | solution.py:257
  73.6 13.7 %collective-permute-start.17 = (bf16[112,1024]{1,0:T(8,128)(2,1)S(1)}, bf16[112,1024]{1,0:T(8,128)(2,1)S(1)}, u32[]{:S(2)}, u32[]{:S(2)}) collective-permute-start(bf16[112,1024]{1,0:T(8,128)(2,1)S(1)} %add.58), channel_id=1, source_target_pairs={{0,28},{1,29},{2,30},{3,31},{4,0},{5,1},{6,2},{7,3},{8,4},{9,5},{1... | collective-permute-start | bytes 688136 | tf_op jit(solution)/shard_map/ppermute | solution.py:257
  79.0 11.6 %collective-permute-start.22 = (bf16[112,1024]{1,0:T(8,128)(2,1)S(1)}, bf16[112,1024]{1,0:T(8,128)(2,1)S(1)}, u32[]{:S(2)}, u32[]{:S(2)}) collective-permute-start(bf16[112,1024]{1,0:T(8,128)(2,1)S(1)} %add.62), channel_id=1, source_target_pairs={{0,28},{1,29},{2,30},{3,31},{4,0},{5,1},{6,2},{7,3},{8,4},{9,5},{1... | collective-permute-start | bytes 688136 | tf_op jit(solution)/shard_map/ppermute | solution.py:257
  82.2 9.8 %collective-permute-start.26 = (bf16[112,1024]{1,0:T(8,128)(2,1)S(1)}, bf16[112,1024]{1,0:T(8,128)(2,1)S(1)}, u32[]{:S(2)}, u32[]{:S(2)}) collective-permute-start(bf16[112,1024]{1,0:T(8,128)(2,1)S(1)} %add.66), channel_id=1, source_target_pairs={{0,4},{1,5},{2,6},{3,7},{4,8},{5,9},{6,10},{7,11},{8,12},{9,13},{1... | collective-permute-start | bytes 688136 | tf_op jit(solution)/shard_map/ppermute | solution.py:257
  82.3 17.3 %collective-permute-start.20 = (bf16[112,1024]{1,0:T(8,128)(2,1)}, bf16[112,1024]{1,0:T(8,128)(2,1)S(1)}, u32[]{:S(2)}, u32[]{:S(2)}) collective-permute-start(bf16[112,1024]{1,0:T(8,128)(2,1)} %get-tuple-element.65), channel_id=1, source_target_pairs={{0,1},{1,0},{2,3},{3,2},{4,5},{5,4},{6,7},{7,6},{8,9},{9,8},{10,11... | collective-permute-start | bytes 688136 | tf_op jit(solution)/shard_map/ppermute | solution.py:270
  87.1 8.9 %collective-permute-start.15 = (bf16[112,1024]{1,0:T(8,128)(2,1)S(1)}, bf16[112,1024]{1,0:T(8,128)(2,1)S(1)}, u32[]{:S(2)}, u32[]{:S(2)}) collective-permute-start(bf16[112,1024]{1,0:T(8,128)(2,1)S(1)} %add.55), channel_id=1, source_target_pairs={{0,4},{1,5},{2,6},{3,7},{4,8},{5,9},{6,10},{7,11},{8,12},{9,13},{1... | collective-permute-start | bytes 688136 | tf_op jit(solution)/shard_map/ppermute | solution.py:257
  87.3 8.9 %collective-permute-start.18 = (bf16[112,1024]{1,0:T(8,128)(2,1)S(1)}, bf16[112,1024]{1,0:T(8,128)(2,1)S(1)}, u32[]{:S(2)}, u32[]{:S(2)}) collective-permute-start(bf16[112,1024]{1,0:T(8,128)(2,1)S(1)} %add.59), channel_id=1, source_target_pairs={{0,28},{1,29},{2,30},{3,31},{4,0},{5,1},{6,2},{7,3},{8,4},{9,5},{1... | collective-permute-start | bytes 688136 | tf_op jit(solution)/shard_map/ppermute | solution.py:257
  90.7 9.7 %collective-permute-start.23 = (bf16[112,1024]{1,0:T(8,128)(2,1)S(1)}, bf16[112,1024]{1,0:T(8,128)(2,1)S(1)}, u32[]{:S(2)}, u32[]{:S(2)}) collective-permute-start(bf16[112,1024]{1,0:T(8,128)(2,1)S(1)} %add.63), channel_id=1, source_target_pairs={{0,29},{1,28},{2,31},{3,30},{4,1},{5,0},{6,3},{7,2},{8,5},{9,4},{1... | collective-permute-start | bytes 688136 | tf_op jit(solution)/shard_map/ppermute | solution.py:257
  92.8 9.6 %collective-permute-start.27 = (bf16[112,1024]{1,0:T(8,128)(2,1)}, bf16[112,1024]{1,0:T(8,128)(2,1)}, u32[]{:S(2)}, u32[]{:S(2)}) collective-permute-start(bf16[112,1024]{1,0:T(8,128)(2,1)} %add.67), channel_id=1, source_target_pairs={{0,5},{1,4},{2,7},{3,6},{4,9},{5,8},{6,11},{7,10},{8,13},{9,12},{1... | collective-permute-start | bytes 688136 | tf_op jit(solution)/shard_map/ppermute | solution.py:257
  96.1 8.9 %collective-permute-start.16 = (bf16[112,1024]{1,0:T(8,128)(2,1)S(1)}, bf16[112,1024]{1,0:T(8,128)(2,1)S(1)}, u32[]{:S(2)}, u32[]{:S(2)}) collective-permute-start(bf16[112,1024]{1,0:T(8,128)(2,1)S(1)} %add.56), channel_id=1, source_target_pairs={{0,4},{1,5},{2,6},{3,7},{4,8},{5,9},{6,10},{7,11},{8,12},{9,13},{1... | collective-permute-start | bytes 688136 | tf_op jit(solution)/shard_map/ppermute | solution.py:257
  (21 other events, 170.0 us)

commit v5 on v4

--- a/solution.py
+++ b/solution.py
@@ -29,6 +29,16 @@
 def send(value, axis, step):
     n = SIZES[axis]
     return lax.ppermute(value, axis, [(i, (i + step) % n) for i in range(n)])
+
+
+def trade(value, axis, near):
+    pairs = [(i, i ^ 1 if near else (i + 2) % 4 ^ 1) for i in range(4)]
+    return lax.ppermute(value, axis, pairs)
+
+
+def neighbours(index):
+    across = lax.rem(index + 2, 4)
+    return index, index ^ 1, across, across ^ 1
 
 
 def together(*values):
@@ -79,10 +89,9 @@
 def copy_acts(blocks, acts, sems):
     x, r, y = (lax.axis_index(name) for name in ("col", "row", "y"))
     copies = []
-    for d, block in enumerate(blocks):
-        at = lax.rem(x + d, 4)
-        for j, turn in enumerate((0, 3, 1, 2)):
-            to = acts.at[(at // 2) ^ r, lax.rem(y + turn, 4), lax.rem(at, 2)]
+    for at, block in zip(neighbours(x), blocks):
+        for j, at_y in enumerate(neighbours(y)):
+            to = acts.at[(at // 2) ^ r, at_y, lax.rem(at, 2)]
             copies.append(pltpu.make_async_copy(block.at[j], to, sems.at[len(copies)]))
     return copies
 
@@ -90,9 +99,10 @@
 def first_kernel(wanted, own_ref, oth_ref, b0, b1, b2, b3, *rest):
     outs, (acts, lhs, sems) = rest[:-3], rest[-3:]
     z = lax.axis_index("z")
+    turn = 1 - 2 * lax.rem(z, 2)
     copies = copy_acts((b0, b1, b2, b3), acts, sems)
     for i, (which, offset) in enumerate(wanted):
-        rows = pl.ds(pl.multiple_of(lax.rem(z + offset, 8) * 112, 16), 112)
+        rows = pl.ds(pl.multiple_of(lax.rem(z + turn * offset + 8, 8) * 112, 16), 112)
         for h, ref in enumerate((own_ref, oth_ref)):
             to = lhs.at[pl.ds(h * 4, 4), pl.ds(i * 112, 112), :]
             sem = sems.at[len(copies)]
@@ -110,6 +120,7 @@
 def rest_kernel(wanted, own_ref, oth_ref, b0, b1, b2, b3, *rest):
     outs, (acts, lhs, done, sems) = rest[:-4], rest[-4:]
     z = lax.axis_index("z")
+    turn = 1 - 2 * lax.rem(z, 2)
     copies = copy_acts((b0, b1, b2, b3), acts, sems)
     for which in range(2):
         for h, ref in enumerate((own_ref, oth_ref)):
@@ -127,7 +138,7 @@
         mine = [(i, offset) for i, (w, offset) in enumerate(wanted) if w == which]
         pieces = []
         for _, offset in mine:
-            rows = pl.ds(pl.multiple_of(lax.rem(z + offset, 8) * 112, 16), 112)
+            rows = pl.ds(pl.multiple_of(lax.rem(z + turn * offset + 8, 8) * 112, 16), 112)
             pieces.append(jnp.concatenate([lhs[which, k, rows, :] for k in range(8)], axis=1))
         both = jnp.concatenate(pieces, axis=0)
         part = jnp.dot(both, acts[...].reshape(1024, 1024), preferred_element_type=F32)
@@ -169,8 +180,7 @@
 
     @pl.when(step == 0)
     def _():
-        for d, ref in enumerate((f0, f1, f2, f3)):
-            at = lax.rem(x + d, 4)
+        for at, ref in zip(neighbours(x), (f0, f1, f2, f3)):
             row = ((at // 2) ^ r) * 128 + lax.rem(at, 2) * 64
             rows_ref[pl.ds(pl.multiple_of(row, 64), 64), :] = ref[...]
 
@@ -249,45 +259,49 @@
     )(keep, *got)
 
 
-def send_z(value, step, swap=False):
+def trade_z(value, near, swap=False):
     pairs = []
     for k in range(8):
+        to = k ^ 1 if near else ((k + 1) ^ 1) - 1
         for y in range(4):
-            pairs.append((k * 4 + y, (k + step) % 8 * 4 + (y ^ 1 if swap else y)))
+            pairs.append((k * 4 + y, to % 8 * 4 + (y ^ 1 if swap else y)))
     return lax.ppermute(value, ("z", "y"), pairs)
 
 
-def reduce_z(piece, step, swap, late=None):
-    far, near = piece[4], piece[-3 * step % 8]
+def reduce_z(piece, near_first, swap, late=None):
+    side = 1 if near_first else -1
+    far, near = piece[4], piece[3 * side % 8]
     for hop in (3, 2, 1):
-        far = send_z(far, step)
+        by = near_first == (hop != 2)
+        far = trade_z(far, by)
         if hop == 3 and late is not None:
             far, late = together(far, late)
-        near = send_z(near, -step, swap and hop == 1)
-        far = far + piece[hop * step % 8]
+        near = trade_z(near, by, swap and hop == 1)
+        side = -side
+        far = far + piece[hop * side % 8]
         if hop > 1:
-            near = near + piece[-(hop - 1) * step % 8]
+            near = near + piece[(hop - 1) * side % 8]
     own = lax.ppermute(piece[0], "y", [(k, k ^ 1) for k in range(4)]) if swap else piece[0]
-    far = send_z(far, step, swap)
-    return own.astype(F32) + near.astype(F32) + far.astype(F32), late
+    far = trade_z(far, not near_first, swap)
+    return (own, near, far), late
 
 
 def on_device(act_forward, weight, act_backward, pre_backward, grad_backward):
     r, x, z, y = (lax.axis_index(name) for name in ("row", "col", "z", "y"))
     ym = y % 2
 
-    left, right = send(act_forward, "col", 1), send(act_forward, "col", -1)
+    left, right = trade(act_forward, "col", False), trade(act_forward, "col", True)
 
     same = lax.dynamic_slice(act_backward, (0, ym * 1024), (64, 1024))
     other = lax.dynamic_slice(act_backward, (0, (1 - ym) * 1024), (64, 1024))
     acts = jnp.concatenate(
-        [same, send(other, "y", 1), send(other, "y", -1), send(same, "y", 2)], axis=0
+        [same, trade(other, "y", True), send(same, "y", 2), trade(other, "y", False)], axis=0
     )
     flipped, halves = grad_pre_flipped(pre_backward, grad_backward)
 
     acts, halves, flipped, left, right = together(acts, halves, flipped, left, right)
     far = send(act_forward, "col", 2)
-    b1, b2, b3 = send(acts, "col", -1), send(acts, "col", 2), send(acts, "col", 1)
+    b1, b2, b3 = trade(acts, "col", True), send(acts, "col", 2), trade(acts, "col", False)
     flipped_other = send(flipped, "row", 1)
     grads_own = lax.all_to_all(halves, "y", 0, 0)
     keep, packed, *gives = both_products(
@@ -309,12 +323,12 @@
         )
         parts.update(zip(wanted, got))
     given, kept = ([parts[w, o] for o in range(8)] for w in range(2))
-    got, _ = reduce_z(given, 1, True)
-    kept, packed = reduce_z(kept, -1, False, packed)
+    got, _ = reduce_z(given, True, True)
+    kept, packed = reduce_z(kept, False, False, packed)
     grad_inputs = packed.astype(F32).sum(axis=0).astype(BF)
-    grad_weight = jnp.where(
-        ym == 0, jnp.concatenate([kept, got], axis=1), jnp.concatenate([got, kept], axis=1)
-    ).T
+    low = sum(jnp.where(ym == 0, a, b).astype(F32) for a, b in zip(kept, got))
+    high = sum(jnp.where(ym == 0, b, a).astype(F32) for a, b in zip(kept, got))
+    grad_weight = jnp.concatenate([low, high], axis=1).T
     return hidden_forward, grad_inputs, grad_weight
 
 

time: 107 us -> 106 us (level)
  waiting for transfers between devices: 18.7 us -> 24.4 us
  starting transfers between devices: 45.3 us -> 40.3 us
  other arithmetic: 7.17 us -> 5.59 us
    ppermute x13 -> x7, starting transfers between devices: 14.3 us -> 3.24 us  [send(): return lax.ppermute(value, axis, [(i, (i + step) % n) for i in range(n)])]
    ppermute x14 -> x20, starting transfers between devices: 22 us -> 29.1 us  [the longest x14 19.9 us: trade_z(): return lax.ppermute(value, ('z', 'y'), pairs)]
    ppermute x14 -> x20, waiting for transfers between devices: 12.7 us -> 15.6 us  [the longest x14 15.4 us: trade_z(): return lax.ppermute(value, ('z', 'y'), pairs)]
    ppermute x13 -> x7, waiting for transfers between devices: 5.98 us -> 8.78 us  [send(): return lax.ppermute(value, axis, [(i, (i + step) % n) for i in range(n)])]
    add x12 -> x11, other arithmetic: 5.18 us -> 3.64 us  [the longest x6 2.23 us: reduce_z(): far = far + piece[hop * side % 8]]
    all_to_all x1, starting transfers between devices: 5.07 us -> 3.86 us  [on_device(): packed = lax.all_to_all(packed, 'col', 0, 0)]
  transfers between devices with their start and end apart: 30 -> 30, of which waited for: 15 -> 14; matrix products, arithmetic and copies ran while one was open for 7% -> 5% of each run, Pallas kernels for 30% -> 30%
where the time goes in v5:
time: 106 us; the launch traced here: 105 us
  starting transfers between devices  40.3 us (38%)
  Pallas kernels  31.7 us (30%)
  waiting for transfers between devices  24.4 us (23%)
  other arithmetic  5.59 us (5%)
  local copies, waits for them, and re-layouts  2.37 us (2%)
    ppermute x14, starting transfers between devices, trade_z(): return lax.ppermute(value, ('z', 'y'), pairs)  19.9 us
    ppermute x14, waiting for transfers between devices, trade_z(): return lax.ppermute(value, ('z', 'y'), pairs)  15.4 us
    pallas_call x1, Pallas kernels, both_products(): pl.pallas_call(both_kernel, grid=(hidden // tile,), in_specs=[pl.BlockSpe...  14.7 us
    pallas_call x2, Pallas kernels, weight_parts(): pl.pallas_call(functools.partial(first_kernel if first else rest_kernel,...  10.5 us
    ppermute x6, starting transfers between devices, trade(): return lax.ppermute(value, axis, pairs)  9.19 us
    ppermute x7, waiting for transfers between devices, send(): return lax.ppermute(value, axis, [(i, (i + step) % n) for i in range(n)])  8.78 us
    all_to_all x1, starting transfers between devices, on_device(): packed = lax.all_to_all(packed, 'col', 0, 0)  3.86 us
    pallas_call x1, Pallas kernels, grad_pre_flipped(): pl.pallas_call(grad_kernel, grid=(cols // tile,), in_specs=[pl.BlockSpec(...  3.77 us
  transfers between devices with their start and end apart: 30, of which 14 were waited for; matrix products, arithmetic and copies ran while one was open for 5% of the time, Pallas kernels for 30%

profile of v5, /device:TPU:2, one launch (start us, length us, event | category | flops | bytes accessed | tf_op | source)
XLA Modules:
  0.0 105.4 jit_solution(8629716829222092656)
XLA Ops:
  0.6 1.6 %collective-permute-start.3 = (bf16[64,2048]{1,0:T(8,128)(2,1)}, bf16[64,2048]{1,0:T(8,128)(2,1)S(1)}, u32[]{:S(2)}, u32[]{:S(2)}) collective-permute-start(bf16[64,2048]{1,0:T(8,128)(2,1)} %f0.1), channel_id=1, source_target_pairs={{0,96},{32,64},{64,32},{96,0},{1,97},{33,65},{65,33},{97,1},{2,98}... | collective-permute-start | bytes 786440 | tf_op jit(solution)/shard_map/ppermute | solution.py:36
  2.2 1.8 %collective-permute-start.4 = (bf16[64,2048]{1,0:T(8,128)(2,1)}, bf16[64,2048]{1,0:T(8,128)(2,1)S(1)}, u32[]{:S(2)}, u32[]{:S(2)}) collective-permute-start(bf16[64,2048]{1,0:T(8,128)(2,1)} %f0.1), channel_id=1, source_target_pairs={{0,32},{32,0},{64,96},{96,64},{1,33},{33,1},{65,97},{97,65},{2,34}... | collective-permute-start | bytes 786440 | tf_op jit(solution)/shard_map/ppermute | solution.py:36
  5.0 3.1 %collective-permute-start.2 = (bf16[64,1024]{1,0:T(8,128)(2,1)S(1)}, bf16[64,1024]{1,0:T(8,128)(2,1)S(1)}, u32[]{:S(2)}, u32[]{:S(2)}) collective-permute-start(bf16[64,1024]{1,0:T(8,128)(2,1)S(1)} %get-tuple-element.76), channel_id=1, source_target_pairs={{0,3},{1,2},{2,1},{3,0},{4,7},{5,6},{6,5},{7,4},{8,11},{9,10},{10,... | collective-permute-start | bytes 393224 | tf_op jit(solution)/shard_map/ppermute | solution.py:36
  9.2 3.8 %shard_map.76 = (bf16[3584,128]{1,0:T(8,128)(2,1)}, bf16[4,2,896,128]{3,2,1,0:T(8,128)(2,1)}) custom-call(bf16[128,3584]{1,0:T(8,128)(2,1)} %pre_ref.1, bf16[128,3584]{1,0:T(8,128)(2,1)} %grad_ref.1), custom_call_target="tpu_custom_call" | custom-call | flops 13762560 | bytes 4587520 | tf_op jit(solution)/shard_map/pallas_call | solution.py:70
  13.1 2.3 %collective-permute-done.1 = bf16[64,1024]{1,0:T(8,128)(2,1)S(1)} collective-permute-done((bf16[64,1024]{1,0:T(8,128)(2,1)S(1)}, bf16[64,1024]{1,0:T(8,128)(2,1)S(1)}, u32[]{:S(2)}, u32[]{:S(2)}) %collective-permute-start.1) | collective-permute-done | bytes 131104 | tf_op jit(solution)/shard_map/ppermute | solution.py:31
  16.5 1.7 %collective-permute-start.9 = (bf16[256,1024]{1,0:T(8,128)(2,1)S(1)}, bf16[256,1024]{1,0:T(8,128)(2,1)S(1)}, u32[]{:S(2)}, u32[]{:S(2)}) collective-permute-start(bf16[256,1024]{1,0:T(8,128)(2,1)S(1)} %pad_maximum_fusion), channel_id=1, source_target_pairs={{0,32},{32,0},{64,96},{96,64},{1,33},{33,1},{65,97},{97,65},{2,34}... | collective-permute-start | bytes 1572872 | tf_op jit(solution)/shard_map/ppermute | solution.py:36
  18.2 1.6 %collective-permute-start.10 = (bf16[256,1024]{1,0:T(8,128)(2,1)S(1)}, bf16[256,1024]{1,0:T(8,128)(2,1)S(1)}, u32[]{:S(2)}, u32[]{:S(2)}) collective-permute-start(bf16[256,1024]{1,0:T(8,128)(2,1)S(1)} %pad_maximum_fusion), channel_id=1, source_target_pairs={{0,64},{32,96},{64,0},{96,32},{1,65},{33,97},{65,1},{97,33},{2,66}... | collective-permute-start | bytes 1572872 | tf_op jit(solution)/shard_map/ppermute | solution.py:31
  20.4 3.6 %all-to-all-start = ((bf16[4,2,896,128]{3,2,1,0:T(8,128)(2,1)}), bf16[4,2,896,128]{3,2,1,0:T(8,128)(2,1)S(1)}, u32[]{:S(2)}, u32[]{:S(2)}) async-start(bf16[4,2,896,128]{3,2,1,0:T(8,128)(2,1)} %get-tuple-element.40), calls=%async_computation | async-start | bytes 3670016 | tf_op jit(solution)/shard_map/all_to_all | solution.py:306
  24.0 3.4 %collective-permute-done.5.f2 = bf16[64,2048]{1,0:T(8,128)(2,1)} collective-permute-done((bf16[64,2048]{1,0:T(8,128)(2,1)}, bf16[64,2048]{1,0:T(8,128)(2,1)}, u32[]{:S(2)}, u32[]{:S(2)}) %collective-permute-start.5) | collective-permute-done | bytes 262176 | tf_op jit(solution)/shard_map/ppermute | solution.py:31
  27.3 14.7 %shard_map.77 = (bf16[128,3584]{1,0:T(8,128)(2,1)}, bf16[4,64,2048]{2,1,0:T(8,128)(2,1)}, bf16[64,3584]{1,0:T(8,128)(2,1)}, bf16[64,3584]{1,0:T(8,128)(2,1)}) custom-call(bf16[64,2048]{1,0:T(8,128)(2,1)} %f0.1, bf16[64,2048]{1,0:T(8,128)(2,1)} %copy-done.14, bf16[64,2048]{1,0:T(8,128)(2,1)} %collective-permute-done.5.f2, bf16[64,2048]{1,0:T(8,128)(2,1)} %copy-done.13, ...), custom_call_target="tpu_custom_call" | custom-call | flops 22548578304 | bytes 14680064 | tf_op jit(solution)/shard_map/pallas_call | solution.py:215
  42.7 1.5 %collective-permute-done.7.refs_0_ = bf16[64,3584]{1,0:T(8,128)(2,1)S(1)} collective-permute-done((bf16[64,3584]{1,0:T(8,128)(2,1)}, bf16[64,3584]{1,0:T(8,128)(2,1)S(1)}, u32[]{:S(2)}, u32[]{:S(2)}) %collective-permute-start.7) | collective-permute-done | bytes 458784 | tf_op jit(solution)/shard_map/ppermute | solution.py:31
  45.0 2.7 %shard_map.78 = bf16[128,3584]{1,0:T(8,128)(2,1)} custom-call(bf16[128,3584]{1,0:T(8,128)(2,1)} %get-tuple-element.44.keep_ref, bf16[64,3584]{1,0:T(8,128)(2,1)} %copy-done.4, bf16[64,3584]{1,0:T(8,128)(2,1)} %collective-permute-done.8.refs_1_), custom_call_target="tpu_custom_call" | custom-call | flops 262144 | bytes 262144 | tf_op jit(solution)/shard_map/pallas_call | solution.py:251
  49.4 3.9 %all-to-all-start.1 = ((bf16[4,64,2048]{2,1,0:T(8,128)(2,1)}), bf16[4,64,2048]{2,1,0:T(8,128)(2,1)S(1)}, u32[]{:S(2)}, u32[]{:S(2)}) async-start(bf16[4,64,2048]{2,1,0:T(8,128)(2,1)} %get-tuple-element.55), calls=%async_computation.1 | async-start | bytes 2097152 | tf_op jit(solution)/shard_map/all_to_all | solution.py:316
  53.2 3.3 %shard_map.79 = (bf16[112,1024]{1,0:T(8,128)(2,1)}, bf16[112,1024]{1,0:T(8,128)(2,1)}) custom-call(bf16[4,2,896,128]{3,2,1,0:T(8,128)(2,1)} %copy-done, bf16[4,2,896,128]{3,2,1,0:T(8,128)(2,1)} %collective-permute-done.12.oth_ref, bf16[4,64,1024]{2,1,0:T(8,128)(2,1)} %bitcast.6, bf16[4,64,1024]{2,1,0:T(8,128)(2,1)} %bitcast.8, ...), custom_call_target="tpu_custom_call" | custom-call | flops 1048576 | bytes 1048576 | tf_op jit(solution)/shard_map/pallas_call | solution.py:164
  56.6 5.9 %collective-permute-start.13 = (bf16[112,1024]{1,0:T(8,128)(2,1)}, bf16[112,1024]{1,0:T(8,128)(2,1)S(1)}, u32[]{:S(2)}, u32[]{:S(2)}) collective-permute-start(bf16[112,1024]{1,0:T(8,128)(2,1)} %get-tuple-element.54), channel_id=1, source_target_pairs={{0,28},{1,29},{2,30},{3,31},{4,8},{5,9},{6,10},{7,11},{8,4},{9,5},... | collective-permute-start | bytes 688136 | tf_op jit(solution)/shard_map/ppermute | solution.py:268
  62.5 7.1 %shard_map.80 = (bf16[112,1024]{1,0:T(8,128)(2,1)}, bf16[112,1024]{1,0:T(8,128)(2,1)}, bf16[112,1024]{1,0:T(8,128)(2,1)}, bf16[112,1024]{1,0:T(8,128)(2,1)}, bf1...) custom-call(bf16[4,2,896,128]{3,2,1,0:T(8,128)(2,1)} %copy-done, ...), custom_call_target="tpu_custom_call" | custom-call | flops 1048576 | bytes 1048576 | tf_op jit(solution)/shard_map/pallas_call | solution.py:164
  69.7 2.1 %collective-permute-start.15 = (bf16[112,1024]{1,0:T(8,128)(2,1)}, bf16[112,1024]{1,0:T(8,128)(2,1)S(1)}, u32[]{:S(2)}, u32[]{:S(2)}) collective-permute-start(bf16[112,1024]{1,0:T(8,128)(2,1)} %get-tuple-element.59), channel_id=1, source_target_pairs={{0,28},{1,29},{2,30},{3,31},{4,8},{5,9},{6,10},{7,11},{8,4},{9,5},... | collective-permute-start | bytes 688136 | tf_op jit(solution)/shard_map/ppermute | solution.py:268
  81.9 3.5 %collective-permute-done.21 = bf16[112,1024]{1,0:T(8,128)(2,1)S(1)} collective-permute-done((bf16[112,1024]{1,0:T(8,128)(2,1)S(1)}, bf16[112,1024]{1,0:T(8,128)(2,1)S(1)}, u32[]{:S(2)}, u32[]{:S(2)}) %collective-permute-start.21) | collective-permute-done | bytes 229408 | tf_op jit(solution)/shard_map/ppermute | solution.py:268
  88.4 2.0 %collective-permute-done.16 = bf16[112,1024]{1,0:T(8,128)(2,1)S(1)} collective-permute-done((bf16[112,1024]{1,0:T(8,128)(2,1)S(1)}, bf16[112,1024]{1,0:T(8,128)(2,1)S(1)}, u32[]{:S(2)}, u32[]{:S(2)}) %collective-permute-start.16) | collective-permute-done | bytes 229408 | tf_op jit(solution)/shard_map/ppermute | solution.py:268
  92.7 2.8 %collective-permute-done.22 = bf16[112,1024]{1,0:T(8,128)(2,1)S(1)} collective-permute-done((bf16[112,1024]{1,0:T(8,128)(2,1)S(1)}, bf16[112,1024]{1,0:T(8,128)(2,1)S(1)}, u32[]{:S(2)}, u32[]{:S(2)}) %collective-permute-start.22) | collective-permute-done | bytes 229408 | tf_op jit(solution)/shard_map/ppermute | solution.py:268
  95.7 1.4 %collective-permute-start.27 = (bf16[112,1024]{1,0:T(8,128)(2,1)S(1)}, bf16[112,1024]{1,0:T(8,128)(2,1)S(1)}, u32[]{:S(2)}, u32[]{:S(2)}) collective-permute-start(bf16[112,1024]{1,0:T(8,128)(2,1)S(1)} %add.65), channel_id=1, source_target_pairs={{0,29},{1,28},{2,31},{3,30},{4,9},{5,8},{6,11},{7,10},{8,5},{9,4},... | collective-permute-start | bytes 688136 | tf_op jit(solution)/shard_map/ppermute | solution.py:268
  98.1 1.8 %collective-permute-done.17 = bf16[112,1024]{1,0:T(8,128)(2,1)S(1)} collective-permute-done((bf16[112,1024]{1,0:T(8,128)(2,1)S(1)}, bf16[112,1024]{1,0:T(8,128)(2,1)S(1)}, u32[]{:S(2)}, u32[]{:S(2)}) %collective-permute-start.17) | collective-permute-done | bytes 229408 | tf_op jit(solution)/shard_map/ppermute | solution.py:268
  100.0 1.7 %collective-permute-done.20 = bf16[112,1024]{1,0:T(8,128)(2,1)S(1)} collective-permute-done((bf16[112,1024]{1,0:T(8,128)(2,1)S(1)}, bf16[112,1024]{1,0:T(8,128)(2,1)S(1)}, u32[]{:S(2)}, u32[]{:S(2)}) %collective-permute-start.20) | collective-permute-done | bytes 229408 | tf_op jit(solution)/shard_map/ppermute | solution.py:268
  101.7 1.5 %collective-permute-done.23 = bf16[112,1024]{1,0:T(8,128)(2,1)S(1)} collective-permute-done((bf16[112,1024]{1,0:T(8,128)(2,1)S(1)}, bf16[112,1024]{1,0:T(8,128)(2,1)S(1)}, u32[]{:S(2)}, u32[]{:S(2)}) %collective-permute-start.23) | collective-permute-done | bytes 229408 | tf_op jit(solution)/shard_map/ppermute | solution.py:268
  (86 shorter events, 25.4 us)
Async XLA Ops:
  0.6 14.8 %collective-permute-start.3 = (bf16[64,2048]{1,0:T(8,128)(2,1)}, bf16[64,2048]{1,0:T(8,128)(2,1)S(1)}, u32[]{:S(2)}, u32[]{:S(2)}) collective-permute-start(bf16[64,2048]{1,0:T(8,128)(2,1)} %f0.1), channel_id=1, source_target_pairs={{0,96},{32,64},{64,32},{96,0},{1,97},{33,65},{65,33},{97,1},{2,98}... | collective-permute-start | bytes 786440 | tf_op jit(solution)/shard_map/ppermute | solution.py:36
  2.2 13.3 %collective-permute-start.4 = (bf16[64,2048]{1,0:T(8,128)(2,1)}, bf16[64,2048]{1,0:T(8,128)(2,1)S(1)}, u32[]{:S(2)}, u32[]{:S(2)}) collective-permute-start(bf16[64,2048]{1,0:T(8,128)(2,1)} %f0.1), channel_id=1, source_target_pairs={{0,32},{32,0},{64,96},{96,64},{1,33},{33,1},{65,97},{97,65},{2,34}... | collective-permute-start | bytes 786440 | tf_op jit(solution)/shard_map/ppermute | solution.py:36
  5.0 8.1 %collective-permute-start.2 = (bf16[64,1024]{1,0:T(8,128)(2,1)S(1)}, bf16[64,1024]{1,0:T(8,128)(2,1)S(1)}, u32[]{:S(2)}, u32[]{:S(2)}) collective-permute-start(bf16[64,1024]{1,0:T(8,128)(2,1)S(1)} %get-tuple-element.76), channel_id=1, source_target_pairs={{0,3},{1,2},{2,1},{3,0},{4,7},{5,6},{6,5},{7,4},{8,11},{9,10},{10,... | collective-permute-start | bytes 393224 | tf_op jit(solution)/shard_map/ppermute | solution.py:36
  15.5 11.8 %collective-permute-start.6 = (bf16[3584,128]{1,0:T(8,128)(2,1)}, bf16[3584,128]{1,0:T(8,128)(2,1)}, u32[]{:S(2)}, u32[]{:S(2)}) collective-permute-start(bf16[3584,128]{1,0:T(8,128)(2,1)} %get-tuple-element.43.own_ref), channel_id=1, source_target_pairs={{0,128},{128,0},{1,129},{129,1},{2,130},{130,2},{3,131},{131,3},{4... | collective-permute-start | bytes 2752520 | tf_op jit(solution)/shard_map/ppermute | solution.py:31
  16.3 11.1 %collective-permute-start.5 = (bf16[64,2048]{1,0:T(8,128)(2,1)}, bf16[64,2048]{1,0:T(8,128)(2,1)}, u32[]{:S(2)}, u32[]{:S(2)}) collective-permute-start(bf16[64,2048]{1,0:T(8,128)(2,1)} %f0.1), channel_id=1, source_target_pairs={{0,64},{32,96},{64,0},{96,32},{1,65},{33,97},{65,1},{97,33},{2,66}... | collective-permute-start | bytes 786440 | tf_op jit(solution)/shard_map/ppermute | solution.py:31
  16.5 31.2 %collective-permute-start.9 = (bf16[256,1024]{1,0:T(8,128)(2,1)S(1)}, bf16[256,1024]{1,0:T(8,128)(2,1)S(1)}, u32[]{:S(2)}, u32[]{:S(2)}) collective-permute-start(bf16[256,1024]{1,0:T(8,128)(2,1)S(1)} %pad_maximum_fusion), channel_id=1, source_target_pairs={{0,32},{32,0},{64,96},{96,64},{1,33},{33,1},{65,97},{97,65},{2,34}... | collective-permute-start | bytes 1572872 | tf_op jit(solution)/shard_map/ppermute | solution.py:36
  18.2 30.4 %collective-permute-start.10 = (bf16[256,1024]{1,0:T(8,128)(2,1)S(1)}, bf16[256,1024]{1,0:T(8,128)(2,1)S(1)}, u32[]{:S(2)}, u32[]{:S(2)}) collective-permute-start(bf16[256,1024]{1,0:T(8,128)(2,1)S(1)} %pad_maximum_fusion), channel_id=1, source_target_pairs={{0,64},{32,96},{64,0},{96,32},{1,65},{33,97},{65,1},{97,33},{2,66}... | collective-permute-start | bytes 1572872 | tf_op jit(solution)/shard_map/ppermute | solution.py:31
  19.8 28.8 %collective-permute-start.11 = (bf16[256,1024]{1,0:T(8,128)(2,1)S(1)}, bf16[256,1024]{1,0:T(8,128)(2,1)}, u32[]{:S(2)}, u32[]{:S(2)}) collective-permute-start(bf16[256,1024]{1,0:T(8,128)(2,1)S(1)} %pad_maximum_fusion), channel_id=1, source_target_pairs={{0,96},{32,64},{64,32},{96,0},{1,97},{33,65},{65,33},{97,1},{2,98}... | collective-permute-start | bytes 1572872 | tf_op jit(solution)/shard_map/ppermute | solution.py:36
  20.4 28.2 %all-to-all-start = ((bf16[4,2,896,128]{3,2,1,0:T(8,128)(2,1)}), bf16[4,2,896,128]{3,2,1,0:T(8,128)(2,1)S(1)}, u32[]{:S(2)}, u32[]{:S(2)}) async-start(bf16[4,2,896,128]{3,2,1,0:T(8,128)(2,1)} %get-tuple-element.40), calls=%async_computation | async-start | bytes 3670016 | tf_op jit(solution)/shard_map/all_to_all | solution.py:306
  49.4 23.5 %all-to-all-start.1 = ((bf16[4,64,2048]{2,1,0:T(8,128)(2,1)}), bf16[4,64,2048]{2,1,0:T(8,128)(2,1)S(1)}, u32[]{:S(2)}, u32[]{:S(2)}) async-start(bf16[4,64,2048]{2,1,0:T(8,128)(2,1)} %get-tuple-element.55), calls=%async_computation.1 | async-start | bytes 2097152 | tf_op jit(solution)/shard_map/all_to_all | solution.py:316
  56.6 16.2 %collective-permute-start.13 = (bf16[112,1024]{1,0:T(8,128)(2,1)}, bf16[112,1024]{1,0:T(8,128)(2,1)S(1)}, u32[]{:S(2)}, u32[]{:S(2)}) collective-permute-start(bf16[112,1024]{1,0:T(8,128)(2,1)} %get-tuple-element.54), channel_id=1, source_target_pairs={{0,28},{1,29},{2,30},{3,31},{4,8},{5,9},{6,10},{7,11},{8,4},{9,5},... | collective-permute-start | bytes 688136 | tf_op jit(solution)/shard_map/ppermute | solution.py:268
  62.5 12.4 %collective-permute-start.24 = (bf16[112,1024]{1,0:T(8,128)(2,1)}, bf16[112,1024]{1,0:T(8,128)(2,1)S(1)}, u32[]{:S(2)}, u32[]{:S(2)}) collective-permute-start(bf16[112,1024]{1,0:T(8,128)(2,1)} %get-tuple-element.69), channel_id=1, source_target_pairs={{0,4},{1,5},{2,6},{3,7},{4,0},{5,1},{6,2},{7,3},{8,12},{9,13},{10,... | collective-permute-start | bytes 688136 | tf_op jit(solution)/shard_map/ppermute | solution.py:268
  69.7 8.7 %collective-permute-start.15 = (bf16[112,1024]{1,0:T(8,128)(2,1)}, bf16[112,1024]{1,0:T(8,128)(2,1)S(1)}, u32[]{:S(2)}, u32[]{:S(2)}) collective-permute-start(bf16[112,1024]{1,0:T(8,128)(2,1)} %get-tuple-element.59), channel_id=1, source_target_pairs={{0,28},{1,29},{2,30},{3,31},{4,8},{5,9},{6,10},{7,11},{8,4},{9,5},... | collective-permute-start | bytes 688136 | tf_op jit(solution)/shard_map/ppermute | solution.py:268
  71.8 8.9 %collective-permute-start.18 = (bf16[112,1024]{1,0:T(8,128)(2,1)}, bf16[112,1024]{1,0:T(8,128)(2,1)S(1)}, u32[]{:S(2)}, u32[]{:S(2)}) collective-permute-start(bf16[112,1024]{1,0:T(8,128)(2,1)} %get-tuple-element.62), channel_id=1, source_target_pairs={{0,4},{1,5},{2,6},{3,7},{4,0},{5,1},{6,2},{7,3},{8,12},{9,13},{10,... | collective-permute-start | bytes 688136 | tf_op jit(solution)/shard_map/ppermute | solution.py:268
  73.8 11.7 %collective-permute-start.21 = (bf16[112,1024]{1,0:T(8,128)(2,1)S(1)}, bf16[112,1024]{1,0:T(8,128)(2,1)S(1)}, u32[]{:S(2)}, u32[]{:S(2)}) collective-permute-start(bf16[112,1024]{1,0:T(8,128)(2,1)S(1)} %add.60), channel_id=1, source_target_pairs={{0,4},{1,5},{2,6},{3,7},{4,0},{5,1},{6,2},{7,3},{8,12},{9,13},{10,... | collective-permute-start | bytes 688136 | tf_op jit(solution)/shard_map/ppermute | solution.py:268
  76.0 10.9 %collective-permute-start.25 = (bf16[112,1024]{1,0:T(8,128)(2,1)S(1)}, bf16[112,1024]{1,0:T(8,128)(2,1)S(1)}, u32[]{:S(2)}, u32[]{:S(2)}) collective-permute-start(bf16[112,1024]{1,0:T(8,128)(2,1)S(1)} %add.63), channel_id=1, source_target_pairs={{0,28},{1,29},{2,30},{3,31},{4,8},{5,9},{6,10},{7,11},{8,4},{9,5},... | collective-permute-start | bytes 688136 | tf_op jit(solution)/shard_map/ppermute | solution.py:268
  79.4 11.0 %collective-permute-start.16 = (bf16[112,1024]{1,0:T(8,128)(2,1)S(1)}, bf16[112,1024]{1,0:T(8,128)(2,1)S(1)}, u32[]{:S(2)}, u32[]{:S(2)}) collective-permute-start(bf16[112,1024]{1,0:T(8,128)(2,1)S(1)} %add.55), channel_id=1, source_target_pairs={{0,4},{1,5},{2,6},{3,7},{4,0},{5,1},{6,2},{7,3},{8,12},{9,13},{10,... | collective-permute-start | bytes 688136 | tf_op jit(solution)/shard_map/ppermute | solution.py:268
  80.7 11.0 %collective-permute-start.19 = (bf16[112,1024]{1,0:T(8,128)(2,1)S(1)}, bf16[112,1024]{1,0:T(8,128)(2,1)S(1)}, u32[]{:S(2)}, u32[]{:S(2)}) collective-permute-start(bf16[112,1024]{1,0:T(8,128)(2,1)S(1)} %add.57), channel_id=1, source_target_pairs={{0,28},{1,29},{2,30},{3,31},{4,8},{5,9},{6,10},{7,11},{8,4},{9,5},... | collective-permute-start | bytes 688136 | tf_op jit(solution)/shard_map/ppermute | solution.py:268
  85.5 9.9 %collective-permute-start.22 = (bf16[112,1024]{1,0:T(8,128)(2,1)S(1)}, bf16[112,1024]{1,0:T(8,128)(2,1)S(1)}, u32[]{:S(2)}, u32[]{:S(2)}) collective-permute-start(bf16[112,1024]{1,0:T(8,128)(2,1)S(1)} %add.61), channel_id=1, source_target_pairs={{0,28},{1,29},{2,30},{3,31},{4,8},{5,9},{6,10},{7,11},{8,4},{9,5},... | collective-permute-start | bytes 688136 | tf_op jit(solution)/shard_map/ppermute | solution.py:268
  86.9 8.7 %collective-permute-start.26 = (bf16[112,1024]{1,0:T(8,128)(2,1)S(1)}, bf16[112,1024]{1,0:T(8,128)(2,1)S(1)}, u32[]{:S(2)}, u32[]{:S(2)}) collective-permute-start(bf16[112,1024]{1,0:T(8,128)(2,1)S(1)} %add.64), channel_id=1, source_target_pairs={{0,4},{1,5},{2,6},{3,7},{4,0},{5,1},{6,2},{7,3},{8,12},{9,13},{10,... | collective-permute-start | bytes 688136 | tf_op jit(solution)/shard_map/ppermute | solution.py:268
  87.8 10.3 %collective-permute-start.14 = (bf16[112,1024]{1,0:T(8,128)(2,1)}, bf16[112,1024]{1,0:T(8,128)(2,1)S(1)}, u32[]{:S(2)}, u32[]{:S(2)}) collective-permute-start(bf16[112,1024]{1,0:T(8,128)(2,1)} %get-tuple-element.58), channel_id=1, source_target_pairs={{0,1},{1,0},{2,3},{3,2},{4,5},{5,4},{6,7},{7,6},{8,9},{9,8},{10,11... | collective-permute-start | bytes 688136 | tf_op jit(solution)/shard_map/ppermute | solution.py:284
  90.5 9.5 %collective-permute-start.17 = (bf16[112,1024]{1,0:T(8,128)(2,1)S(1)}, bf16[112,1024]{1,0:T(8,128)(2,1)S(1)}, u32[]{:S(2)}, u32[]{:S(2)}) collective-permute-start(bf16[112,1024]{1,0:T(8,128)(2,1)S(1)} %add.56), channel_id=1, source_target_pairs={{0,28},{1,29},{2,30},{3,31},{4,8},{5,9},{6,10},{7,11},{8,4},{9,5},... | collective-permute-start | bytes 688136 | tf_op jit(solution)/shard_map/ppermute | solution.py:268
  91.8 9.8 %collective-permute-start.20 = (bf16[112,1024]{1,0:T(8,128)(2,1)S(1)}, bf16[112,1024]{1,0:T(8,128)(2,1)S(1)}, u32[]{:S(2)}, u32[]{:S(2)}) collective-permute-start(bf16[112,1024]{1,0:T(8,128)(2,1)S(1)} %add.58), channel_id=1, source_target_pairs={{0,5},{1,4},{2,7},{3,6},{4,1},{5,0},{6,3},{7,2},{8,13},{9,12},{10,... | collective-permute-start | bytes 688136 | tf_op jit(solution)/shard_map/ppermute | solution.py:268
  95.7 8.4 %collective-permute-start.27 = (bf16[112,1024]{1,0:T(8,128)(2,1)S(1)}, bf16[112,1024]{1,0:T(8,128)(2,1)S(1)}, u32[]{:S(2)}, u32[]{:S(2)}) collective-permute-start(bf16[112,1024]{1,0:T(8,128)(2,1)S(1)} %add.65), channel_id=1, source_target_pairs={{0,29},{1,28},{2,31},{3,30},{4,9},{5,8},{6,11},{7,10},{8,5},{9,4},... | collective-permute-start | bytes 688136 | tf_op jit(solution)/shard_map/ppermute | solution.py:268
  (21 other events, 170.7 us)

commit v6 on v5

--- a/solution.py
+++ b/solution.py
@@ -315,7 +315,7 @@
     grads_other = send(grads_own, "row", 1)
     packed = lax.all_to_all(packed, "col", 0, 0)
     parts = {}
-    first = [(0, 4), (1, 4)]
+    first = [(0, 4), (1, 4), (0, 3), (1, 5)]
     others = [(w, o) for w in range(2) for o in range(8) if (w, o) not in first]
     for wanted in (first, others):
         got = weight_parts(

time: 106 us -> 106 us (level)
  starting transfers between devices: 40.3 us -> 38.7 us
  waiting for transfers between devices: 24.4 us -> 25.6 us
    ppermute x14, starting transfers between devices: 19.9 us -> 18.2 us  [trade_z(): return lax.ppermute(value, ('z', 'y'), pairs)]
    ppermute x14, waiting for transfers between devices: 15.4 us -> 16.6 us  [trade_z(): return lax.ppermute(value, ('z', 'y'), pairs)]
where the time goes in v6:
time: 106 us; the launch traced here: 105 us
  starting transfers between devices  38.7 us (37%)
  Pallas kernels  31.9 us (30%)
  waiting for transfers between devices  25.6 us (24%)
  other arithmetic  5.66 us (5%)
  local copies, waits for them, and re-layouts  2.37 us (2%)
    ppermute x14, starting transfers between devices, trade_z(): return lax.ppermute(value, ('z', 'y'), pairs)  18.2 us
    ppermute x14, waiting for transfers between devices, trade_z(): return lax.ppermute(value, ('z', 'y'), pairs)  16.6 us
    pallas_call x1, Pallas kernels, both_products(): pl.pallas_call(both_kernel, grid=(hidden // tile,), in_specs=[pl.BlockSpe...  14.7 us
    pallas_call x2, Pallas kernels, weight_parts(): pl.pallas_call(functools.partial(first_kernel if first else rest_kernel,...  10.7 us
    ppermute x6, starting transfers between devices, trade(): return lax.ppermute(value, axis, pairs)  9.19 us
    ppermute x7, waiting for transfers between devices, send(): return lax.ppermute(value, axis, [(i, (i + step) % n) for i in range(n)])  8.78 us
    all_to_all x1, starting transfers between devices, on_device(): packed = lax.all_to_all(packed, 'col', 0, 0)  3.86 us
    pallas_call x1, Pallas kernels, grad_pre_flipped(): pl.pallas_call(grad_kernel, grid=(cols // tile,), in_specs=[pl.BlockSpec(...  3.77 us
  transfers between devices with their start and end apart: 30, of which 14 were waited for; matrix products, arithmetic and copies ran while one was open for 5% of the time, Pallas kernels for 30%

profile of v6, /device:TPU:2, one launch (start us, length us, event | category | flops | bytes accessed | tf_op | source)
XLA Modules:
  0.0 105.2 jit_solution(12979631461159320844)
XLA Ops:
  0.6 1.6 %collective-permute-start.3 = (bf16[64,2048]{1,0:T(8,128)(2,1)}, bf16[64,2048]{1,0:T(8,128)(2,1)S(1)}, u32[]{:S(2)}, u32[]{:S(2)}) collective-permute-start(bf16[64,2048]{1,0:T(8,128)(2,1)} %f0.1), channel_id=1, source_target_pairs={{0,96},{32,64},{64,32},{96,0},{1,97},{33,65},{65,33},{97,1},{2,98}... | collective-permute-start | bytes 786440 | tf_op jit(solution)/shard_map/ppermute | solution.py:36
  2.2 1.8 %collective-permute-start.4 = (bf16[64,2048]{1,0:T(8,128)(2,1)}, bf16[64,2048]{1,0:T(8,128)(2,1)S(1)}, u32[]{:S(2)}, u32[]{:S(2)}) collective-permute-start(bf16[64,2048]{1,0:T(8,128)(2,1)} %f0.1), channel_id=1, source_target_pairs={{0,32},{32,0},{64,96},{96,64},{1,33},{33,1},{65,97},{97,65},{2,34}... | collective-permute-start | bytes 786440 | tf_op jit(solution)/shard_map/ppermute | solution.py:36
  5.0 3.1 %collective-permute-start.2 = (bf16[64,1024]{1,0:T(8,128)(2,1)S(1)}, bf16[64,1024]{1,0:T(8,128)(2,1)S(1)}, u32[]{:S(2)}, u32[]{:S(2)}) collective-permute-start(bf16[64,1024]{1,0:T(8,128)(2,1)S(1)} %get-tuple-element.76), channel_id=1, source_target_pairs={{0,3},{1,2},{2,1},{3,0},{4,7},{5,6},{6,5},{7,4},{8,11},{9,10},{10,... | collective-permute-start | bytes 393224 | tf_op jit(solution)/shard_map/ppermute | solution.py:36
  9.2 3.8 %shard_map.76 = (bf16[3584,128]{1,0:T(8,128)(2,1)}, bf16[4,2,896,128]{3,2,1,0:T(8,128)(2,1)}) custom-call(bf16[128,3584]{1,0:T(8,128)(2,1)} %pre_ref.1, bf16[128,3584]{1,0:T(8,128)(2,1)} %grad_ref.1), custom_call_target="tpu_custom_call" | custom-call | flops 13762560 | bytes 4587520 | tf_op jit(solution)/shard_map/pallas_call | solution.py:70
  13.1 2.3 %collective-permute-done.1 = bf16[64,1024]{1,0:T(8,128)(2,1)S(1)} collective-permute-done((bf16[64,1024]{1,0:T(8,128)(2,1)S(1)}, bf16[64,1024]{1,0:T(8,128)(2,1)S(1)}, u32[]{:S(2)}, u32[]{:S(2)}) %collective-permute-start.1) | collective-permute-done | bytes 131104 | tf_op jit(solution)/shard_map/ppermute | solution.py:31
  16.5 1.7 %collective-permute-start.9 = (bf16[256,1024]{1,0:T(8,128)(2,1)S(1)}, bf16[256,1024]{1,0:T(8,128)(2,1)S(1)}, u32[]{:S(2)}, u32[]{:S(2)}) collective-permute-start(bf16[256,1024]{1,0:T(8,128)(2,1)S(1)} %pad_maximum_fusion), channel_id=1, source_target_pairs={{0,32},{32,0},{64,96},{96,64},{1,33},{33,1},{65,97},{97,65},{2,34}... | collective-permute-start | bytes 1572872 | tf_op jit(solution)/shard_map/ppermute | solution.py:36
  18.2 1.6 %collective-permute-start.10 = (bf16[256,1024]{1,0:T(8,128)(2,1)S(1)}, bf16[256,1024]{1,0:T(8,128)(2,1)S(1)}, u32[]{:S(2)}, u32[]{:S(2)}) collective-permute-start(bf16[256,1024]{1,0:T(8,128)(2,1)S(1)} %pad_maximum_fusion), channel_id=1, source_target_pairs={{0,64},{32,96},{64,0},{96,32},{1,65},{33,97},{65,1},{97,33},{2,66}... | collective-permute-start | bytes 1572872 | tf_op jit(solution)/shard_map/ppermute | solution.py:31
  20.4 3.6 %all-to-all-start = ((bf16[4,2,896,128]{3,2,1,0:T(8,128)(2,1)}), bf16[4,2,896,128]{3,2,1,0:T(8,128)(2,1)S(1)}, u32[]{:S(2)}, u32[]{:S(2)}) async-start(bf16[4,2,896,128]{3,2,1,0:T(8,128)(2,1)} %get-tuple-element.40), calls=%async_computation | async-start | bytes 3670016 | tf_op jit(solution)/shard_map/all_to_all | solution.py:306
  24.0 3.4 %collective-permute-done.5.f2 = bf16[64,2048]{1,0:T(8,128)(2,1)} collective-permute-done((bf16[64,2048]{1,0:T(8,128)(2,1)}, bf16[64,2048]{1,0:T(8,128)(2,1)}, u32[]{:S(2)}, u32[]{:S(2)}) %collective-permute-start.5) | collective-permute-done | bytes 262176 | tf_op jit(solution)/shard_map/ppermute | solution.py:31
  27.3 14.7 %shard_map.77 = (bf16[128,3584]{1,0:T(8,128)(2,1)}, bf16[4,64,2048]{2,1,0:T(8,128)(2,1)}, bf16[64,3584]{1,0:T(8,128)(2,1)}, bf16[64,3584]{1,0:T(8,128)(2,1)}) custom-call(bf16[64,2048]{1,0:T(8,128)(2,1)} %f0.1, bf16[64,2048]{1,0:T(8,128)(2,1)} %copy-done.14, bf16[64,2048]{1,0:T(8,128)(2,1)} %collective-permute-done.5.f2, bf16[64,2048]{1,0:T(8,128)(2,1)} %copy-done.13, ...), custom_call_target="tpu_custom_call" | custom-call | flops 22548578304 | bytes 14680064 | tf_op jit(solution)/shard_map/pallas_call | solution.py:215
  42.7 1.5 %collective-permute-done.7.refs_0_ = bf16[64,3584]{1,0:T(8,128)(2,1)S(1)} collective-permute-done((bf16[64,3584]{1,0:T(8,128)(2,1)}, bf16[64,3584]{1,0:T(8,128)(2,1)S(1)}, u32[]{:S(2)}, u32[]{:S(2)}) %collective-permute-start.7) | collective-permute-done | bytes 458784 | tf_op jit(solution)/shard_map/ppermute | solution.py:31
  45.0 2.7 %shard_map.78 = bf16[128,3584]{1,0:T(8,128)(2,1)} custom-call(bf16[128,3584]{1,0:T(8,128)(2,1)} %get-tuple-element.44.keep_ref, bf16[64,3584]{1,0:T(8,128)(2,1)} %copy-done.4, bf16[64,3584]{1,0:T(8,128)(2,1)} %collective-permute-done.8.refs_1_), custom_call_target="tpu_custom_call" | custom-call | flops 262144 | bytes 262144 | tf_op jit(solution)/shard_map/pallas_call | solution.py:251
  49.4 3.9 %all-to-all-start.1 = ((bf16[4,64,2048]{2,1,0:T(8,128)(2,1)}), bf16[4,64,2048]{2,1,0:T(8,128)(2,1)S(1)}, u32[]{:S(2)}, u32[]{:S(2)}) async-start(bf16[4,64,2048]{2,1,0:T(8,128)(2,1)} %get-tuple-element.55), calls=%async_computation.1 | async-start | bytes 2097152 | tf_op jit(solution)/shard_map/all_to_all | solution.py:316
  53.2 4.1 %shard_map.79 = (bf16[112,1024]{1,0:T(8,128)(2,1)}, bf16[112,1024]{1,0:T(8,128)(2,1)}, bf16[112,1024]{1,0:T(8,128)(2,1)}, bf16[112,1024]{1,0:T(8,128)(2,1)}) custom-call(bf16[4,2,896,128]{3,2,1,0:T(8,128)(2,1)} %copy-done, bf16[4,2,896,128]{3,2,1,0:T(8,128)(2,1)} %collective-permute-done.12.oth_ref, bf16[4,64,1024]{2,1,0:T(8,128)(2,1)} %bitcast.6, ...), custom_call_target="tpu_custom_call" | custom-call | flops 1048576 | bytes 1048576 | tf_op jit(solution)/shard_map/pallas_call | solution.py:164
  57.3 5.9 %collective-permute-start.13 = (bf16[112,1024]{1,0:T(8,128)(2,1)}, bf16[112,1024]{1,0:T(8,128)(2,1)S(1)}, u32[]{:S(2)}, u32[]{:S(2)}) collective-permute-start(bf16[112,1024]{1,0:T(8,128)(2,1)} %get-tuple-element.54), channel_id=1, source_target_pairs={{0,28},{1,29},{2,30},{3,31},{4,8},{5,9},{6,10},{7,11},{8,4},{9,5},... | collective-permute-start | bytes 688136 | tf_op jit(solution)/shard_map/ppermute | solution.py:268
  63.3 2.0 %collective-permute-start.15 = (bf16[112,1024]{1,0:T(8,128)(2,1)}, bf16[112,1024]{1,0:T(8,128)(2,1)S(1)}, u32[]{:S(2)}, u32[]{:S(2)}) collective-permute-start(bf16[112,1024]{1,0:T(8,128)(2,1)} %get-tuple-element.59), channel_id=1, source_target_pairs={{0,28},{1,29},{2,30},{3,31},{4,8},{5,9},{6,10},{7,11},{8,4},{9,5},... | collective-permute-start | bytes 688136 | tf_op jit(solution)/shard_map/ppermute | solution.py:268
  66.3 6.6 %shard_map.80 = (bf16[112,1024]{1,0:T(8,128)(2,1)}, bf16[112,1024]{1,0:T(8,128)(2,1)}, bf16[112,1024]{1,0:T(8,128)(2,1)}, bf16[112,1024]{1,0:T(8,128)(2,1)}, bf1...) custom-call(bf16[4,2,896,128]{3,2,1,0:T(8,128)(2,1)} %copy-done, ...), custom_call_target="tpu_custom_call" | custom-call | flops 1048576 | bytes 1048576 | tf_op jit(solution)/shard_map/pallas_call | solution.py:164
  81.2 1.7 %collective-permute-start.22 = (bf16[112,1024]{1,0:T(8,128)(2,1)S(1)}, bf16[112,1024]{1,0:T(8,128)(2,1)S(1)}, u32[]{:S(2)}, u32[]{:S(2)}) collective-permute-start(bf16[112,1024]{1,0:T(8,128)(2,1)S(1)} %add.61), channel_id=1, source_target_pairs={{0,28},{1,29},{2,30},{3,31},{4,8},{5,9},{6,10},{7,11},{8,4},{9,5},... | collective-permute-start | bytes 688136 | tf_op jit(solution)/shard_map/ppermute | solution.py:268
  82.9 2.7 %collective-permute-done.25 = bf16[112,1024]{1,0:T(8,128)(2,1)S(1)} collective-permute-done((bf16[112,1024]{1,0:T(8,128)(2,1)S(1)}, bf16[112,1024]{1,0:T(8,128)(2,1)S(1)}, u32[]{:S(2)}, u32[]{:S(2)}) %collective-permute-start.25) | collective-permute-done | bytes 229408 | tf_op jit(solution)/shard_map/ppermute | solution.py:268
  88.2 2.4 %collective-permute-done.19 = bf16[112,1024]{1,0:T(8,128)(2,1)S(1)} collective-permute-done((bf16[112,1024]{1,0:T(8,128)(2,1)S(1)}, bf16[112,1024]{1,0:T(8,128)(2,1)S(1)}, u32[]{:S(2)}, u32[]{:S(2)}) %collective-permute-start.19) | collective-permute-done | bytes 229408 | tf_op jit(solution)/shard_map/ppermute | solution.py:268
  90.7 4.7 %collective-permute-done.22 = bf16[112,1024]{1,0:T(8,128)(2,1)S(1)} collective-permute-done((bf16[112,1024]{1,0:T(8,128)(2,1)S(1)}, bf16[112,1024]{1,0:T(8,128)(2,1)S(1)}, u32[]{:S(2)}, u32[]{:S(2)}) %collective-permute-start.22) | collective-permute-done | bytes 229408 | tf_op jit(solution)/shard_map/ppermute | solution.py:268
  95.7 1.6 %collective-permute-start.27 = (bf16[112,1024]{1,0:T(8,128)(2,1)S(1)}, bf16[112,1024]{1,0:T(8,128)(2,1)S(1)}, u32[]{:S(2)}, u32[]{:S(2)}) collective-permute-start(bf16[112,1024]{1,0:T(8,128)(2,1)S(1)} %add.65), channel_id=1, source_target_pairs={{0,29},{1,28},{2,31},{3,30},{4,9},{5,8},{6,11},{7,10},{8,5},{9,4},... | collective-permute-start | bytes 688136 | tf_op jit(solution)/shard_map/ppermute | solution.py:268
  98.3 2.1 %collective-permute-done.17 = bf16[112,1024]{1,0:T(8,128)(2,1)S(1)} collective-permute-done((bf16[112,1024]{1,0:T(8,128)(2,1)S(1)}, bf16[112,1024]{1,0:T(8,128)(2,1)S(1)}, u32[]{:S(2)}, u32[]{:S(2)}) %collective-permute-start.17) | collective-permute-done | bytes 229408 | tf_op jit(solution)/shard_map/ppermute | solution.py:268
  101.7 2.3 %collective-permute-done.27 = bf16[112,1024]{1,0:T(8,128)(2,1)S(1)} collective-permute-done((bf16[112,1024]{1,0:T(8,128)(2,1)S(1)}, bf16[112,1024]{1,0:T(8,128)(2,1)S(1)}, u32[]{:S(2)}, u32[]{:S(2)}) %collective-permute-start.27) | collective-permute-done | bytes 229408 | tf_op jit(solution)/shard_map/ppermute | solution.py:268
  (86 shorter events, 22.3 us)
Async XLA Ops:
  0.6 14.8 %collective-permute-start.3 = (bf16[64,2048]{1,0:T(8,128)(2,1)}, bf16[64,2048]{1,0:T(8,128)(2,1)S(1)}, u32[]{:S(2)}, u32[]{:S(2)}) collective-permute-start(bf16[64,2048]{1,0:T(8,128)(2,1)} %f0.1), channel_id=1, source_target_pairs={{0,96},{32,64},{64,32},{96,0},{1,97},{33,65},{65,33},{97,1},{2,98}... | collective-permute-start | bytes 786440 | tf_op jit(solution)/shard_map/ppermute | solution.py:36
  2.2 13.3 %collective-permute-start.4 = (bf16[64,2048]{1,0:T(8,128)(2,1)}, bf16[64,2048]{1,0:T(8,128)(2,1)S(1)}, u32[]{:S(2)}, u32[]{:S(2)}) collective-permute-start(bf16[64,2048]{1,0:T(8,128)(2,1)} %f0.1), channel_id=1, source_target_pairs={{0,32},{32,0},{64,96},{96,64},{1,33},{33,1},{65,97},{97,65},{2,34}... | collective-permute-start | bytes 786440 | tf_op jit(solution)/shard_map/ppermute | solution.py:36
  5.0 8.1 %collective-permute-start.2 = (bf16[64,1024]{1,0:T(8,128)(2,1)S(1)}, bf16[64,1024]{1,0:T(8,128)(2,1)S(1)}, u32[]{:S(2)}, u32[]{:S(2)}) collective-permute-start(bf16[64,1024]{1,0:T(8,128)(2,1)S(1)} %get-tuple-element.76), channel_id=1, source_target_pairs={{0,3},{1,2},{2,1},{3,0},{4,7},{5,6},{6,5},{7,4},{8,11},{9,10},{10,... | collective-permute-start | bytes 393224 | tf_op jit(solution)/shard_map/ppermute | solution.py:36
  8.1 7.3 %collective-permute-start.1 = (bf16[64,1024]{1,0:T(8,128)(2,1)S(1)}, bf16[64,1024]{1,0:T(8,128)(2,1)S(1)}, u32[]{:S(2)}, u32[]{:S(2)}) collective-permute-start(bf16[64,1024]{1,0:T(8,128)(2,1)S(1)} %get-tuple-element.75), channel_id=1, source_target_pairs={{0,2},{1,3},{2,0},{3,1},{4,6},{5,7},{6,4},{7,5},{8,10},{9,11},{10,... | collective-permute-start | bytes 393224 | tf_op jit(solution)/shard_map/ppermute | solution.py:31
  15.5 11.8 %collective-permute-start.6 = (bf16[3584,128]{1,0:T(8,128)(2,1)}, bf16[3584,128]{1,0:T(8,128)(2,1)}, u32[]{:S(2)}, u32[]{:S(2)}) collective-permute-start(bf16[3584,128]{1,0:T(8,128)(2,1)} %get-tuple-element.43.own_ref), channel_id=1, source_target_pairs={{0,128},{128,0},{1,129},{129,1},{2,130},{130,2},{3,131},{131,3},{4... | collective-permute-start | bytes 2752520 | tf_op jit(solution)/shard_map/ppermute | solution.py:31
  16.3 11.1 %collective-permute-start.5 = (bf16[64,2048]{1,0:T(8,128)(2,1)}, bf16[64,2048]{1,0:T(8,128)(2,1)}, u32[]{:S(2)}, u32[]{:S(2)}) collective-permute-start(bf16[64,2048]{1,0:T(8,128)(2,1)} %f0.1), channel_id=1, source_target_pairs={{0,64},{32,96},{64,0},{96,32},{1,65},{33,97},{65,1},{97,33},{2,66}... | collective-permute-start | bytes 786440 | tf_op jit(solution)/shard_map/ppermute | solution.py:31
  16.5 31.2 %collective-permute-start.9 = (bf16[256,1024]{1,0:T(8,128)(2,1)S(1)}, bf16[256,1024]{1,0:T(8,128)(2,1)S(1)}, u32[]{:S(2)}, u32[]{:S(2)}) collective-permute-start(bf16[256,1024]{1,0:T(8,128)(2,1)S(1)} %pad_maximum_fusion), channel_id=1, source_target_pairs={{0,32},{32,0},{64,96},{96,64},{1,33},{33,1},{65,97},{97,65},{2,34}... | collective-permute-start | bytes 1572872 | tf_op jit(solution)/shard_map/ppermute | solution.py:36
  18.2 30.4 %collective-permute-start.10 = (bf16[256,1024]{1,0:T(8,128)(2,1)S(1)}, bf16[256,1024]{1,0:T(8,128)(2,1)S(1)}, u32[]{:S(2)}, u32[]{:S(2)}) collective-permute-start(bf16[256,1024]{1,0:T(8,128)(2,1)S(1)} %pad_maximum_fusion), channel_id=1, source_target_pairs={{0,64},{32,96},{64,0},{96,32},{1,65},{33,97},{65,1},{97,33},{2,66}... | collective-permute-start | bytes 1572872 | tf_op jit(solution)/shard_map/ppermute | solution.py:31
  19.8 28.8 %collective-permute-start.11 = (bf16[256,1024]{1,0:T(8,128)(2,1)S(1)}, bf16[256,1024]{1,0:T(8,128)(2,1)}, u32[]{:S(2)}, u32[]{:S(2)}) collective-permute-start(bf16[256,1024]{1,0:T(8,128)(2,1)S(1)} %pad_maximum_fusion), channel_id=1, source_target_pairs={{0,96},{32,64},{64,32},{96,0},{1,97},{33,65},{65,33},{97,1},{2,98}... | collective-permute-start | bytes 1572872 | tf_op jit(solution)/shard_map/ppermute | solution.py:36
  20.4 28.2 %all-to-all-start = ((bf16[4,2,896,128]{3,2,1,0:T(8,128)(2,1)}), bf16[4,2,896,128]{3,2,1,0:T(8,128)(2,1)S(1)}, u32[]{:S(2)}, u32[]{:S(2)}) async-start(bf16[4,2,896,128]{3,2,1,0:T(8,128)(2,1)} %get-tuple-element.40), calls=%async_computation | async-start | bytes 3670016 | tf_op jit(solution)/shard_map/all_to_all | solution.py:306
  49.4 23.6 %all-to-all-start.1 = ((bf16[4,64,2048]{2,1,0:T(8,128)(2,1)}), bf16[4,64,2048]{2,1,0:T(8,128)(2,1)S(1)}, u32[]{:S(2)}, u32[]{:S(2)}) async-start(bf16[4,64,2048]{2,1,0:T(8,128)(2,1)} %get-tuple-element.55), calls=%async_computation.1 | async-start | bytes 2097152 | tf_op jit(solution)/shard_map/all_to_all | solution.py:316
  57.3 15.6 %collective-permute-start.13 = (bf16[112,1024]{1,0:T(8,128)(2,1)}, bf16[112,1024]{1,0:T(8,128)(2,1)S(1)}, u32[]{:S(2)}, u32[]{:S(2)}) collective-permute-start(bf16[112,1024]{1,0:T(8,128)(2,1)} %get-tuple-element.54), channel_id=1, source_target_pairs={{0,28},{1,29},{2,30},{3,31},{4,8},{5,9},{6,10},{7,11},{8,4},{9,5},... | collective-permute-start | bytes 688136 | tf_op jit(solution)/shard_map/ppermute | solution.py:268
  63.3 11.9 %collective-permute-start.24 = (bf16[112,1024]{1,0:T(8,128)(2,1)}, bf16[112,1024]{1,0:T(8,128)(2,1)S(1)}, u32[]{:S(2)}, u32[]{:S(2)}) collective-permute-start(bf16[112,1024]{1,0:T(8,128)(2,1)} %get-tuple-element.69), channel_id=1, source_target_pairs={{0,4},{1,5},{2,6},{3,7},{4,0},{5,1},{6,2},{7,3},{8,12},{9,13},{10,... | collective-permute-start | bytes 688136 | tf_op jit(solution)/shard_map/ppermute | solution.py:268
  63.3 14.2 %collective-permute-start.15 = (bf16[112,1024]{1,0:T(8,128)(2,1)}, bf16[112,1024]{1,0:T(8,128)(2,1)S(1)}, u32[]{:S(2)}, u32[]{:S(2)}) collective-permute-start(bf16[112,1024]{1,0:T(8,128)(2,1)} %get-tuple-element.59), channel_id=1, source_target_pairs={{0,28},{1,29},{2,30},{3,31},{4,8},{5,9},{6,10},{7,11},{8,4},{9,5},... | collective-permute-start | bytes 688136 | tf_op jit(solution)/shard_map/ppermute | solution.py:268
  65.3 14.1 %collective-permute-start.18 = (bf16[112,1024]{1,0:T(8,128)(2,1)}, bf16[112,1024]{1,0:T(8,128)(2,1)S(1)}, u32[]{:S(2)}, u32[]{:S(2)}) collective-permute-start(bf16[112,1024]{1,0:T(8,128)(2,1)} %get-tuple-element.62), channel_id=1, source_target_pairs={{0,4},{1,5},{2,6},{3,7},{4,0},{5,1},{6,2},{7,3},{8,12},{9,13},{10,... | collective-permute-start | bytes 688136 | tf_op jit(solution)/shard_map/ppermute | solution.py:268
  76.1 9.5 %collective-permute-start.25 = (bf16[112,1024]{1,0:T(8,128)(2,1)S(1)}, bf16[112,1024]{1,0:T(8,128)(2,1)S(1)}, u32[]{:S(2)}, u32[]{:S(2)}) collective-permute-start(bf16[112,1024]{1,0:T(8,128)(2,1)S(1)} %add.63), channel_id=1, source_target_pairs={{0,28},{1,29},{2,30},{3,31},{4,8},{5,9},{6,10},{7,11},{8,4},{9,5},... | collective-permute-start | bytes 688136 | tf_op jit(solution)/shard_map/ppermute | solution.py:268
  78.5 8.6 %collective-permute-start.16 = (bf16[112,1024]{1,0:T(8,128)(2,1)S(1)}, bf16[112,1024]{1,0:T(8,128)(2,1)S(1)}, u32[]{:S(2)}, u32[]{:S(2)}) collective-permute-start(bf16[112,1024]{1,0:T(8,128)(2,1)S(1)} %add.55), channel_id=1, source_target_pairs={{0,4},{1,5},{2,6},{3,7},{4,0},{5,1},{6,2},{7,3},{8,12},{9,13},{10,... | collective-permute-start | bytes 688136 | tf_op jit(solution)/shard_map/ppermute | solution.py:268
  79.5 11.1 %collective-permute-start.19 = (bf16[112,1024]{1,0:T(8,128)(2,1)S(1)}, bf16[112,1024]{1,0:T(8,128)(2,1)S(1)}, u32[]{:S(2)}, u32[]{:S(2)}) collective-permute-start(bf16[112,1024]{1,0:T(8,128)(2,1)S(1)} %add.57), channel_id=1, source_target_pairs={{0,28},{1,29},{2,30},{3,31},{4,8},{5,9},{6,10},{7,11},{8,4},{9,5},... | collective-permute-start | bytes 688136 | tf_op jit(solution)/shard_map/ppermute | solution.py:268
  81.2 14.3 %collective-permute-start.22 = (bf16[112,1024]{1,0:T(8,128)(2,1)S(1)}, bf16[112,1024]{1,0:T(8,128)(2,1)S(1)}, u32[]{:S(2)}, u32[]{:S(2)}) collective-permute-start(bf16[112,1024]{1,0:T(8,128)(2,1)S(1)} %add.61), channel_id=1, source_target_pairs={{0,28},{1,29},{2,30},{3,31},{4,8},{5,9},{6,10},{7,11},{8,4},{9,5},... | collective-permute-start | bytes 688136 | tf_op jit(solution)/shard_map/ppermute | solution.py:268
  85.7 9.9 %collective-permute-start.26 = (bf16[112,1024]{1,0:T(8,128)(2,1)S(1)}, bf16[112,1024]{1,0:T(8,128)(2,1)S(1)}, u32[]{:S(2)}, u32[]{:S(2)}) collective-permute-start(bf16[112,1024]{1,0:T(8,128)(2,1)S(1)} %add.64), channel_id=1, source_target_pairs={{0,4},{1,5},{2,6},{3,7},{4,0},{5,1},{6,2},{7,3},{8,12},{9,13},{10,... | collective-permute-start | bytes 688136 | tf_op jit(solution)/shard_map/ppermute | solution.py:268
  85.8 12.4 %collective-permute-start.14 = (bf16[112,1024]{1,0:T(8,128)(2,1)}, bf16[112,1024]{1,0:T(8,128)(2,1)S(1)}, u32[]{:S(2)}, u32[]{:S(2)}) collective-permute-start(bf16[112,1024]{1,0:T(8,128)(2,1)} %get-tuple-element.58), channel_id=1, source_target_pairs={{0,1},{1,0},{2,3},{3,2},{4,5},{5,4},{6,7},{7,6},{8,9},{9,8},{10,11... | collective-permute-start | bytes 688136 | tf_op jit(solution)/shard_map/ppermute | solution.py:284
  87.2 13.2 %collective-permute-start.17 = (bf16[112,1024]{1,0:T(8,128)(2,1)S(1)}, bf16[112,1024]{1,0:T(8,128)(2,1)S(1)}, u32[]{:S(2)}, u32[]{:S(2)}) collective-permute-start(bf16[112,1024]{1,0:T(8,128)(2,1)S(1)} %add.56), channel_id=1, source_target_pairs={{0,28},{1,29},{2,30},{3,31},{4,8},{5,9},{6,10},{7,11},{8,4},{9,5},... | collective-permute-start | bytes 688136 | tf_op jit(solution)/shard_map/ppermute | solution.py:268
  90.6 9.8 %collective-permute-start.20 = (bf16[112,1024]{1,0:T(8,128)(2,1)S(1)}, bf16[112,1024]{1,0:T(8,128)(2,1)S(1)}, u32[]{:S(2)}, u32[]{:S(2)}) collective-permute-start(bf16[112,1024]{1,0:T(8,128)(2,1)S(1)} %add.58), channel_id=1, source_target_pairs={{0,5},{1,4},{2,7},{3,6},{4,1},{5,0},{6,3},{7,2},{8,13},{9,12},{10,... | collective-permute-start | bytes 688136 | tf_op jit(solution)/shard_map/ppermute | solution.py:268
  95.7 8.2 %collective-permute-start.27 = (bf16[112,1024]{1,0:T(8,128)(2,1)S(1)}, bf16[112,1024]{1,0:T(8,128)(2,1)S(1)}, u32[]{:S(2)}, u32[]{:S(2)}) collective-permute-start(bf16[112,1024]{1,0:T(8,128)(2,1)S(1)} %add.65), channel_id=1, source_target_pairs={{0,29},{1,28},{2,31},{3,30},{4,9},{5,8},{6,11},{7,10},{8,5},{9,4},... | collective-permute-start | bytes 688136 | tf_op jit(solution)/shard_map/ppermute | solution.py:268
  (21 other events, 152.9 us)

commit v7 on v6

--- a/solution.py
+++ b/solution.py
@@ -323,8 +323,8 @@
         )
         parts.update(zip(wanted, got))
     given, kept = ([parts[w, o] for o in range(8)] for w in range(2))
-    got, _ = reduce_z(given, True, True)
-    kept, packed = reduce_z(kept, False, False, packed)
+    got, packed = reduce_z(given, True, True, packed)
+    kept, _ = reduce_z(kept, False, False)
     grad_inputs = packed.astype(F32).sum(axis=0).astype(BF)
     low = sum(jnp.where(ym == 0, a, b).astype(F32) for a, b in zip(kept, got))
     high = sum(jnp.where(ym == 0, b, a).astype(F32) for a, b in zip(kept, got))

time: 106 us -> 105 us (level)
  waiting for transfers between devices: 25.6 us -> 20.5 us
  starting transfers between devices: 38.7 us -> 42.9 us
    ppermute x14, waiting for transfers between devices: 16.6 us -> 11.5 us  [trade_z(): return lax.ppermute(value, ('z', 'y'), pairs)]
    ppermute x14, starting transfers between devices: 18.2 us -> 22.3 us  [trade_z(): return lax.ppermute(value, ('z', 'y'), pairs)]
  transfers between devices with their start and end apart: 30 -> 30, of which waited for: 14 -> 13; matrix products, arithmetic and copies ran while one was open for 5% -> 5% of each run, Pallas kernels for 30% -> 31%
where the time goes in v7:
time: 105 us; the launch traced here: 104 us
  starting transfers between devices  42.9 us (41%)
  Pallas kernels  31.9 us (30%)
  waiting for transfers between devices  20.5 us (20%)
  other arithmetic  5.67 us (5%)
  local copies, waits for them, and re-layouts  2.37 us (2%)
    ppermute x14, starting transfers between devices, trade_z(): return lax.ppermute(value, ('z', 'y'), pairs)  22.3 us
    pallas_call x1, Pallas kernels, both_products(): pl.pallas_call(both_kernel, grid=(hidden // tile,), in_specs=[pl.BlockSpe...  14.7 us
    ppermute x14, waiting for transfers between devices, trade_z(): return lax.ppermute(value, ('z', 'y'), pairs)  11.5 us
    pallas_call x2, Pallas kernels, weight_parts(): pl.pallas_call(functools.partial(first_kernel if first else rest_kernel,...  10.7 us
    ppermute x6, starting transfers between devices, trade(): return lax.ppermute(value, axis, pairs)  9.19 us
    ppermute x7, waiting for transfers between devices, send(): return lax.ppermute(value, axis, [(i, (i + step) % n) for i in range(n)])  8.78 us
    all_to_all x1, starting transfers between devices, on_device(): packed = lax.all_to_all(packed, 'col', 0, 0)  3.86 us
    pallas_call x1, Pallas kernels, grad_pre_flipped(): pl.pallas_call(grad_kernel, grid=(cols // tile,), in_specs=[pl.BlockSpec(...  3.77 us
  transfers between devices with their start and end apart: 30, of which 13 were waited for; matrix products, arithmetic and copies ran while one was open for 5% of the time, Pallas kernels for 31%

profile of v7, /device:TPU:2, one launch (start us, length us, event | category | flops | bytes accessed | tf_op | source)
XLA Modules:
  0.0 104.3 jit_solution(4848619617458255739)
XLA Ops:
  0.6 1.6 %collective-permute-start.3 = (bf16[64,2048]{1,0:T(8,128)(2,1)}, bf16[64,2048]{1,0:T(8,128)(2,1)S(1)}, u32[]{:S(2)}, u32[]{:S(2)}) collective-permute-start(bf16[64,2048]{1,0:T(8,128)(2,1)} %f0.1), channel_id=1, source_target_pairs={{0,96},{32,64},{64,32},{96,0},{1,97},{33,65},{65,33},{97,1},{2,98}... | collective-permute-start | bytes 786440 | tf_op jit(solution)/shard_map/ppermute | solution.py:36
  2.2 1.8 %collective-permute-start.4 = (bf16[64,2048]{1,0:T(8,128)(2,1)}, bf16[64,2048]{1,0:T(8,128)(2,1)S(1)}, u32[]{:S(2)}, u32[]{:S(2)}) collective-permute-start(bf16[64,2048]{1,0:T(8,128)(2,1)} %f0.1), channel_id=1, source_target_pairs={{0,32},{32,0},{64,96},{96,64},{1,33},{33,1},{65,97},{97,65},{2,34}... | collective-permute-start | bytes 786440 | tf_op jit(solution)/shard_map/ppermute | solution.py:36
  5.0 3.1 %collective-permute-start.2 = (bf16[64,1024]{1,0:T(8,128)(2,1)S(1)}, bf16[64,1024]{1,0:T(8,128)(2,1)S(1)}, u32[]{:S(2)}, u32[]{:S(2)}) collective-permute-start(bf16[64,1024]{1,0:T(8,128)(2,1)S(1)} %get-tuple-element.76), channel_id=1, source_target_pairs={{0,3},{1,2},{2,1},{3,0},{4,7},{5,6},{6,5},{7,4},{8,11},{9,10},{10,... | collective-permute-start | bytes 393224 | tf_op jit(solution)/shard_map/ppermute | solution.py:36
  9.2 3.8 %shard_map.76 = (bf16[3584,128]{1,0:T(8,128)(2,1)}, bf16[4,2,896,128]{3,2,1,0:T(8,128)(2,1)}) custom-call(bf16[128,3584]{1,0:T(8,128)(2,1)} %pre_ref.1, bf16[128,3584]{1,0:T(8,128)(2,1)} %grad_ref.1), custom_call_target="tpu_custom_call" | custom-call | flops 13762560 | bytes 4587520 | tf_op jit(solution)/shard_map/pallas_call | solution.py:70
  13.1 2.3 %collective-permute-done.1 = bf16[64,1024]{1,0:T(8,128)(2,1)S(1)} collective-permute-done((bf16[64,1024]{1,0:T(8,128)(2,1)S(1)}, bf16[64,1024]{1,0:T(8,128)(2,1)S(1)}, u32[]{:S(2)}, u32[]{:S(2)}) %collective-permute-start.1) | collective-permute-done | bytes 131104 | tf_op jit(solution)/shard_map/ppermute | solution.py:31
  16.5 1.7 %collective-permute-start.9 = (bf16[256,1024]{1,0:T(8,128)(2,1)S(1)}, bf16[256,1024]{1,0:T(8,128)(2,1)S(1)}, u32[]{:S(2)}, u32[]{:S(2)}) collective-permute-start(bf16[256,1024]{1,0:T(8,128)(2,1)S(1)} %pad_maximum_fusion), channel_id=1, source_target_pairs={{0,32},{32,0},{64,96},{96,64},{1,33},{33,1},{65,97},{97,65},{2,34}... | collective-permute-start | bytes 1572872 | tf_op jit(solution)/shard_map/ppermute | solution.py:36
  18.2 1.6 %collective-permute-start.10 = (bf16[256,1024]{1,0:T(8,128)(2,1)S(1)}, bf16[256,1024]{1,0:T(8,128)(2,1)S(1)}, u32[]{:S(2)}, u32[]{:S(2)}) collective-permute-start(bf16[256,1024]{1,0:T(8,128)(2,1)S(1)} %pad_maximum_fusion), channel_id=1, source_target_pairs={{0,64},{32,96},{64,0},{96,32},{1,65},{33,97},{65,1},{97,33},{2,66}... | collective-permute-start | bytes 1572872 | tf_op jit(solution)/shard_map/ppermute | solution.py:31
  20.4 3.6 %all-to-all-start = ((bf16[4,2,896,128]{3,2,1,0:T(8,128)(2,1)}), bf16[4,2,896,128]{3,2,1,0:T(8,128)(2,1)S(1)}, u32[]{:S(2)}, u32[]{:S(2)}) async-start(bf16[4,2,896,128]{3,2,1,0:T(8,128)(2,1)} %get-tuple-element.40), calls=%async_computation | async-start | bytes 3670016 | tf_op jit(solution)/shard_map/all_to_all | solution.py:306
  24.0 3.4 %collective-permute-done.5.f2 = bf16[64,2048]{1,0:T(8,128)(2,1)} collective-permute-done((bf16[64,2048]{1,0:T(8,128)(2,1)}, bf16[64,2048]{1,0:T(8,128)(2,1)}, u32[]{:S(2)}, u32[]{:S(2)}) %collective-permute-start.5) | collective-permute-done | bytes 262176 | tf_op jit(solution)/shard_map/ppermute | solution.py:31
  27.3 14.7 %shard_map.77 = (bf16[128,3584]{1,0:T(8,128)(2,1)}, bf16[4,64,2048]{2,1,0:T(8,128)(2,1)}, bf16[64,3584]{1,0:T(8,128)(2,1)}, bf16[64,3584]{1,0:T(8,128)(2,1)}) custom-call(bf16[64,2048]{1,0:T(8,128)(2,1)} %f0.1, bf16[64,2048]{1,0:T(8,128)(2,1)} %copy-done.14, bf16[64,2048]{1,0:T(8,128)(2,1)} %collective-permute-done.5.f2, bf16[64,2048]{1,0:T(8,128)(2,1)} %copy-done.13, ...), custom_call_target="tpu_custom_call" | custom-call | flops 22548578304 | bytes 14680064 | tf_op jit(solution)/shard_map/pallas_call | solution.py:215
  45.0 2.7 %shard_map.78 = bf16[128,3584]{1,0:T(8,128)(2,1)} custom-call(bf16[128,3584]{1,0:T(8,128)(2,1)} %get-tuple-element.44.keep_ref, bf16[64,3584]{1,0:T(8,128)(2,1)} %copy-done.4, bf16[64,3584]{1,0:T(8,128)(2,1)} %collective-permute-done.8.refs_1_), custom_call_target="tpu_custom_call" | custom-call | flops 262144 | bytes 262144 | tf_op jit(solution)/shard_map/pallas_call | solution.py:251
  49.4 3.9 %all-to-all-start.1 = ((bf16[4,64,2048]{2,1,0:T(8,128)(2,1)}), bf16[4,64,2048]{2,1,0:T(8,128)(2,1)S(1)}, u32[]{:S(2)}, u32[]{:S(2)}) async-start(bf16[4,64,2048]{2,1,0:T(8,128)(2,1)} %get-tuple-element.55), calls=%async_computation.1 | async-start | bytes 2097152 | tf_op jit(solution)/shard_map/all_to_all | solution.py:316
  53.2 4.1 %shard_map.79 = (bf16[112,1024]{1,0:T(8,128)(2,1)}, bf16[112,1024]{1,0:T(8,128)(2,1)}, bf16[112,1024]{1,0:T(8,128)(2,1)}, bf16[112,1024]{1,0:T(8,128)(2,1)}) custom-call(bf16[4,2,896,128]{3,2,1,0:T(8,128)(2,1)} %copy-done, bf16[4,2,896,128]{3,2,1,0:T(8,128)(2,1)} %collective-permute-done.12.oth_ref, bf16[4,64,1024]{2,1,0:T(8,128)(2,1)} %bitcast.6, ...), custom_call_target="tpu_custom_call" | custom-call | flops 1048576 | bytes 1048576 | tf_op jit(solution)/shard_map/pallas_call | solution.py:164
  57.3 2.0 %collective-permute-start.13 = (bf16[112,1024]{1,0:T(8,128)(2,1)}, bf16[112,1024]{1,0:T(8,128)(2,1)S(1)}, u32[]{:S(2)}, u32[]{:S(2)}) collective-permute-start(bf16[112,1024]{1,0:T(8,128)(2,1)} %get-tuple-element.54), channel_id=1, source_target_pairs={{0,4},{1,5},{2,6},{3,7},{4,0},{5,1},{6,2},{7,3},{8,12},{9,13},{10,... | collective-permute-start | bytes 688136 | tf_op jit(solution)/shard_map/ppermute | solution.py:268
  59.3 4.9 %collective-permute-start.21 = (bf16[112,1024]{1,0:T(8,128)(2,1)}, bf16[112,1024]{1,0:T(8,128)(2,1)S(1)}, u32[]{:S(2)}, u32[]{:S(2)}) collective-permute-start(bf16[112,1024]{1,0:T(8,128)(2,1)} %get-tuple-element.65), channel_id=1, source_target_pairs={{0,28},{1,29},{2,30},{3,31},{4,8},{5,9},{6,10},{7,11},{8,4},{9,5},... | collective-permute-start | bytes 688136 | tf_op jit(solution)/shard_map/ppermute | solution.py:268
  64.3 6.6 %shard_map.80 = (bf16[112,1024]{1,0:T(8,128)(2,1)}, bf16[112,1024]{1,0:T(8,128)(2,1)}, bf16[112,1024]{1,0:T(8,128)(2,1)}, bf16[112,1024]{1,0:T(8,128)(2,1)}, bf1...) custom-call(bf16[4,2,896,128]{3,2,1,0:T(8,128)(2,1)} %copy-done, ...), custom_call_target="tpu_custom_call" | custom-call | flops 1048576 | bytes 1048576 | tf_op jit(solution)/shard_map/pallas_call | solution.py:164
  72.1 2.1 %collective-permute-start.22 = (bf16[112,1024]{1,0:T(8,128)(2,1)S(1)}, bf16[112,1024]{1,0:T(8,128)(2,1)S(1)}, u32[]{:S(2)}, u32[]{:S(2)}) collective-permute-start(bf16[112,1024]{1,0:T(8,128)(2,1)S(1)} %add.60), channel_id=1, source_target_pairs={{0,4},{1,5},{2,6},{3,7},{4,0},{5,1},{6,2},{7,3},{8,12},{9,13},{10,... | collective-permute-start | bytes 688136 | tf_op jit(solution)/shard_map/ppermute | solution.py:268
  75.2 3.3 %collective-permute-start.25 = (bf16[112,1024]{1,0:T(8,128)(2,1)S(1)}, bf16[112,1024]{1,0:T(8,128)(2,1)S(1)}, u32[]{:S(2)}, u32[]{:S(2)}) collective-permute-start(bf16[112,1024]{1,0:T(8,128)(2,1)S(1)} %add.63), channel_id=1, source_target_pairs={{0,28},{1,29},{2,30},{3,31},{4,8},{5,9},{6,10},{7,11},{8,4},{9,5},... | collective-permute-start | bytes 688136 | tf_op jit(solution)/shard_map/ppermute | solution.py:268
  80.9 2.5 %collective-permute-start.23 = (bf16[112,1024]{1,0:T(8,128)(2,1)S(1)}, bf16[112,1024]{1,0:T(8,128)(2,1)S(1)}, u32[]{:S(2)}, u32[]{:S(2)}) collective-permute-start(bf16[112,1024]{1,0:T(8,128)(2,1)S(1)} %add.61), channel_id=1, source_target_pairs={{0,28},{1,29},{2,30},{3,31},{4,8},{5,9},{6,10},{7,11},{8,4},{9,5},... | collective-permute-start | bytes 688136 | tf_op jit(solution)/shard_map/ppermute | solution.py:268
  85.4 2.3 %collective-permute-done.16 = bf16[112,1024]{1,0:T(8,128)(2,1)S(1)} collective-permute-done((bf16[112,1024]{1,0:T(8,128)(2,1)S(1)}, bf16[112,1024]{1,0:T(8,128)(2,1)S(1)}, u32[]{:S(2)}, u32[]{:S(2)}) %collective-permute-start.16) | collective-permute-done | bytes 229408 | tf_op jit(solution)/shard_map/ppermute | solution.py:268
  90.5 4.0 %collective-permute-done.23 = bf16[112,1024]{1,0:T(8,128)(2,1)S(1)} collective-permute-done((bf16[112,1024]{1,0:T(8,128)(2,1)S(1)}, bf16[112,1024]{1,0:T(8,128)(2,1)S(1)}, u32[]{:S(2)}, u32[]{:S(2)}) %collective-permute-start.23) | collective-permute-done | bytes 229408 | tf_op jit(solution)/shard_map/ppermute | solution.py:268
  94.9 3.5 %collective-permute-start.27 = (bf16[112,1024]{1,0:T(8,128)(2,1)S(1)}, bf16[112,1024]{1,0:T(8,128)(2,1)S(1)}, u32[]{:S(2)}, u32[]{:S(2)}) collective-permute-start(bf16[112,1024]{1,0:T(8,128)(2,1)S(1)} %add.65), channel_id=1, source_target_pairs={{0,29},{1,28},{2,31},{3,30},{4,9},{5,8},{6,11},{7,10},{8,5},{9,4},... | collective-permute-start | bytes 688136 | tf_op jit(solution)/shard_map/ppermute | solution.py:268
  99.4 1.7 %collective-permute-done.24 = bf16[112,1024]{1,0:T(8,128)(2,1)S(1)} collective-permute-done((bf16[112,1024]{1,0:T(8,128)(2,1)S(1)}, bf16[112,1024]{1,0:T(8,128)(2,1)S(1)}, u32[]{:S(2)}, u32[]{:S(2)}) %collective-permute-start.24) | collective-permute-done | bytes 229408 | tf_op jit(solution)/shard_map/ppermute | solution.py:268
  101.1 2.0 %collective-permute-done.27 = bf16[112,1024]{1,0:T(8,128)(2,1)S(1)} collective-permute-done((bf16[112,1024]{1,0:T(8,128)(2,1)S(1)}, bf16[112,1024]{1,0:T(8,128)(2,1)S(1)}, u32[]{:S(2)}, u32[]{:S(2)}) %collective-permute-start.27) | collective-permute-done | bytes 229408 | tf_op jit(solution)/shard_map/ppermute | solution.py:268
  (86 shorter events, 20.2 us)
Async XLA Ops:
  0.6 14.8 %collective-permute-start.3 = (bf16[64,2048]{1,0:T(8,128)(2,1)}, bf16[64,2048]{1,0:T(8,128)(2,1)S(1)}, u32[]{:S(2)}, u32[]{:S(2)}) collective-permute-start(bf16[64,2048]{1,0:T(8,128)(2,1)} %f0.1), channel_id=1, source_target_pairs={{0,96},{32,64},{64,32},{96,0},{1,97},{33,65},{65,33},{97,1},{2,98}... | collective-permute-start | bytes 786440 | tf_op jit(solution)/shard_map/ppermute | solution.py:36
  2.2 13.3 %collective-permute-start.4 = (bf16[64,2048]{1,0:T(8,128)(2,1)}, bf16[64,2048]{1,0:T(8,128)(2,1)S(1)}, u32[]{:S(2)}, u32[]{:S(2)}) collective-permute-start(bf16[64,2048]{1,0:T(8,128)(2,1)} %f0.1), channel_id=1, source_target_pairs={{0,32},{32,0},{64,96},{96,64},{1,33},{33,1},{65,97},{97,65},{2,34}... | collective-permute-start | bytes 786440 | tf_op jit(solution)/shard_map/ppermute | solution.py:36
  5.0 8.1 %collective-permute-start.2 = (bf16[64,1024]{1,0:T(8,128)(2,1)S(1)}, bf16[64,1024]{1,0:T(8,128)(2,1)S(1)}, u32[]{:S(2)}, u32[]{:S(2)}) collective-permute-start(bf16[64,1024]{1,0:T(8,128)(2,1)S(1)} %get-tuple-element.76), channel_id=1, source_target_pairs={{0,3},{1,2},{2,1},{3,0},{4,7},{5,6},{6,5},{7,4},{8,11},{9,10},{10,... | collective-permute-start | bytes 393224 | tf_op jit(solution)/shard_map/ppermute | solution.py:36
  15.5 11.8 %collective-permute-start.6 = (bf16[3584,128]{1,0:T(8,128)(2,1)}, bf16[3584,128]{1,0:T(8,128)(2,1)}, u32[]{:S(2)}, u32[]{:S(2)}) collective-permute-start(bf16[3584,128]{1,0:T(8,128)(2,1)} %get-tuple-element.43.own_ref), channel_id=1, source_target_pairs={{0,128},{128,0},{1,129},{129,1},{2,130},{130,2},{3,131},{131,3},{4... | collective-permute-start | bytes 2752520 | tf_op jit(solution)/shard_map/ppermute | solution.py:31
  16.3 11.1 %collective-permute-start.5 = (bf16[64,2048]{1,0:T(8,128)(2,1)}, bf16[64,2048]{1,0:T(8,128)(2,1)}, u32[]{:S(2)}, u32[]{:S(2)}) collective-permute-start(bf16[64,2048]{1,0:T(8,128)(2,1)} %f0.1), channel_id=1, source_target_pairs={{0,64},{32,96},{64,0},{96,32},{1,65},{33,97},{65,1},{97,33},{2,66}... | collective-permute-start | bytes 786440 | tf_op jit(solution)/shard_map/ppermute | solution.py:31
  16.5 31.2 %collective-permute-start.9 = (bf16[256,1024]{1,0:T(8,128)(2,1)S(1)}, bf16[256,1024]{1,0:T(8,128)(2,1)S(1)}, u32[]{:S(2)}, u32[]{:S(2)}) collective-permute-start(bf16[256,1024]{1,0:T(8,128)(2,1)S(1)} %pad_maximum_fusion), channel_id=1, source_target_pairs={{0,32},{32,0},{64,96},{96,64},{1,33},{33,1},{65,97},{97,65},{2,34}... | collective-permute-start | bytes 1572872 | tf_op jit(solution)/shard_map/ppermute | solution.py:36
  18.2 30.4 %collective-permute-start.10 = (bf16[256,1024]{1,0:T(8,128)(2,1)S(1)}, bf16[256,1024]{1,0:T(8,128)(2,1)S(1)}, u32[]{:S(2)}, u32[]{:S(2)}) collective-permute-start(bf16[256,1024]{1,0:T(8,128)(2,1)S(1)} %pad_maximum_fusion), channel_id=1, source_target_pairs={{0,64},{32,96},{64,0},{96,32},{1,65},{33,97},{65,1},{97,33},{2,66}... | collective-permute-start | bytes 1572872 | tf_op jit(solution)/shard_map/ppermute | solution.py:31
  19.8 28.8 %collective-permute-start.11 = (bf16[256,1024]{1,0:T(8,128)(2,1)S(1)}, bf16[256,1024]{1,0:T(8,128)(2,1)}, u32[]{:S(2)}, u32[]{:S(2)}) collective-permute-start(bf16[256,1024]{1,0:T(8,128)(2,1)S(1)} %pad_maximum_fusion), channel_id=1, source_target_pairs={{0,96},{32,64},{64,32},{96,0},{1,97},{33,65},{65,33},{97,1},{2,98}... | collective-permute-start | bytes 1572872 | tf_op jit(solution)/shard_map/ppermute | solution.py:36
  20.4 28.2 %all-to-all-start = ((bf16[4,2,896,128]{3,2,1,0:T(8,128)(2,1)}), bf16[4,2,896,128]{3,2,1,0:T(8,128)(2,1)S(1)}, u32[]{:S(2)}, u32[]{:S(2)}) async-start(bf16[4,2,896,128]{3,2,1,0:T(8,128)(2,1)} %get-tuple-element.40), calls=%async_computation | async-start | bytes 3670016 | tf_op jit(solution)/shard_map/all_to_all | solution.py:306
  49.4 21.6 %all-to-all-start.1 = ((bf16[4,64,2048]{2,1,0:T(8,128)(2,1)}), bf16[4,64,2048]{2,1,0:T(8,128)(2,1)S(1)}, u32[]{:S(2)}, u32[]{:S(2)}) async-start(bf16[4,64,2048]{2,1,0:T(8,128)(2,1)} %get-tuple-element.55), calls=%async_computation.1 | async-start | bytes 2097152 | tf_op jit(solution)/shard_map/all_to_all | solution.py:316
  57.3 13.6 %collective-permute-start.13 = (bf16[112,1024]{1,0:T(8,128)(2,1)}, bf16[112,1024]{1,0:T(8,128)(2,1)S(1)}, u32[]{:S(2)}, u32[]{:S(2)}) collective-permute-start(bf16[112,1024]{1,0:T(8,128)(2,1)} %get-tuple-element.54), channel_id=1, source_target_pairs={{0,4},{1,5},{2,6},{3,7},{4,0},{5,1},{6,2},{7,3},{8,12},{9,13},{10,... | collective-permute-start | bytes 688136 | tf_op jit(solution)/shard_map/ppermute | solution.py:268
  59.3 11.7 %collective-permute-start.21 = (bf16[112,1024]{1,0:T(8,128)(2,1)}, bf16[112,1024]{1,0:T(8,128)(2,1)S(1)}, u32[]{:S(2)}, u32[]{:S(2)}) collective-permute-start(bf16[112,1024]{1,0:T(8,128)(2,1)} %get-tuple-element.65), channel_id=1, source_target_pairs={{0,28},{1,29},{2,30},{3,31},{4,8},{5,9},{6,10},{7,11},{8,4},{9,5},... | collective-permute-start | bytes 688136 | tf_op jit(solution)/shard_map/ppermute | solution.py:268
  64.3 14.2 %collective-permute-start.15 = (bf16[112,1024]{1,0:T(8,128)(2,1)}, bf16[112,1024]{1,0:T(8,128)(2,1)S(1)}, u32[]{:S(2)}, u32[]{:S(2)}) collective-permute-start(bf16[112,1024]{1,0:T(8,128)(2,1)} %get-tuple-element.59), channel_id=1, source_target_pairs={{0,28},{1,29},{2,30},{3,31},{4,8},{5,9},{6,10},{7,11},{8,4},{9,5},... | collective-permute-start | bytes 688136 | tf_op jit(solution)/shard_map/ppermute | solution.py:268
  64.3 15.3 %collective-permute-start.18 = (bf16[112,1024]{1,0:T(8,128)(2,1)}, bf16[112,1024]{1,0:T(8,128)(2,1)S(1)}, u32[]{:S(2)}, u32[]{:S(2)}) collective-permute-start(bf16[112,1024]{1,0:T(8,128)(2,1)} %get-tuple-element.62), channel_id=1, source_target_pairs={{0,4},{1,5},{2,6},{3,7},{4,0},{5,1},{6,2},{7,3},{8,12},{9,13},{10,... | collective-permute-start | bytes 688136 | tf_op jit(solution)/shard_map/ppermute | solution.py:268
  72.1 8.7 %collective-permute-start.22 = (bf16[112,1024]{1,0:T(8,128)(2,1)S(1)}, bf16[112,1024]{1,0:T(8,128)(2,1)S(1)}, u32[]{:S(2)}, u32[]{:S(2)}) collective-permute-start(bf16[112,1024]{1,0:T(8,128)(2,1)S(1)} %add.60), channel_id=1, source_target_pairs={{0,4},{1,5},{2,6},{3,7},{4,0},{5,1},{6,2},{7,3},{8,12},{9,13},{10,... | collective-permute-start | bytes 688136 | tf_op jit(solution)/shard_map/ppermute | solution.py:268
  75.2 9.4 %collective-permute-start.25 = (bf16[112,1024]{1,0:T(8,128)(2,1)S(1)}, bf16[112,1024]{1,0:T(8,128)(2,1)S(1)}, u32[]{:S(2)}, u32[]{:S(2)}) collective-permute-start(bf16[112,1024]{1,0:T(8,128)(2,1)S(1)} %add.63), channel_id=1, source_target_pairs={{0,28},{1,29},{2,30},{3,31},{4,8},{5,9},{6,10},{7,11},{8,4},{9,5},... | collective-permute-start | bytes 688136 | tf_op jit(solution)/shard_map/ppermute | solution.py:268
  79.5 8.2 %collective-permute-start.16 = (bf16[112,1024]{1,0:T(8,128)(2,1)S(1)}, bf16[112,1024]{1,0:T(8,128)(2,1)S(1)}, u32[]{:S(2)}, u32[]{:S(2)}) collective-permute-start(bf16[112,1024]{1,0:T(8,128)(2,1)S(1)} %add.55), channel_id=1, source_target_pairs={{0,4},{1,5},{2,6},{3,7},{4,0},{5,1},{6,2},{7,3},{8,12},{9,13},{10,... | collective-permute-start | bytes 688136 | tf_op jit(solution)/shard_map/ppermute | solution.py:268
  79.7 9.8 %collective-permute-start.19 = (bf16[112,1024]{1,0:T(8,128)(2,1)S(1)}, bf16[112,1024]{1,0:T(8,128)(2,1)S(1)}, u32[]{:S(2)}, u32[]{:S(2)}) collective-permute-start(bf16[112,1024]{1,0:T(8,128)(2,1)S(1)} %add.57), channel_id=1, source_target_pairs={{0,28},{1,29},{2,30},{3,31},{4,8},{5,9},{6,10},{7,11},{8,4},{9,5},... | collective-permute-start | bytes 688136 | tf_op jit(solution)/shard_map/ppermute | solution.py:268
  80.9 13.6 %collective-permute-start.23 = (bf16[112,1024]{1,0:T(8,128)(2,1)S(1)}, bf16[112,1024]{1,0:T(8,128)(2,1)S(1)}, u32[]{:S(2)}, u32[]{:S(2)}) collective-permute-start(bf16[112,1024]{1,0:T(8,128)(2,1)S(1)} %add.61), channel_id=1, source_target_pairs={{0,28},{1,29},{2,30},{3,31},{4,8},{5,9},{6,10},{7,11},{8,4},{9,5},... | collective-permute-start | bytes 688136 | tf_op jit(solution)/shard_map/ppermute | solution.py:268
  84.6 10.2 %collective-permute-start.26 = (bf16[112,1024]{1,0:T(8,128)(2,1)S(1)}, bf16[112,1024]{1,0:T(8,128)(2,1)S(1)}, u32[]{:S(2)}, u32[]{:S(2)}) collective-permute-start(bf16[112,1024]{1,0:T(8,128)(2,1)S(1)} %add.64), channel_id=1, source_target_pairs={{0,4},{1,5},{2,6},{3,7},{4,0},{5,1},{6,2},{7,3},{8,12},{9,13},{10,... | collective-permute-start | bytes 688136 | tf_op jit(solution)/shard_map/ppermute | solution.py:268
  84.7 14.6 %collective-permute-start.14 = (bf16[112,1024]{1,0:T(8,128)(2,1)}, bf16[112,1024]{1,0:T(8,128)(2,1)S(1)}, u32[]{:S(2)}, u32[]{:S(2)}) collective-permute-start(bf16[112,1024]{1,0:T(8,128)(2,1)} %get-tuple-element.58), channel_id=1, source_target_pairs={{0,1},{1,0},{2,3},{3,2},{4,5},{5,4},{6,7},{7,6},{8,9},{9,8},{10,11... | collective-permute-start | bytes 688136 | tf_op jit(solution)/shard_map/ppermute | solution.py:284
  87.8 11.6 %collective-permute-start.17 = (bf16[112,1024]{1,0:T(8,128)(2,1)S(1)}, bf16[112,1024]{1,0:T(8,128)(2,1)S(1)}, u32[]{:S(2)}, u32[]{:S(2)}) collective-permute-start(bf16[112,1024]{1,0:T(8,128)(2,1)S(1)} %add.56), channel_id=1, source_target_pairs={{0,28},{1,29},{2,30},{3,31},{4,8},{5,9},{6,10},{7,11},{8,4},{9,5},... | collective-permute-start | bytes 688136 | tf_op jit(solution)/shard_map/ppermute | solution.py:268
  89.6 9.8 %collective-permute-start.20 = (bf16[112,1024]{1,0:T(8,128)(2,1)S(1)}, bf16[112,1024]{1,0:T(8,128)(2,1)S(1)}, u32[]{:S(2)}, u32[]{:S(2)}) collective-permute-start(bf16[112,1024]{1,0:T(8,128)(2,1)S(1)} %add.58), channel_id=1, source_target_pairs={{0,5},{1,4},{2,7},{3,6},{4,1},{5,0},{6,3},{7,2},{8,13},{9,12},{10,... | collective-permute-start | bytes 688136 | tf_op jit(solution)/shard_map/ppermute | solution.py:268
  94.9 8.2 %collective-permute-start.27 = (bf16[112,1024]{1,0:T(8,128)(2,1)S(1)}, bf16[112,1024]{1,0:T(8,128)(2,1)S(1)}, u32[]{:S(2)}, u32[]{:S(2)}) collective-permute-start(bf16[112,1024]{1,0:T(8,128)(2,1)S(1)} %add.65), channel_id=1, source_target_pairs={{0,29},{1,28},{2,31},{3,30},{4,9},{5,8},{6,11},{7,10},{8,5},{9,4},... | collective-permute-start | bytes 688136 | tf_op jit(solution)/shard_map/ppermute | solution.py:268
  (21 other events, 156.1 us)
